TPU v7x, 32 devices: a whole 2x2x4 slice. The times are simulated.
32 devices in a mesh: fsdp: 8 (over y, x, core), tp: 4 (over z).
Axes of the slice: x: 2, y: 2, z: 4, core: 2. Of those that a mesh axis runs over, the one named last changes fastest.
Arguments:
- layer_input: bfloat16 [8192, 2048], P(('fsdp', 'tp')), may hold values from -6 to 6
- norm_gains: float32 [2, 2048], replicated, may hold values from 0.1 to 1.9
- w_qkv: bfloat16 [3, 2048, 2048], P(None, 'fsdp', 'tp'), may hold values from -0.125 to 0.125
- w_out: bfloat16 [2048, 2048], P('tp', 'fsdp'), may hold values from -0.5 to 0.5
- w_gate_up: bfloat16 [2, 2048, 5504], P(None, 'fsdp', 'tp'), may hold values from -0.125 to 0.125
- w_down: bfloat16 [5504, 2048], P('tp', 'fsdp'), may hold values from -0.078125 to 0.078125
- doc_start: int32 [8192], P('fsdp'), may hold values from 0 to 8191, as said below
- out_cotangent: bfloat16 [8192, 2048], P(('fsdp', 'tp')), may hold values from -6 to 6
Outputs:
- layer_output: bfloat16 [8192, 2048], P(('fsdp', 'tp'))
- input_grad: bfloat16 [8192, 2048], P(('fsdp', 'tp'))
- gain_grad: float32 [2, 2048], replicated
- w_qkv_grad: float32 [3, 2048, 2048], P(None, 'fsdp', 'tp')
- w_out_grad: float32 [2048, 2048], P('tp', 'fsdp')
- w_gate_up_grad: float32 [2, 2048, 5504], P(None, 'fsdp', 'tp')
- w_down_grad: float32 [5504, 2048], P('tp', 'fsdp')
Inputs may be any that keep to these rules, and one draw needn't show every extreme that they name: Documents are runs of consecutive tokens: doc_start[p] is p or doc_start[p - 1]. A document starts at every multiple of 4096 and at the last position, and never at a position p with p % 1024 < 256 that is not a multiple of 4096.
All inputs are finite; a program needn't handle non-finite values.
Results may differ from a plain program's by a relative error of at most 0.02.
Values may be sent and summed in bfloat16 or wider, within the bound.
No kernel may reach another device: no remote copies, remote signals or barrier semaphores. Data moves between devices by JAX's collectives and lax.ppermute only.
A program may use at most 320 MiB of HBM per device.

v0:
```python
import math

import jax
import jax.numpy as jnp
from jax import lax
from jax.sharding import PartitionSpec as P

HEAD_DIM = 128
WINDOW = 1024
QBLOCK = 512


EPS = 1e-06
MASKED = -1e30


def from_behind(block, axis, distance):
    devices = range(lax.axis_size(axis))
    route = [(i - distance, i) for i in devices if i - distance in devices]
    return lax.ppermute(block, axis, route)


def normalize(values):
    inverse = lax.rsqrt(jnp.mean(values * values, axis=-1, keepdims=True) + EPS)
    return (values * inverse, inverse)


def norm_back(grad, gain, unit, inverse):
    scaled = grad * gain
    return inverse * (scaled - unit * jnp.mean(scaled * unit, axis=-1, keepdims=True))


def block_scores(block_index, queries, key_rows, doc_first, offset):
    first_row = block_index * QBLOCK
    local_heads = queries.shape[1] // HEAD_DIM
    q_block = lax.dynamic_slice_in_dim(queries, first_row, QBLOCK, 0).reshape(
        QBLOCK, local_heads, HEAD_DIM
    )
    k_block = lax.dynamic_slice_in_dim(key_rows, first_row, WINDOW + QBLOCK, 0).reshape(
        WINDOW + QBLOCK, local_heads, HEAD_DIM
    )
    raw_scores = jnp.einsum(
        "qhe,khe->hqk", q_block, k_block, preferred_element_type=jnp.float32
    ) * (1.0 / math.sqrt(HEAD_DIM))
    query_pos = offset + first_row + jnp.arange(QBLOCK, dtype=jnp.int32)
    key_pos = offset + first_row - WINDOW + jnp.arange(WINDOW + QBLOCK, dtype=jnp.int32)
    doc_block = lax.dynamic_slice_in_dim(doc_first, first_row, QBLOCK, 0)
    allowed = (
        (key_pos[None, :] <= query_pos[:, None])
        & (key_pos[None, :] > query_pos[:, None] - WINDOW)
        & (key_pos[None, :] >= doc_block[:, None])
    )
    return (jnp.where(allowed[None], raw_scores, MASKED), q_block, k_block)


def per_device(layer_input, norm_gains, w_qkv, w_out, w_gate_up, w_down, doc_start, out_cotangent):
    span_len = doc_start.shape[0]
    offset = lax.axis_index("fsdp") * span_len
    block_ids = jnp.arange(span_len // QBLOCK, dtype=jnp.int32)
    scale = 1.0 / math.sqrt(HEAD_DIM)
    full_qkv, full_out, full_gate_up, full_down = (
        lax.all_gather(w_qkv, "fsdp", axis=1, tiled=True),
        lax.all_gather(w_out, "fsdp", axis=1, tiled=True),
        lax.all_gather(w_gate_up, "fsdp", axis=1, tiled=True),
        lax.all_gather(w_down, "fsdp", axis=1, tiled=True),
    )
    input_f32 = layer_input.astype(jnp.float32)
    unit_one, inverse_one = normalize(input_f32)
    normed_one = (unit_one * norm_gains[0]).astype(jnp.bfloat16)
    attn_rows = lax.all_gather(normed_one, "tp", axis=0, tiled=True)
    qkv = jnp.einsum("td,sde->ste", attn_rows, full_qkv, preferred_element_type=jnp.float32).astype(
        jnp.bfloat16
    )
    prev_kv = from_behind(qkv[1:, span_len - WINDOW :], "fsdp", 1)
    key_value = jnp.concatenate([prev_kv, qkv[1:]], axis=1)
    queries = qkv[0]
    key_rows = key_value[0]
    value_rows = key_value[1]
    local_heads = queries.shape[1] // HEAD_DIM
    head_width = local_heads * HEAD_DIM

    def value_block(block_index):
        return lax.dynamic_slice_in_dim(
            value_rows, block_index * QBLOCK, WINDOW + QBLOCK, 0
        ).reshape(WINDOW + QBLOCK, local_heads, HEAD_DIM)

    def attend(block_index):
        scores, q_block, k_block = block_scores(block_index, queries, key_rows, doc_start, offset)
        row_max = jnp.max(scores, axis=-1, keepdims=True)
        exponent = jnp.exp(scores - row_max)
        row_total = jnp.sum(exponent, axis=-1, keepdims=True)
        weights = (exponent / row_total).astype(jnp.bfloat16)
        mixed = jnp.einsum(
            "hqk,khe->qhe", weights, value_block(block_index), preferred_element_type=jnp.float32
        )
        return (mixed.reshape(QBLOCK, head_width), row_max, row_total)

    mixed_blocks, block_max, block_total = lax.map(attend, block_ids)
    heads_out = mixed_blocks.reshape(span_len, head_width).astype(jnp.bfloat16)
    residual_mid = input_f32 + lax.psum_scatter(
        jnp.dot(heads_out, full_out, preferred_element_type=jnp.float32).astype(jnp.bfloat16),
        "tp",
        scatter_dimension=0,
        tiled=True,
    ).astype(jnp.float32)
    unit_two, inverse_two = normalize(residual_mid)
    normed_two = (unit_two * norm_gains[1]).astype(jnp.bfloat16)
    mlp_rows, cot_rows = (
        lax.all_gather(normed_two, "tp", axis=0, tiled=True),
        lax.all_gather(out_cotangent, "tp", axis=0, tiled=True),
    )
    gate_up = jnp.einsum("td,sdf->stf", mlp_rows, full_gate_up, preferred_element_type=jnp.float32)
    gate_pre = gate_up[0]
    up_pre = gate_up[1]
    sigmoid_gate = jax.nn.sigmoid(gate_pre)
    act = (gate_pre * sigmoid_gate * up_pre).astype(jnp.bfloat16)
    layer_output = (
        residual_mid
        + lax.psum_scatter(
            jnp.dot(act, full_down, preferred_element_type=jnp.float32).astype(jnp.bfloat16),
            "tp",
            scatter_dimension=0,
            tiled=True,
        ).astype(jnp.float32)
    ).astype(jnp.bfloat16)
    full_qkv, full_out, full_gate_up, full_down = (
        lax.all_gather(w_qkv, "fsdp", axis=1, tiled=True),
        lax.all_gather(w_out, "fsdp", axis=1, tiled=True),
        lax.all_gather(w_gate_up, "fsdp", axis=1, tiled=True),
        lax.all_gather(w_down, "fsdp", axis=1, tiled=True),
    )
    contract_first = (((0,), (0,)), ((), ()))
    contract_last = (((1,), (1,)), ((), ()))
    grad_act = lax.dot_general(
        cot_rows, full_down, contract_last, preferred_element_type=jnp.float32
    )
    down_grad = lax.dot_general(act, cot_rows, contract_first, preferred_element_type=jnp.float32)
    grad_up = grad_act * gate_pre * sigmoid_gate
    grad_gate = grad_act * up_pre * sigmoid_gate * (1.0 + gate_pre * (1.0 - sigmoid_gate))
    grad_gate_up = jnp.stack([grad_gate, grad_up]).astype(jnp.bfloat16)
    gate_up_grad = jnp.einsum(
        "td,stf->sdf", mlp_rows, grad_gate_up, preferred_element_type=jnp.float32
    )
    piece = grad_gate_up
    grad_normed_two = lax.psum_scatter(
        jnp.einsum("stf,sdf->td", piece, full_gate_up, preferred_element_type=jnp.float32).astype(
            jnp.bfloat16
        ),
        "tp",
        scatter_dimension=0,
        tiled=True,
    ).astype(jnp.float32)
    grad_mid = out_cotangent.astype(jnp.float32) + norm_back(
        grad_normed_two, norm_gains[1], unit_two, inverse_two
    )
    grad_branch = lax.all_gather(grad_mid.astype(jnp.bfloat16), "tp", axis=0, tiled=True)
    out_grad = lax.dot_general(
        heads_out, grad_branch, contract_first, preferred_element_type=jnp.float32
    )
    grad_heads = lax.dot_general(
        grad_branch, full_out, contract_last, preferred_element_type=jnp.float32
    ).astype(jnp.bfloat16)

    def back_step(key_grads, block_index):
        scores, q_block, k_block = block_scores(block_index, queries, key_rows, doc_start, offset)
        probs = jnp.exp(scores - block_max[block_index]) / block_total[block_index]
        weights = probs.astype(jnp.bfloat16)
        first_row = block_index * QBLOCK
        grad_block = lax.dynamic_slice_in_dim(grad_heads, first_row, QBLOCK, 0).reshape(
            QBLOCK, local_heads, HEAD_DIM
        )
        grad_probs = jnp.einsum(
            "qhe,khe->hqk", grad_block, value_block(block_index), preferred_element_type=jnp.float32
        )
        grad_scores = (
            probs * (grad_probs - jnp.sum(grad_probs * probs, axis=-1, keepdims=True))
        ).astype(jnp.bfloat16)
        grad_query = (
            jnp.einsum("hqk,khe->qhe", grad_scores, k_block, preferred_element_type=jnp.float32)
            * scale
        )
        grad_key = (
            jnp.einsum("hqk,qhe->khe", grad_scores, q_block, preferred_element_type=jnp.float32)
            * scale
        )
        grad_value = jnp.einsum(
            "hqk,qhe->khe", weights, grad_block, preferred_element_type=jnp.float32
        )
        update = jnp.stack([grad_key, grad_value]).reshape(2, WINDOW + QBLOCK, head_width)
        current = lax.dynamic_slice_in_dim(key_grads, first_row, WINDOW + QBLOCK, 1)
        key_grads = lax.dynamic_update_slice_in_dim(key_grads, current + update, first_row, 1)
        return (key_grads, grad_query.reshape(QBLOCK, head_width))

    start_grads = jnp.zeros((2, WINDOW + span_len, head_width), jnp.float32)
    key_grads, query_blocks = lax.scan(back_step, start_grads, block_ids)
    returned = from_behind(key_grads[:, :WINDOW].astype(jnp.bfloat16), "fsdp", -1).astype(
        jnp.float32
    )
    own_grads = key_grads[:, WINDOW:].at[:, span_len - WINDOW :].add(returned)
    grad_qkv = jnp.concatenate(
        [query_blocks.reshape(1, span_len, head_width), own_grads], axis=0
    ).astype(jnp.bfloat16)
    qkv_grad = jnp.einsum("td,ste->sde", attn_rows, grad_qkv, preferred_element_type=jnp.float32)
    piece = grad_qkv
    grad_normed_one = lax.psum_scatter(
        jnp.einsum("ste,sde->td", piece, full_qkv, preferred_element_type=jnp.float32).astype(
            jnp.bfloat16
        ),
        "tp",
        scatter_dimension=0,
        tiled=True,
    ).astype(jnp.float32)
    input_grad = (
        grad_mid + norm_back(grad_normed_one, norm_gains[0], unit_one, inverse_one)
    ).astype(jnp.bfloat16)
    gain_parts = jnp.stack(
        [jnp.sum(grad_normed_one * unit_one, axis=0), jnp.sum(grad_normed_two * unit_two, axis=0)]
    )
    gain_grad = lax.psum(gain_parts, ("fsdp", "tp"))
    qkv_owned, out_owned, gate_up_owned, down_owned = (
        lax.psum_scatter(
            qkv_grad.astype(jnp.bfloat16), "fsdp", scatter_dimension=1, tiled=True
        ).astype(jnp.float32),
        lax.psum_scatter(
            out_grad.astype(jnp.bfloat16), "fsdp", scatter_dimension=1, tiled=True
        ).astype(jnp.float32),
        lax.psum_scatter(
            gate_up_grad.astype(jnp.bfloat16), "fsdp", scatter_dimension=1, tiled=True
        ).astype(jnp.float32),
        lax.psum_scatter(
            down_grad.astype(jnp.bfloat16), "fsdp", scatter_dimension=1, tiled=True
        ).astype(jnp.float32),
    )
    return (layer_output, input_grad, gain_grad, qkv_owned, out_owned, gate_up_owned, down_owned)


def solution(mesh):
    in_specs = (
        P(("fsdp", "tp"), None),
        P(),
        P(None, "fsdp", "tp"),
        P("tp", "fsdp"),
        P(None, "fsdp", "tp"),
        P("tp", "fsdp"),
        P("fsdp"),
        P(("fsdp", "tp"), None),
    )
    out_specs = (
        P(("fsdp", "tp"), None),
        P(("fsdp", "tp"), None),
        P(),
        P(None, "fsdp", "tp"),
        P("tp", "fsdp"),
        P(None, "fsdp", "tp"),
        P("tp", "fsdp"),
    )
    return jax.shard_map(
        per_device, mesh=mesh, in_specs=in_specs, out_specs=out_specs, check_vma=False
    )
```

profile of v0, /device:TPU:8, one launch (start us, length us, event | category | flops | bytes accessed | tf_op | source)
XLA Modules:
  0.0 1254.8 jit_solution(167034253222710362)
XLA Ops:
  14.0 78.6 %all-gather.9.cloned.1.call-done = bf16[1024,2048]{1,0:T(8,128)(2,1)} async-done(((bf16[256,2048]{1,0:T(8,128)(2,1)}), bf16[1024,2048]{1,0:T(8,128)(2,1)}) %all-gather.9.cloned.1.call-update) | async-done | bytes 4194320 | tf_op jit(solution)/shard_map/all_gather | solution.py:70
  92.7 48.6 %all-gather.11.cloned.1.call-done = bf16[3,2048,512]{2,1,0:T(8,128)(2,1)} async-done(((bf16[3,256,512]{2,1,0:T(8,128)(2,1)}), bf16[3,2048,512]{2,1,0:T(8,128)(2,1)}) %all-gather.11.cloned.1.call-update) | async-done | bytes 6291472 | tf_op jit(solution)/shard_map/all_gather | solution.py:62
  172.5 36.5 %while.34 = (s32[]{:T(128)}, bf16[2,512,512]{2,1,0:T(8,128)(2,1)}, f32[2,4,512,1]{2,1,3,0:T(4,128)S(1)}, f32[2,4,512,1]{2,1,3,0:T(4,128)S(1)}, s32[2]{0:T(128)S(...) while((s32[]{:T(128)}, bf16[2,512,512]{2,1,0:T(8,128)(2,1)}, ...), condition=%wide.region_4.5_spmd, body=%wide.region_1.4_spmd.sunk | while | flops 1652292608 | bytes 54627104 | solution.py:98
  216.8 106.7 %reduce-scatter.9.cloned.1.call-done = bf16[256,2048]{1,0:T(8,128)(2,1)} async-done(((bf16[1024,2048]{1,0:T(8,128)(2,1)}), bf16[256,2048]{1,0:T(8,128)(2,1)}) %reduce-scatter.9.cloned.1.call-update) | async-done | bytes 1048592 | tf_op jit(solution)/shard_map/reduce_scatter | solution.py:100
  329.5 65.2 %all-gather.17.cloned.1.call-done = bf16[2,2048,1376]{1,2,0:T(8,128)(2,1)} async-done(((bf16[2,256,1376]{1,2,0:T(8,128)(2,1)}), bf16[2,2048,1376]{1,2,0:T(8,128)(2,1)}) %all-gather.17.cloned.1.call-update) | async-done | bytes 11272208 | tf_op jit(solution)/shard_map/all_gather | solution.py:64
  394.6 80.2 %all-gather.15.cloned.1.call-done = bf16[1024,2048]{1,0:T(8,128)(2,1)} async-done(((bf16[256,2048]{1,0:T(8,128)(2,1)}), bf16[1024,2048]{1,0:T(8,128)(2,1)}) %all-gather.15.cloned.1.call-update) | async-done | bytes 4194320 | tf_op jit(solution)/shard_map/all_gather | solution.py:109
  474.9 17.6 %convolution_bitcast_fusion = f32[2,1024,1376]{1,2,0:T(8,128)} fusion(bf16[2,2048,1376]{1,2,0:T(8,128)(2,1)} %all-gather.17.cloned.1.call-done, bf16[1024,2048]{1,0:T(8,128)(2,1)} %all-gather.15.cloned.1.call-done), kind=kOutput, calls=%fused_computation.43 | convolution fusion | flops 11542724608 | bytes 26738688 | tf_op jit(solution)/shard_map/td,sdf->stf/dot_general | solution.py:112
  492.4 63.4 %all-gather.21.cloned.1.call-done = bf16[1024,2048]{1,0:T(8,128)(2,1)} async-done(((bf16[256,2048]{1,0:T(8,128)(2,1)}), bf16[1024,2048]{1,0:T(8,128)(2,1)}) %all-gather.21.cloned.1.call-update) | async-done | bytes 4194320 | tf_op jit(solution)/shard_map/all_gather | solution.py:110
  555.8 47.0 %all-gather.19.cloned.1.call-done = bf16[1376,2048]{1,0:T(8,128)(2,1)} async-done(((bf16[1376,256]{1,0:T(8,128)(2,1)}), bf16[1376,2048]{1,0:T(8,128)(2,1)}) %all-gather.19.cloned.1.call-update) | async-done | bytes 5636112 | tf_op jit(solution)/shard_map/all_gather | solution.py:65
  602.8 14.8 %fusion.17 = (bf16[1,1024,1376]{1,2,0:T(8,128)(2,1)S(1)}, bf16[1,1024,1376]{1,2,0:T(8,128)(2,1)S(1)}, bf16[1024,1376]{0,1:T(8,128)(2,1)}) fusion(f32[2,1024,1376]{1,2,0:T(8,128)} %convolution_bitcast_fusion, bf16[1024,2048]{1,0:T(8,128)(2,1)} %all-gather.21.cloned.1.call-done, bf16[1376,2048]{1,0:T(8,128)(2,1)} %all-gather.19.cloned.1.call-done), kind=kOutput, calls=%fused_computation.74 | convolution fusion | flops 5793906688 | bytes 29556736 | tf_op jit(solution)/shard_map/dot_general | solution.py:134
  620.2 16.8 %bitcast_convert_fusion.1 = bf16[1024,2048]{1,0:T(8,128)(2,1)} fusion(bf16[2,2048,1376]{1,2,0:T(8,128)(2,1)} %all-gather.17.cloned.1.call-done, bf16[1,1024,1376]{1,2,0:T(8,128)(2,1)S(1)} %get-tuple-element.472, bf16[1,1024,1376]{1,2,0:T(8,128)(2,1)S(1)} %get-tuple-element.471), kind=kOutput, calls=%fused_computation.41 | convolution fusion | flops 11547639808 | bytes 21102592 | tf_op jit(solution)/shard_map/stf,sdf->td/dot_general | solution.py:146
  637.0 76.9 %reduce-scatter.13.cloned.1.call-done = bf16[256,2048]{1,0:T(8,128)(2,1)} async-done(((bf16[1024,2048]{1,0:T(8,128)(2,1)}), bf16[256,2048]{1,0:T(8,128)(2,1)}) %reduce-scatter.13.cloned.1.call-update) | async-done | bytes 1048592 | tf_op jit(solution)/shard_map/reduce_scatter | solution.py:145
  731.7 17.5 %convert_bitcast_fusion = bf16[2,2048,1376]{1,2,0:T(8,128)(2,1)} fusion(bf16[1024,2048]{1,0:T(8,128)(2,1)} %all-gather.15.cloned.1.call-done, bf16[1,1024,1376]{1,2,0:T(8,128)(2,1)} %copy-done.35, bf16[1,1024,1376]{1,2,0:T(8,128)(2,1)S(1)} %copy-done.34), kind=kOutput, calls=%fused_computation.39 | convolution fusion | flops 11551178752 | bytes 21102592 | tf_op jit(solution)/shard_map/td,stf->sdf/dot_general | solution.py:141
  749.2 49.0 %all-gather.23.cloned.1.call-done = bf16[1024,2048]{1,0:T(8,128)(2,1)} async-done(((bf16[256,2048]{1,0:T(8,128)(2,1)}), bf16[1024,2048]{1,0:T(8,128)(2,1)}) %all-gather.23.cloned.1.call-update) | async-done | bytes 4194320 | tf_op jit(solution)/shard_map/all_gather | solution.py:156
  808.0 159.6 %while.35 = (s32[]{:T(128)}, f32[2,2048,512]{2,1,0:T(8,128)}, bf16[2,512,512]{1,2,0:T(8,128)(2,1)}, s32[2]{0:T(128)S(1)}, bf16[1024,512]{0,1:T(8,128)(2,1)}, /*i...) while((s32[]{:T(128)}, f32[2,2048,512]{2,1,0:T(8,128)}, ...), condition=%wide.region_12.13_spmd, body=%wide.region_10.12_spmd.sunk | while | flops 4066378240 | bytes 306801408 | solution.py:195
  825.4 12.8 %multiply_reduce_fusion.3 = (f32[4,512]{1,0:T(4,128)S(1)}, f32[4,512,1536]{2,1,0:T(8,128)}) fusion(f32[4,512,1536]{2,1,0:T(8,128)} %exponential_divide_fusion.2, bf16[512,4,128]{0,2,1:T(8,128)(2,1)S(1)} %bitcast.181, bf16[1536,4,128]{0,2,1:T(8,128)(2,1)S(1)} %bitcast.180), kind=kOutput, calls=%fused_computation.19.clone.1 | convolution fusion | flops 811595776 | bytes 27271168 | tf_op jit(solution)/shard_map/while/body/eval_jaxpr/qhe,khe->hqk/dot_general | solution.py:172
  906.0 12.6 %multiply_reduce_fusion.3 = (f32[4,512]{1,0:T(4,128)S(1)}, f32[4,512,1536]{2,1,0:T(8,128)}) fusion(f32[4,512,1536]{2,1,0:T(8,128)} %exponential_divide_fusion.2, bf16[512,4,128]{0,2,1:T(8,128)(2,1)S(1)} %bitcast.181, bf16[1536,4,128]{0,2,1:T(8,128)(2,1)S(1)} %bitcast.180), kind=kOutput, calls=%fused_computation.19.clone.1 | convolution fusion | flops 811595776 | bytes 27271168 | tf_op jit(solution)/shard_map/while/body/eval_jaxpr/qhe,khe->hqk/dot_general | solution.py:172
  981.7 11.0 bitcast_convert_fusion
  992.8 11.0 convolution_convert_fusion.1
  1003.8 11.1 convert_bitcast_fusion.1
  1022.5 76.8 %reduce-scatter.15.cloned.1.call-done = bf16[256,2048]{1,0:T(8,128)(2,1)} async-done(((bf16[1024,2048]{1,0:T(8,128)(2,1)}), bf16[256,2048]{1,0:T(8,128)(2,1)}) %reduce-scatter.15.cloned.1.call-update) | async-done | bytes 1048592 | tf_op jit(solution)/shard_map/reduce_scatter | solution.py:205
  1101.4 45.5 %psum.7 = f32[2,2048]{1,0:T(2,128)} all-reduce(f32[2,2048]{1,0:T(2,128)S(1)} %pad_maximum_fusion.7), channel_id=1, replica_groups=mesh['fsdp'=8,'tp'=4] {'fsdp','tp'}, use_global_device_ids=true, to_apply=%region_17.18 | all-reduce | flops 4096 | bytes 32768 | tf_op jit(solution)/shard_map/psum | solution.py:219
  1146.9 33.0 %reduce-scatter.11.cloned.1.call-done = bf16[256,2048]{1,0:T(8,128)(2,1)} async-done(((bf16[1024,2048]{1,0:T(8,128)(2,1)}), bf16[256,2048]{1,0:T(8,128)(2,1)}) %reduce-scatter.11.cloned.1.call-update) | async-done | bytes 1048592 | tf_op jit(solution)/shard_map/reduce_scatter | solution.py:119
  1184.8 60.6 %reduce-scatter.17.cloned.1.call-done = bf16[3,256,512]{1,2,0:T(8,128)(2,1)} async-done(((bf16[3,2048,512]{1,2,0:T(8,128)(2,1)}), bf16[3,256,512]{1,2,0:T(8,128)(2,1)}) %reduce-scatter.17.cloned.1.call-update) | async-done | bytes 786448 | tf_op jit(solution)/shard_map/reduce_scatter | solution.py:221
  (267 shorter events, 276.3 us)
Async XLA Ops:
  7.2 85.5 %all-gather.9.cloned.1.call-start = ((), (), s32[]{:S(2)}) async-start(), calls=%async_computation.8 | async-start | bytes 5242880 | tf_op jit(solution)/shard_map/all_gather | solution.py:70
  13.2 128.1 %all-gather.11.cloned.1.call-start = ((), (), s32[]{:S(2)}) async-start(), calls=%async_computation.9 | async-start | bytes 7077888 | tf_op jit(solution)/shard_map/all_gather | solution.py:62
  14.0 195.0 %all-gather.13.cloned.1.call-start = ((), (), s32[]{:S(2)}) async-start(), calls=%async_computation.10 | async-start | bytes 2359296 | tf_op jit(solution)/shard_map/all_gather | solution.py:63
  154.6 6.3 collective-permute-start
  158.1 165.4 %reduce-scatter.9.cloned.1.call-start = ((), (), s32[]{:S(2)}) async-start(), calls=%async_computation.11 | async-start | bytes 5242880 | tf_op jit(solution)/shard_map/reduce_scatter | solution.py:100
  216.2 178.5 %all-gather.17.cloned.1.call-start = ((), (), s32[]{:S(2)}) async-start(), calls=%async_computation.13 | async-start | bytes 12681216 | tf_op jit(solution)/shard_map/all_gather | solution.py:64
  216.8 258.1 %all-gather.15.cloned.1.call-start = ((), (), s32[]{:S(2)}) async-start(), calls=%async_computation.12 | async-start | bytes 5242880 | tf_op jit(solution)/shard_map/all_gather | solution.py:109
  325.1 391.7 %copy-start.25 = (f32[256]{0:T(256)}, f32[256]{0:T(256)S(1)}, u32[]{:S(2)}) copy-start(f32[256]{0:T(256)S(1)} %add_rsqrt_fusion) | copy-start | bytes 3076
  327.8 228.1 %all-gather.21.cloned.1.call-start = ((), (), s32[]{:S(2)}) async-start(), calls=%async_computation.16 | async-start | bytes 5242880 | tf_op jit(solution)/shard_map/all_gather | solution.py:110
  328.5 274.3 %all-gather.19.cloned.1.call-start = ((), (), s32[]{:S(2)}) async-start(), calls=%async_computation.14 | async-start | bytes 6340608 | tf_op jit(solution)/shard_map/all_gather | solution.py:65
  329.3 384.7 %reduce-scatter.13.cloned.1.call-start = ((), (), s32[]{:S(2)}) async-start(), calls=%async_computation.17 | async-start | bytes 5242880 | tf_op jit(solution)/shard_map/reduce_scatter | solution.py:145
  637.0 161.2 %all-gather.23.cloned.1.call-start = ((), (), s32[]{:S(2)}) async-start(), calls=%async_computation.18 | async-start | bytes 5242880 | tf_op jit(solution)/shard_map/all_gather | solution.py:156
  719.4 295.6 %reduce-scatter.23.cloned.1.call-start = ((), (), s32[]{:S(2)}) async-start(), calls=%async_computation.23 | async-start | bytes 6340608 | tf_op jit(solution)/shard_map/reduce_scatter | solution.py:230
  729.7 287.7 %reduce-scatter.21.cloned.1.call-start = ((), (), s32[]{:S(2)}) async-start(), calls=%async_computation.22 | async-start | bytes 12681216 | tf_op jit(solution)/shard_map/reduce_scatter | solution.py:227
  749.2 271.6 %reduce-scatter.19.cloned.1.call-start = ((), (), s32[]{:S(2)}) async-start(), calls=%async_computation.21 | async-start | bytes 2359296 | tf_op jit(solution)/shard_map/reduce_scatter | solution.py:224
  970.3 7.9 collective-permute-start.1
  976.6 122.7 %reduce-scatter.15.cloned.1.call-start = ((), (), s32[]{:S(2)}) async-start(), calls=%async_computation.19 | async-start | bytes 5242880 | tf_op jit(solution)/shard_map/reduce_scatter | solution.py:205
  992.7 187.2 %reduce-scatter.11.cloned.1.call-start = ((), (), s32[]{:S(2)}) async-start(), calls=%async_computation.15 | async-start | bytes 5242880 | tf_op jit(solution)/shard_map/reduce_scatter | solution.py:119
  1003.8 241.6 %reduce-scatter.17.cloned.1.call-start = ((), (), s32[]{:S(2)}) async-start(), calls=%async_computation.20 | async-start | bytes 7077888 | tf_op jit(solution)/shard_map/reduce_scatter | solution.py:221
  1017.4 162.5 %copy-start.11 = (bf16[256,2048]{1,0:T(8,128)(2,1)S(1)}, bf16[256,2048]{1,0:T(8,128)(2,1)}, u32[]{:S(2)}) copy-start(bf16[256,2048]{1,0:T(8,128)(2,1)} %reduce-scatter.9.cloned.1.call-done) | copy-start | bytes 3145732
  1017.4 162.5 %copy-start.13 = (bf16[256,2048]{1,0:T(8,128)(2,1)S(1)}, bf16[256,2048]{1,0:T(8,128)(2,1)}, u32[]{:S(2)}) copy-start(bf16[256,2048]{1,0:T(8,128)(2,1)} %param.23) | copy-start | bytes 3145732
  1017.4 162.5 %copy-start.20 = (f32[1,2048]{1,0:T(1,128)S(1)}, f32[1,2048]{1,0:T(1,128)}, u32[]{:S(2)}) copy-start(f32[1,2048]{1,0:T(1,128)} %get-tuple-element.478) | copy-start | bytes 24580
  1017.4 162.5 %copy-start.26 = (f32[256]{0:T(256)S(1)}, f32[256]{0:T(256)}, u32[]{:S(2)}) copy-start(f32[256]{0:T(256)} %copy-done.25) | copy-start | bytes 3076
  1017.4 162.5 %copy-start.30 = (f32[256]{0:T(256)S(1)}, f32[256]{0:T(256)}, u32[]{:S(2)}) copy-start(f32[256]{0:T(256)} %copy-done.29) | copy-start | bytes 3076
  (50 other events, 1012.9 us)
Sparse Core Ops, SparseCore 0:
  13.4 79.2 all-gather.8
  94.6 46.6 all-gather.10
  158.2 31.4 all-gather.12
  216.3 107.1 reduce-scatter.8
  325.3 69.2 all-gather.16
  396.7 78.1 all-gather.14
  476.5 79.2 all-gather.20
  557.9 44.9 all-gather.18
  637.1 76.7 reduce-scatter.12
  719.5 78.6 all-gather.22
  801.7 59.6 reduce-scatter.22
  864.8 85.3 reduce-scatter.20
  976.7 43.6 reduce-scatter.18
  1022.5 76.7 reduce-scatter.14
  1101.6 78.3 reduce-scatter.10
  1183.2 62.2 reduce-scatter.16
where the time goes:
time: 1260 us; the launch traced here: 1250 us
  waiting for transfers between devices  789 us (63%)
  matrix products  206 us (16%)
  local copies, waits for them, and re-layouts  111 us (9%)
  other arithmetic  75 us (6%)
  blocking collectives  45.5 us (4%)
  between operations  14.5 us (1%)
    reduce_scatter x1, waiting for transfers between devices, per_device(): lax.psum_scatter(jnp.dot(heads_out, full_out, preferred_element_type=jnp....  107 us
    all_gather x1, waiting for transfers between devices, per_device(): lax.all_gather(normed_two, 'tp', axis=0, tiled=True)  80.2 us
    all_gather x1, waiting for transfers between devices, per_device(): attn_rows = lax.all_gather(normed_one, 'tp', axis=0, tiled=True)  78.6 us
    reduce_scatter x1, waiting for transfers between devices, per_device(): lax.psum_scatter(jnp.einsum('stf,sdf->td', piece, full_gate_up, preferred...  76.9 us
    reduce_scatter x1, waiting for transfers between devices, per_device(): lax.psum_scatter(jnp.einsum('ste,sde->td', piece, full_qkv, preferred_ele...  76.8 us
    all_gather x1, waiting for transfers between devices, per_device(): lax.all_gather(w_gate_up, 'fsdp', axis=1, tiled=True)  65.2 us
    all_gather x1, waiting for transfers between devices, per_device(): lax.all_gather(out_cotangent, 'tp', axis=0, tiled=True)  63.4 us
    reduce_scatter x1, waiting for transfers between devices, per_device(): lax.psum_scatter(qkv_grad.astype(jnp.bfloat16), 'fsdp', scatter_dimension...  60.6 us
  transfers between devices with their start and end apart: 18, of which 13 were waited for; matrix products, arithmetic and copies ran while one was open for 25% of the time, Pallas kernels for 0%

commit v1 on v0

v1 whole, which is shorter than its diff:
```python
import functools
import math

import jax
import jax.numpy as jnp
from jax import lax
from jax.experimental import pallas as pl
from jax.experimental.pallas import tpu as pltpu
from jax.sharding import PartitionSpec as P

HEAD_DIM = 128
WINDOW = 1024
SEQ_LEN = 4096
QB = 256
SCALE = 1.0 / math.sqrt(HEAD_DIM)
LOG2E = 1.4426950408889634
EPS = 1e-06
MASKED = -1e30
NT = (((1,), (1,)), ((), ()))

def nt(a, b): return lax.dot_general(a, b, NT, preferred_element_type=jnp.float32)
def nn(a, b): return jnp.dot(a, b, preferred_element_type=jnp.float32)

def masked_scores(k_j, q, j, lo):
    s = nt(k_j, q)
    row = lax.broadcasted_iota(jnp.int32, s.shape, 0) + j * QB
    ok = row >= lo
    if (j + 1) * QB > WINDOW:
        hi = lax.broadcasted_iota(jnp.int32, (1, QB), 1) + WINDOW
        ok = ok & (row <= hi)
    return jnp.where(ok, s, MASKED)

def low_bound(doc_ref, b, off):
    q_row = lax.broadcasted_iota(jnp.int32, (1, QB), 1)
    doc = doc_ref[:, b * QB:(b + 1) * QB]
    return jnp.maximum(q_row + 1, doc - off + (WINDOW - b * QB))

def attend_kernel(off_ref, doc_ref, q_ref, kp_ref, vp_ref, ko_ref, vo_ref, o_ref, lse_ref, k_s, vt_s):
    h = pl.program_id(0)
    off = off_ref[0]
    span = q_ref.shape[0]
    k_s[:WINDOW] = kp_ref[...]
    k_s[WINDOW:] = ko_ref[...]
    vt_s[:, :WINDOW] = vp_ref[...].T
    vt_s[:, WINDOW:] = vo_ref[...].T
    c = SCALE * LOG2E
    n = WINDOW // QB + 1
    for b in range(span // QB):
        q = q_ref[b * QB:(b + 1) * QB]
        lo = low_bound(doc_ref, b, off)
        ss = [masked_scores(k_s[(b + j) * QB:(b + j + 1) * QB], q, j, lo) for j in range(n)]
        m = functools.reduce(jnp.maximum, [jnp.max(s, axis=0, keepdims=True) for s in ss])
        l = jnp.zeros((1, QB), jnp.float32)
        acc = jnp.zeros((HEAD_DIM, QB), jnp.float32)
        for j in range(n):
            p = jnp.exp2((ss[j] - m) * c)
            l = l + jnp.sum(p, axis=0, keepdims=True)
            acc = acc + nn(vt_s[:, (b + j) * QB:(b + j + 1) * QB], p.astype(jnp.bfloat16))
        o_ref[b * QB:(b + 1) * QB] = (acc / l).T.astype(o_ref.dtype)
        lse_ref[pl.ds(h, 1), b * QB:(b + 1) * QB] = m * c + jnp.log2(l)

def back_kernel(off_ref, doc_ref, lse_ref, q_ref, do_ref, kp_ref, vp_ref, ko_ref, vo_ref,
                dq_ref, dkp_ref, dvp_ref, dko_ref, dvo_ref, k_s, v_s, kt_s, dk_s, dv_s):
    h = pl.program_id(0)
    off = off_ref[0]
    span = q_ref.shape[0]
    k_s[:WINDOW] = kp_ref[...]
    k_s[WINDOW:] = ko_ref[...]
    v_s[:WINDOW] = vp_ref[...]
    v_s[WINDOW:] = vo_ref[...]
    kt_s[:, :WINDOW] = kp_ref[...].T
    kt_s[:, WINDOW:] = ko_ref[...].T
    c = SCALE * LOG2E
    n = WINDOW // QB + 1
    seen = 0
    for b in range(span // QB):
        q = q_ref[b * QB:(b + 1) * QB]
        do = do_ref[b * QB:(b + 1) * QB]
        lse = lse_ref[pl.ds(h, 1), b * QB:(b + 1) * QB]
        lo = low_bound(doc_ref, b, off)
        delta = jnp.zeros((1, QB), jnp.float32)
        ps, dps = [], []
        for j in range(n):
            rows = slice((b + j) * QB, (b + j + 1) * QB)
            s = masked_scores(k_s[rows], q, j, lo)
            p = jnp.exp2(s * c - lse)
            dp = nt(v_s[rows], do)
            delta = delta + jnp.sum(p * dp, axis=0, keepdims=True)
            dv = nn(p.astype(jnp.bfloat16), do)
            if b + j >= seen:
                dv_s[rows] = dv
            else:
                dv_s[rows] += dv
            ps.append(p); dps.append(dp)
        dqt = jnp.zeros((HEAD_DIM, QB), jnp.float32)
        for j in range(n):
            rows = slice((b + j) * QB, (b + j + 1) * QB)
            ds = (ps[j] * (dps[j] - delta)).astype(jnp.bfloat16)
            dk = nn(ds, q)
            if b + j >= seen:
                dk_s[rows] = dk
            else:
                dk_s[rows] += dk
            dqt = dqt + nn(kt_s[:, rows], ds)
        seen = b + n
        dq_ref[b * QB:(b + 1) * QB] = (dqt * SCALE).T.astype(dq_ref.dtype)
    dkp_ref[...] = (dk_s[:WINDOW] * SCALE).astype(dkp_ref.dtype)
    dvp_ref[...] = dv_s[:WINDOW].astype(dvp_ref.dtype)
    dko_ref[...] = dk_s[WINDOW:] * SCALE
    dvo_ref[...] = dv_s[WINDOW:]

def head_spec(rows): return pl.BlockSpec((rows, HEAD_DIM), lambda h: (0, h))
def whole(shape): return pl.BlockSpec(shape, lambda h: (0, 0))

def attend(off, doc, q, kp, vp, ko, vo):
    span, width = q.shape
    heads = width // HEAD_DIM
    return pl.pallas_call(
        attend_kernel, grid=(heads,),
        in_specs=[pl.BlockSpec(memory_space=pltpu.SMEM), whole((1, span)), head_spec(span), head_spec(WINDOW), head_spec(WINDOW), head_spec(span), head_spec(span)],
        out_specs=[head_spec(span), whole((heads, span))],
        out_shape=[jax.ShapeDtypeStruct((span, width), jnp.bfloat16), jax.ShapeDtypeStruct((heads, span), jnp.float32)],
        scratch_shapes=[pltpu.VMEM((WINDOW + span, HEAD_DIM), jnp.bfloat16), pltpu.VMEM((HEAD_DIM, WINDOW + span), jnp.bfloat16)],
        compiler_params=pltpu.CompilerParams(vmem_limit_bytes=40 << 20),
        cost_estimate=pl.CostEstimate(flops=4 * heads * span * 1280 * HEAD_DIM, bytes_accessed=6 * span * width * 2, transcendentals=heads * span * 1280),
    )(off, doc, q, kp, vp, ko, vo)

def attend_back(off, doc, lse, q, do, kp, vp, ko, vo):
    span, width = q.shape
    heads = width // HEAD_DIM
    bf, f32 = jnp.bfloat16, jnp.float32
    sd = lambda rows, t: jax.ShapeDtypeStruct((rows, width), t)
    return pl.pallas_call(
        back_kernel, grid=(heads,),
        in_specs=[pl.BlockSpec(memory_space=pltpu.SMEM), whole((1, span)), whole((heads, span)), head_spec(span), head_spec(span), head_spec(WINDOW), head_spec(WINDOW), head_spec(span), head_spec(span)],
        out_specs=[head_spec(span), head_spec(WINDOW), head_spec(WINDOW), head_spec(span), head_spec(span)],
        out_shape=[sd(span, bf), sd(WINDOW, bf), sd(WINDOW, bf), sd(span, f32), sd(span, f32)],
        scratch_shapes=[pltpu.VMEM((WINDOW + span, HEAD_DIM), bf)] * 2 + [pltpu.VMEM((HEAD_DIM, WINDOW + span), bf)] + [pltpu.VMEM((WINDOW + span, HEAD_DIM), f32)] * 2,
        compiler_params=pltpu.CompilerParams(vmem_limit_bytes=40 << 20),
        cost_estimate=pl.CostEstimate(flops=10 * heads * span * 1280 * HEAD_DIM, bytes_accessed=14 * span * width * 2, transcendentals=heads * span * 1280),
    )(off, doc, lse, q, do, kp, vp, ko, vo)

PAIRS = [(0, 1), (1, 0), (2, 3), (3, 2)]
MIDDLE = [(1, 2), (2, 1)]
OUTWARD = [(1, 0), (2, 3)]
INWARD = [(0, 1), (3, 2)]


def is_middle():
    me = lax.axis_index("tp")
    return (me == 1) | (me == 2)


def send(block, route, axis="tp"):
    return lax.ppermute(block, axis, route)


def gather_rows(block):
    me = lax.axis_index("tp")
    rows = block.shape[0]
    mid = is_middle()
    one = send(block, PAIRS)
    near = send(block, MIDDLE)
    far = send(one, MIDDLE)
    two = jnp.where(mid, far, send(near, OUTWARD))
    three = jnp.where(mid, near, send(far, OUTWARD))
    whole_rows = jnp.zeros((4 * rows,) + block.shape[1:], block.dtype)
    for k, part in enumerate((block, one, two, three)):
        whole_rows = lax.dynamic_update_slice_in_dim(whole_rows, part, (me ^ k) * rows, 0)
    return whole_rows


def scatter_rows(part_of):
    three = part_of(3)
    t1 = send(three, INWARD)
    two = part_of(2)
    t2 = send(two, INWARD)
    t3 = send(two + t1, MIDDLE)
    one = part_of(1)
    t4 = send(three + t2, MIDDLE)
    t5 = send(one + t3, PAIRS)
    own = part_of(0)
    f32 = jnp.float32
    return own.astype(f32) + t4.astype(f32) + t5.astype(f32)


def row_parts(partial):
    me = lax.axis_index("tp")
    rows = partial.shape[0] // 4
    return lambda k: lax.dynamic_slice_in_dim(partial, (me ^ k) * rows, rows, 0)


def sum_everywhere(values):
    for axis in ("tp", "fsdp"):
        size = lax.axis_size(axis)
        step = 1
        while step < size:
            values = values + send(values, [(i, i ^ step) for i in range(size)], axis)
            step *= 2
    return values


def behind_route(axis, distance, per_seq):
    size = lax.axis_size(axis)
    pairs = [(i - 1, i) for i in range(1, size) if i % per_seq]
    return pairs if distance > 0 else [(b, a) for a, b in pairs]


def normalize(values):
    inverse = lax.rsqrt(jnp.mean(values * values, axis=-1, keepdims=True) + EPS)
    return (values * inverse, inverse)


def norm_back(grad, gain, unit, inverse):
    scaled = grad * gain
    return inverse * (scaled - unit * jnp.mean(scaled * unit, axis=-1, keepdims=True))


def per_device(layer_input, norm_gains, w_qkv, w_out, w_gate_up, w_down, doc_start, out_cotangent):
    bf, f32 = jnp.bfloat16, jnp.float32
    span_len = doc_start.shape[0]
    offset = (lax.axis_index("fsdp") * span_len).astype(jnp.int32).reshape(1)
    doc_row = doc_start.reshape(1, span_len)
    per_seq = SEQ_LEN // span_len
    full_qkv = lax.all_gather(w_qkv, "fsdp", axis=1, tiled=True)
    full_out = lax.all_gather(w_out, "fsdp", axis=1, tiled=True)
    full_gate_up = lax.all_gather(w_gate_up, "fsdp", axis=1, tiled=True)
    full_down = lax.all_gather(w_down, "fsdp", axis=1, tiled=True)
    input_f32 = layer_input.astype(f32)
    unit_one, inverse_one = normalize(input_f32)
    normed_one = (unit_one * norm_gains[0]).astype(bf)
    attn_rows = gather_rows(normed_one)
    cot_rows = gather_rows(out_cotangent)
    keys = nn(attn_rows, full_qkv[1]).astype(bf)
    values = nn(attn_rows, full_qkv[2]).astype(bf)
    prev_k = send(keys, behind_route("fsdp", 1, per_seq), "fsdp")
    prev_v = send(values, behind_route("fsdp", 1, per_seq), "fsdp")
    queries = nn(attn_rows, full_qkv[0]).astype(bf)
    heads_out, lse = attend(offset, doc_row, queries, prev_k, prev_v, keys, values)
    attn_part = nn(heads_out, full_out).astype(bf)
    residual_mid = input_f32 + scatter_rows(row_parts(attn_part))
    unit_two, inverse_two = normalize(residual_mid)
    normed_two = (unit_two * norm_gains[1]).astype(bf)
    mlp_rows = gather_rows(normed_two)
    gate_up = jnp.einsum("td,sdf->stf", mlp_rows, full_gate_up, preferred_element_type=f32)
    gate_pre = gate_up[0]
    up_pre = gate_up[1]
    sigmoid_gate = jax.nn.sigmoid(gate_pre)
    act = (gate_pre * sigmoid_gate * up_pre).astype(bf)
    contract_first = (((0,), (0,)), ((), ()))
    contract_last = (((1,), (1,)), ((), ()))
    grad_act = lax.dot_general(cot_rows, full_down, contract_last, preferred_element_type=f32)
    grad_up = grad_act * gate_pre * sigmoid_gate
    grad_gate = grad_act * up_pre * sigmoid_gate * (1.0 + gate_pre * (1.0 - sigmoid_gate))
    grad_gate_up = jnp.stack([grad_gate, grad_up]).astype(bf)
    gn2_part = jnp.einsum("stf,sdf->td", grad_gate_up, full_gate_up, preferred_element_type=f32)
    grad_normed_two = scatter_rows(row_parts(gn2_part.astype(bf)))
    down_part = nn(act, full_down).astype(bf)
    layer_output = (residual_mid + scatter_rows(row_parts(down_part))).astype(bf)
    down_grad = lax.dot_general(act, cot_rows, contract_first, preferred_element_type=f32)
    gate_up_grad = jnp.einsum("td,stf->sdf", mlp_rows, grad_gate_up, preferred_element_type=f32)
    grad_mid = out_cotangent.astype(f32) + norm_back(
        grad_normed_two, norm_gains[1], unit_two, inverse_two
    )
    grad_branch = gather_rows(grad_mid.astype(bf))
    grad_heads = lax.dot_general(
        grad_branch, full_out, contract_last, preferred_element_type=f32
    ).astype(bf)
    out_grad = lax.dot_general(heads_out, grad_branch, contract_first, preferred_element_type=f32)
    grad_q, prev_dk, prev_dv, own_dk, own_dv = attend_back(
        offset, doc_row, lse, queries, grad_heads, prev_k, prev_v, keys, values
    )
    back_route = behind_route("fsdp", -1, per_seq)
    grad_k = (own_dk + send(prev_dk, back_route, "fsdp").astype(f32)).astype(bf)
    grad_v = (own_dv + send(prev_dv, back_route, "fsdp").astype(f32)).astype(bf)
    grad_qkv = jnp.stack([grad_q, grad_k, grad_v])
    gn1_part = jnp.einsum("ste,sde->td", grad_qkv, full_qkv, preferred_element_type=f32)
    gn1_part = gn1_part.astype(bf)
    grad_normed_one = scatter_rows(row_parts(gn1_part))
    qkv_grad = jnp.einsum("td,ste->sde", attn_rows, grad_qkv, preferred_element_type=f32)
    input_grad = (
        grad_mid + norm_back(grad_normed_one, norm_gains[0], unit_one, inverse_one)
    ).astype(bf)
    gain_one = jnp.sum(gn1_part.astype(f32) * attn_rows.astype(f32), axis=0) / norm_gains[0]
    gain_two = jnp.sum(grad_normed_two * unit_two, axis=0)
    gain_grad = sum_everywhere(jnp.stack([gain_one, gain_two]))
    owned = [
        lax.psum_scatter(g.astype(bf), "fsdp", scatter_dimension=1, tiled=True).astype(f32)
        for g in (down_grad, gate_up_grad, out_grad, qkv_grad)
    ]
    return (layer_output, input_grad, gain_grad, owned[3], owned[2], owned[1], owned[0])


def solution(mesh):
    in_specs = (
        P(("fsdp", "tp"), None),
        P(),
        P(None, "fsdp", "tp"),
        P("tp", "fsdp"),
        P(None, "fsdp", "tp"),
        P("tp", "fsdp"),
        P("fsdp"),
        P(("fsdp", "tp"), None),
    )
    out_specs = (
        P(("fsdp", "tp"), None),
        P(("fsdp", "tp"), None),
        P(),
        P(None, "fsdp", "tp"),
        P("tp", "fsdp"),
        P(None, "fsdp", "tp"),
        P("tp", "fsdp"),
    )
    return jax.shard_map(
        per_device, mesh=mesh, in_specs=in_specs, out_specs=out_specs, check_vma=False
    )
```

time: 1260 us -> 818 us (0.65)
  waiting for transfers between devices: 789 us -> 438 us
  starting transfers between devices: 6.11 us -> 112 us
  local copies, waits for them, and re-layouts: 111 us -> 23.8 us
  matrix products: 206 us -> 132 us
  blocking collectives: 45.5 us -> 0 us
  Pallas kernels: 0 us -> 35.6 us
  other arithmetic: 75 us -> 53.7 us
    ppermute x2 -> x49, waiting for transfers between devices: 0.32 us -> 436 us  [send(): return lax.ppermute(block, axis, route)]
    all_gather x8 -> x4, waiting for transfers between devices: 432 us -> 0.01 us  [the longest x1 0.01 us: per_device(): full_qkv = lax.all_gather(w_qkv, 'fsdp', axis=1, tiled=True)]
    reduce_scatter x8 -> x4, waiting for transfers between devices: 354 us -> 0.01 us  [per_device(): lax.psum_scatter(g.astype(bf), 'fsdp', scatter_dimension=1, tiled=True)]
    ppermute x2 -> x49, starting transfers between devices: 4.76 us -> 111 us  [send(): return lax.ppermute(block, axis, route)]
    dot_general x21 -> x9, matrix products: 145 us -> 72.7 us  [the longest x5 27.1 us: nn(): return jnp.dot(a, b, preferred_element_type=jnp.float32)]
    psum x1 -> x0, blocking collectives: 45.5 us -> none  [per_device(): gain_grad = lax.psum(gain_parts, ('fsdp', 'tp'))]
    dynamic_slice x26 -> x4, local copies, waits for them, and re-layouts: 43.1 us -> 0.4 us  [row_parts(): return lambda k: lax.dynamic_slice_in_dim(partial, (me ^ k) * rows, rows, 0)]
    pallas_call x0 -> x2, Pallas kernels: none -> 35.6 us  [the longest x1 22.6 us: attend_back(): pl.pallas_call(back_kernel, grid=(heads,), in_specs=[pl.BlockSpec(memory_...]
  transfers between devices with their start and end apart: 18 -> 57, of which waited for: 13 -> 34; matrix products, arithmetic and copies ran while one was open for 25% -> 22% of each run, Pallas kernels for 0% -> 4%
where the time goes in v1:
time: 818 us; the launch traced here: 810 us
  waiting for transfers between devices  438 us (54%)
  matrix products  132 us (16%)
  starting transfers between devices  112 us (14%)
  other arithmetic  53.7 us (7%)
  Pallas kernels  35.6 us (4%)
  local copies, waits for them, and re-layouts  23.8 us (3%)
  between operations  15.5 us (2%)
    ppermute x49, waiting for transfers between devices, send(): return lax.ppermute(block, axis, route)  436 us
    ppermute x49, starting transfers between devices, send(): return lax.ppermute(block, axis, route)  111 us
    dot_general x5, matrix products, nn(): return jnp.dot(a, b, preferred_element_type=jnp.float32)  27.1 us
    pallas_call x1, Pallas kernels, attend_back(): pl.pallas_call(back_kernel, grid=(heads,), in_specs=[pl.BlockSpec(memory_...  22.6 us
    dot_general x1, matrix products, per_device(): jnp.einsum('td,sdf->stf', mlp_rows, full_gate_up, preferred_element_type=...  17.6 us
    dot_general x1, matrix products, per_device(): jnp.einsum('td,stf->sdf', mlp_rows, grad_gate_up, preferred_element_type=...  17.5 us
  transfers between devices with their start and end apart: 57, of which 34 were waited for; matrix products, arithmetic and copies ran while one was open for 22% of the time, Pallas kernels for 4%

profile of v1, /device:TPU:8, one launch (start us, length us, event | category | flops | bytes accessed | tf_op | source)
XLA Modules:
  0.0 810.4 jit_solution(11764799483958244394)
XLA Ops:
  19.8 19.8 %collective-permute-done = bf16[256,2048]{1,0:T(8,128)(2,1)S(1)} collective-permute-done((bf16[256,2048]{1,0:T(8,128)(2,1)S(1)}, bf16[256,2048]{1,0:T(8,128)(2,1)S(1)}, u32[]{:S(2)}, u32[]{:S(2)}) %collective-permute-start) | collective-permute-done | bytes 1048608 | tf_op jit(solution)/shard_map/ppermute | solution.py:155
  45.4 20.2 %collective-permute-done.1 = bf16[256,2048]{1,0:T(8,128)(2,1)S(1)} collective-permute-done((bf16[256,2048]{1,0:T(8,128)(2,1)S(1)}, bf16[256,2048]{1,0:T(8,128)(2,1)S(1)}, u32[]{:S(2)}, u32[]{:S(2)}) %collective-permute-start.1) | collective-permute-done | bytes 1048608 | tf_op jit(solution)/shard_map/ppermute | solution.py:155
  70.4 18.0 %collective-permute-done.4 = bf16[256,2048]{1,0:T(8,128)(2,1)} collective-permute-done((bf16[256,2048]{1,0:T(8,128)(2,1)S(1)}, bf16[256,2048]{1,0:T(8,128)(2,1)}, u32[]{:S(2)}, u32[]{:S(2)}) %collective-permute-start.4) | collective-permute-done | bytes 1048608 | tf_op jit(solution)/shard_map/ppermute | solution.py:155
  132.7 16.0 %collective-permute-done.7 = bf16[256,2048]{1,0:T(8,128)(2,1)S(1)} collective-permute-done((bf16[256,2048]{1,0:T(8,128)(2,1)S(1)}, bf16[256,2048]{1,0:T(8,128)(2,1)S(1)}, u32[]{:S(2)}, u32[]{:S(2)}) %collective-permute-start.7) | collective-permute-done | bytes 1048608 | tf_op jit(solution)/shard_map/ppermute | solution.py:155
  151.3 15.4 %collective-permute-done.9 = bf16[256,2048]{1,0:T(8,128)(2,1)S(1)} collective-permute-done((bf16[256,2048]{1,0:T(8,128)(2,1)S(1)}, bf16[256,2048]{1,0:T(8,128)(2,1)S(1)}, u32[]{:S(2)}, u32[]{:S(2)}) %collective-permute-start.9) | collective-permute-done | bytes 1048608 | tf_op jit(solution)/shard_map/ppermute | solution.py:155
  196.2 13.8 %collective-permute-done.11 = bf16[256,2048]{1,0:T(8,128)(2,1)S(1)} collective-permute-done((bf16[256,2048]{1,0:T(8,128)(2,1)S(1)}, bf16[256,2048]{1,0:T(8,128)(2,1)S(1)}, u32[]{:S(2)}, u32[]{:S(2)}) %collective-permute-start.11) | collective-permute-done | bytes 1048608 | tf_op jit(solution)/shard_map/ppermute | solution.py:155
  238.5 13.8 %collective-permute-done.23 = bf16[256,2048]{1,0:T(8,128)(2,1)S(1)} collective-permute-done((bf16[256,2048]{1,0:T(8,128)(2,1)S(1)}, bf16[256,2048]{1,0:T(8,128)(2,1)S(1)}, u32[]{:S(2)}, u32[]{:S(2)}) %collective-permute-start.23) | collective-permute-done | bytes 1048608 | tf_op jit(solution)/shard_map/ppermute | solution.py:155
  258.5 16.3 %collective-permute-done.14 = bf16[256,2048]{1,0:T(8,128)(2,1)S(1)} collective-permute-done((bf16[256,2048]{1,0:T(8,128)(2,1)S(1)}, bf16[256,2048]{1,0:T(8,128)(2,1)S(1)}, u32[]{:S(2)}, u32[]{:S(2)}) %collective-permute-start.14) | collective-permute-done | bytes 1048608 | tf_op jit(solution)/shard_map/ppermute | solution.py:155
  277.6 19.4 %collective-permute-done.13 = bf16[256,2048]{1,0:T(8,128)(2,1)S(1)} collective-permute-done((bf16[256,2048]{1,0:T(8,128)(2,1)S(1)}, bf16[256,2048]{1,0:T(8,128)(2,1)S(1)}, u32[]{:S(2)}, u32[]{:S(2)}) %collective-permute-start.13) | collective-permute-done | bytes 1048608 | tf_op jit(solution)/shard_map/ppermute | solution.py:155
  302.4 19.8 %collective-permute-done.16 = bf16[256,2048]{1,0:T(8,128)(2,1)S(1)} collective-permute-done((bf16[256,2048]{1,0:T(8,128)(2,1)S(1)}, bf16[256,2048]{1,0:T(8,128)(2,1)S(1)}, u32[]{:S(2)}, u32[]{:S(2)}) %collective-permute-start.16) | collective-permute-done | bytes 1048608 | tf_op jit(solution)/shard_map/ppermute | solution.py:155
  323.6 17.6 %convolution_bitcast_fusion = f32[2,1024,1376]{1,2,0:T(8,128)} fusion(bf16[2,2048,1376]{1,2,0:T(8,128)(2,1)} %all-gather.9.cloned.1.call-done, bf16[1024,2048]{1,0:T(8,128)(2,1)} %select_dynamic-update-slice_fusion.4), kind=kOutput, calls=%fused_computation.5 | convolution fusion | flops 11542724608 | bytes 26738688 | tf_op jit(solution)/shard_map/td,sdf->stf/dot_general | solution.py:245
  341.2 14.9 %fusion.7 = (bf16[1,1024,1376]{1,2,0:T(8,128)(2,1)S(1)}, bf16[1,1024,1376]{1,2,0:T(8,128)(2,1)}, bf16[1024,1376]{0,1:T(8,128)(2,1)S(1)}) fusion(f32[2,1024,1376]{1,2,0:T(8,128)} %convolution_bitcast_fusion, bf16[1024,2048]{1,0:T(8,128)(2,1)} %select_dynamic-update-slice_fusion.2, bf16[1376,2048]{1,0:T(8,128)(2,1)} %all-gather.11.cloned.1.call-done), kind=kOutput, calls=%fused_computation.28 | convolution fusion | flops 5793906688 | bytes 29556736 | tf_op jit(solution)/shard_map/dot_general | solution.py:252
  365.2 16.0 %bitcast_convert_fusion.1 = bf16[1024,2048]{1,0:T(8,128)(2,1)S(1)} fusion(bf16[2,2048,1376]{1,2,0:T(8,128)(2,1)} %all-gather.9.cloned.1.call-done, bf16[1,1024,1376]{1,2,0:T(8,128)(2,1)} %get-tuple-element.48, bf16[1,1024,1376]{1,2,0:T(8,128)(2,1)S(1)} %get-tuple-element.47), kind=kOutput, calls=%fused_computation.2 | convolution fusion | flops 11547639808 | bytes 21102592 | tf_op jit(solution)/shard_map/stf,sdf->td/dot_general | solution.py:256
  421.7 17.5 %collective-permute-done.29 = bf16[256,2048]{1,0:T(8,128)(2,1)} collective-permute-done((bf16[256,2048]{1,0:T(8,128)(2,1)}, bf16[256,2048]{1,0:T(8,128)(2,1)}, u32[]{:S(2)}, u32[]{:S(2)}) %collective-permute-start.29) | collective-permute-done | bytes 1048608 | tf_op jit(solution)/shard_map/ppermute | solution.py:155
  458.2 16.7 %collective-permute-done.18 = bf16[256,2048]{1,0:T(8,128)(2,1)S(1)} collective-permute-done((bf16[256,2048]{1,0:T(8,128)(2,1)S(1)}, bf16[256,2048]{1,0:T(8,128)(2,1)S(1)}, u32[]{:S(2)}, u32[]{:S(2)}) %collective-permute-start.18) | collective-permute-done | bytes 1048608 | tf_op jit(solution)/shard_map/ppermute | solution.py:155
  474.9 22.5 %collective-permute-done.28 = bf16[256,2048]{1,0:T(8,128)(2,1)S(1)} collective-permute-done((bf16[256,2048]{1,0:T(8,128)(2,1)S(1)}, bf16[256,2048]{1,0:T(8,128)(2,1)S(1)}, u32[]{:S(2)}, u32[]{:S(2)}) %collective-permute-start.28) | collective-permute-done | bytes 1048608 | tf_op jit(solution)/shard_map/ppermute | solution.py:155
  507.9 20.6 %collective-permute-done.32 = bf16[256,2048]{1,0:T(8,128)(2,1)S(1)} collective-permute-done((bf16[256,2048]{1,0:T(8,128)(2,1)S(1)}, bf16[256,2048]{1,0:T(8,128)(2,1)S(1)}, u32[]{:S(2)}, u32[]{:S(2)}) %collective-permute-start.32) | collective-permute-done | bytes 1048608 | tf_op jit(solution)/shard_map/ppermute | solution.py:155
  549.5 19.8 %collective-permute-done.36 = bf16[256,2048]{1,0:T(8,128)(2,1)S(1)} collective-permute-done((bf16[256,2048]{1,0:T(8,128)(2,1)S(1)}, bf16[256,2048]{1,0:T(8,128)(2,1)S(1)}, u32[]{:S(2)}, u32[]{:S(2)}) %collective-permute-start.36) | collective-permute-done | bytes 1048608 | tf_op jit(solution)/shard_map/ppermute | solution.py:155
  575.6 17.5 %convert_bitcast_fusion = bf16[2,2048,1376]{1,2,0:T(8,128)(2,1)} fusion(bf16[1024,2048]{1,0:T(8,128)(2,1)} %select_dynamic-update-slice_fusion.4, bf16[1,1024,1376]{1,2,0:T(8,128)(2,1)} %get-tuple-element.48, bf16[1,1024,1376]{1,2,0:T(8,128)(2,1)} %copy-done.31), kind=kOutput, calls=%fused_computation | convolution fusion | flops 11551178752 | bytes 21102592 | tf_op jit(solution)/shard_map/td,stf->sdf/dot_general | solution.py:261
  598.7 22.6 %shard_map.136 = (bf16[1024,512]{1,0:T(8,128)(2,1)S(1)}, bf16[1024,512]{1,0:T(8,128)(2,1)S(1)}, bf16[1024,512]{1,0:T(8,128)(2,1)S(1)}, f32[1024,512]{1,0:T(8,128)S(1)}, f32[1024,512]{1,0:T(8,128)S(1)}) custom-call(s32[1]{0:T(128)} %bitcast.off_ref, s32[1,1024]{1,0:T(1,128)S(1)} %bitcast.87, f32[4,1024]{1,0:T(4,128)S(1)} %get-tuple-element.15.lse_ref, ...), custom_call_target="tpu_custom_call" | custom-call | flops 6710886400 | bytes 14680064 | tf_op jit(solution)/shard_map/pallas_call | solution.py:133
  624.2 26.7 %collective-permute-done.37 = bf16[1024,512]{1,0:T(8,128)(2,1)S(1)} collective-permute-done((bf16[1024,512]{1,0:T(8,128)(2,1)S(1)}, bf16[1024,512]{1,0:T(8,128)(2,1)S(1)}, u32[]{:S(2)}, u32[]{:S(2)}) %collective-permute-start.37) | collective-permute-done | bytes 1048608 | tf_op jit(solution)/shard_map/ppermute | solution.py:155
  676.8 15.4 %collective-permute-done.39 = bf16[256,2048]{1,0:T(8,128)(2,1)S(1)} collective-permute-done((bf16[256,2048]{1,0:T(8,128)(2,1)S(1)}, bf16[256,2048]{1,0:T(8,128)(2,1)S(1)}, u32[]{:S(2)}, u32[]{:S(2)}) %collective-permute-start.39) | collective-permute-done | bytes 1048608 | tf_op jit(solution)/shard_map/ppermute | solution.py:155
  695.0 25.4 %collective-permute-done.41 = bf16[256,2048]{1,0:T(8,128)(2,1)S(1)} collective-permute-done((bf16[256,2048]{1,0:T(8,128)(2,1)S(1)}, bf16[256,2048]{1,0:T(8,128)(2,1)S(1)}, u32[]{:S(2)}, u32[]{:S(2)}) %collective-permute-start.41) | collective-permute-done | bytes 1048608 | tf_op jit(solution)/shard_map/ppermute | solution.py:155
  758.9 20.7 %collective-permute-start.46 = (f32[2,2048]{1,0:T(2,128)S(1)}, f32[2,2048]{1,0:T(2,128)S(1)}, u32[]{:S(2)}, u32[]{:S(2)}) collective-permute-start(f32[2,2048]{1,0:T(2,128)S(1)} %fusion.52), channel_id=1, source_target_pairs={{0,4},{4,0},{8,12},{12,8},{16,20},{20,16},{24,28},{28,24},{1,5},{5... | collective-permute-start | bytes 49160 | tf_op jit(solution)/shard_map/ppermute | solution.py:155
  (237 shorter events, 348.4 us)
Async XLA Ops:
  7.2 82.7 %all-gather.5.cloned.1.call-start = ((), (), s32[]{:S(2)}) async-start(), calls=%async_computation.4 | async-start | bytes 7077888 | tf_op jit(solution)/shard_map/all_gather | solution.py:225
  7.9 118.2 %all-gather.7.cloned.1.call-start = ((), (), s32[]{:S(2)}) async-start(), calls=%async_computation.5 | async-start | bytes 2359296 | tf_op jit(solution)/shard_map/all_gather | solution.py:226
  8.7 314.9 %all-gather.9.cloned.1.call-start = ((), (), s32[]{:S(2)}) async-start(), calls=%async_computation.6 | async-start | bytes 12681216 | tf_op jit(solution)/shard_map/all_gather | solution.py:227
  9.4 331.8 %all-gather.11.cloned.1.call-start = ((), (), s32[]{:S(2)}) async-start(), calls=%async_computation.7 | async-start | bytes 6340608 | tf_op jit(solution)/shard_map/all_gather | solution.py:228
  171.0 614.7 %reduce-scatter.11.cloned.1.call-start = ((), (), s32[]{:S(2)}) async-start(), calls=%async_computation.11 | async-start | bytes 6340608 | tf_op jit(solution)/shard_map/reduce_scatter | solution.py:288
  187.1 37.3 %collective-permute-start.22 = (bf16[256,2048]{1,0:T(8,128)(2,1)}, bf16[256,2048]{1,0:T(8,128)(2,1)S(1)}, u32[]{:S(2)}, u32[]{:S(2)}) collective-permute-start(bf16[256,2048]{1,0:T(8,128)(2,1)} %param.15), channel_id=1, source_target_pairs={{0,1},{1,0},{2,3},{3,2},{4,5},{5,4},{6,7},{7,6},{8,9},{9,8},{10,11... | collective-permute-start | bytes 3145736 | tf_op jit(solution)/shard_map/ppermute | solution.py:155
  189.1 41.1 %collective-permute-start.24 = (bf16[256,2048]{1,0:T(8,128)(2,1)}, bf16[256,2048]{1,0:T(8,128)(2,1)S(1)}, u32[]{:S(2)}, u32[]{:S(2)}) collective-permute-start(bf16[256,2048]{1,0:T(8,128)(2,1)} %param.15), channel_id=1, source_target_pairs={{1,2},{2,1},{5,6},{6,5},{9,10},{10,9},{13,14},{14,13},{17,18},{18,... | collective-permute-start | bytes 3145736 | tf_op jit(solution)/shard_map/ppermute | solution.py:155
  227.3 47.5 %collective-permute-start.14 = (bf16[256,2048]{1,0:T(8,128)(2,1)S(1)}, bf16[256,2048]{1,0:T(8,128)(2,1)S(1)}, u32[]{:S(2)}, u32[]{:S(2)}) collective-permute-start(bf16[256,2048]{1,0:T(8,128)(2,1)S(1)} %get-tuple-element.40), channel_id=1, source_target_pairs={{1,2},{2,1},{5,6},{6,5},{9,10},{10,9},{13,14},{14,13},{17,18},{18,... | collective-permute-start | bytes 3145736 | tf_op jit(solution)/shard_map/ppermute | solution.py:155
  230.2 45.9 %collective-permute-start.25 = (bf16[256,2048]{1,0:T(8,128)(2,1)S(1)}, bf16[256,2048]{1,0:T(8,128)(2,1)S(1)}, u32[]{:S(2)}, u32[]{:S(2)}) collective-permute-start(bf16[256,2048]{1,0:T(8,128)(2,1)S(1)} %collective-permute-done.24), channel_id=1, source_target_pairs={{1,0},{2,3},{5,4},{6,7},{9,8},{10,11},{13,12},{14,15},{17,16},{18,... | collective-permute-start | bytes 3145736 | tf_op jit(solution)/shard_map/ppermute | solution.py:155
  235.6 61.4 %collective-permute-start.13 = (bf16[256,2048]{1,0:T(8,128)(2,1)S(1)}, bf16[256,2048]{1,0:T(8,128)(2,1)S(1)}, u32[]{:S(2)}, u32[]{:S(2)}) collective-permute-start(bf16[256,2048]{1,0:T(8,128)(2,1)S(1)} %collective-permute-done.12), channel_id=1, source_target_pairs={{1,2},{2,1},{5,6},{6,5},{9,10},{10,9},{13,14},{14,13},{17,18},{18,... | collective-permute-start | bytes 3145736 | tf_op jit(solution)/shard_map/ppermute | solution.py:155
  252.3 46.2 %collective-permute-start.26 = (bf16[256,2048]{1,0:T(8,128)(2,1)S(1)}, bf16[256,2048]{1,0:T(8,128)(2,1)S(1)}, u32[]{:S(2)}, u32[]{:S(2)}) collective-permute-start(bf16[256,2048]{1,0:T(8,128)(2,1)S(1)} %collective-permute-done.23), channel_id=1, source_target_pairs={{1,0},{2,3},{5,4},{6,7},{9,8},{10,11},{13,12},{14,15},{17,16},{18,... | collective-permute-start | bytes 3145736 | tf_op jit(solution)/shard_map/ppermute | solution.py:155
  384.5 32.1 %collective-permute-start.19 = (bf16[256,2048]{1,0:T(8,128)(2,1)}, bf16[256,2048]{1,0:T(8,128)(2,1)}, u32[]{:S(2)}, u32[]{:S(2)}) collective-permute-start(bf16[256,2048]{1,0:T(8,128)(2,1)} %get-tuple-element.38), channel_id=1, source_target_pairs={{0,1},{3,2},{4,5},{7,6},{8,9},{11,10},{12,13},{15,14},{16,17},{19,... | collective-permute-start | bytes 3145736 | tf_op jit(solution)/shard_map/ppermute | solution.py:155
  400.0 39.1 %collective-permute-start.29 = (bf16[256,2048]{1,0:T(8,128)(2,1)}, bf16[256,2048]{1,0:T(8,128)(2,1)}, u32[]{:S(2)}, u32[]{:S(2)}) collective-permute-start(bf16[256,2048]{1,0:T(8,128)(2,1)} %get-tuple-element.36), channel_id=1, source_target_pairs={{0,1},{3,2},{4,5},{7,6},{8,9},{11,10},{12,13},{15,14},{16,17},{19,... | collective-permute-start | bytes 3145736 | tf_op jit(solution)/shard_map/ppermute | solution.py:155
  411.3 377.6 %reduce-scatter.7.cloned.1.call-start = ((), (), s32[]{:S(2)}) async-start(), calls=%async_computation.9 | async-start | bytes 2359296 | tf_op jit(solution)/shard_map/reduce_scatter | solution.py:288
  418.6 31.5 %collective-permute-start.20 = (bf16[256,2048]{1,0:T(8,128)(2,1)S(1)}, bf16[256,2048]{1,0:T(8,128)(2,1)S(1)}, u32[]{:S(2)}, u32[]{:S(2)}) collective-permute-start(bf16[256,2048]{1,0:T(8,128)(2,1)S(1)} %fusion.54), channel_id=1, source_target_pairs={{1,2},{2,1},{5,6},{6,5},{9,10},{10,9},{13,14},{14,13},{17,18},{18,... | collective-permute-start | bytes 3145736 | tf_op jit(solution)/shard_map/ppermute | solution.py:155
  444.0 30.9 %collective-permute-start.18 = (bf16[256,2048]{1,0:T(8,128)(2,1)S(1)}, bf16[256,2048]{1,0:T(8,128)(2,1)S(1)}, u32[]{:S(2)}, u32[]{:S(2)}) collective-permute-start(bf16[256,2048]{1,0:T(8,128)(2,1)S(1)} %copy-done.23), channel_id=1, source_target_pairs={{1,2},{2,1},{5,6},{6,5},{9,10},{10,9},{13,14},{14,13},{17,18},{18,... | collective-permute-start | bytes 3145736 | tf_op jit(solution)/shard_map/ppermute | solution.py:155
  446.9 50.5 %collective-permute-start.28 = (bf16[256,2048]{1,0:T(8,128)(2,1)S(1)}, bf16[256,2048]{1,0:T(8,128)(2,1)S(1)}, u32[]{:S(2)}, u32[]{:S(2)}) collective-permute-start(bf16[256,2048]{1,0:T(8,128)(2,1)S(1)} %copy-done.24), channel_id=1, source_target_pairs={{1,2},{2,1},{5,6},{6,5},{9,10},{10,9},{13,14},{14,13},{17,18},{18,... | collective-permute-start | bytes 3145736 | tf_op jit(solution)/shard_map/ppermute | solution.py:155
  451.7 45.7 %collective-permute-start.21 = (bf16[256,2048]{1,0:T(8,128)(2,1)S(1)}, bf16[256,2048]{1,0:T(8,128)(2,1)S(1)}, u32[]{:S(2)}, u32[]{:S(2)}) collective-permute-start(bf16[256,2048]{1,0:T(8,128)(2,1)S(1)} %dynamic-slice_add_fusion.2), channel_id=1, source_target_pairs={{0,1},{1,0},{2,3},{3,2},{4,5},{5,4},{6,7},{7,6},{8,9},{9,8},{10,11... | collective-permute-start | bytes 3145736 | tf_op jit(solution)/shard_map/ppermute | solution.py:155
  458.1 39.2 %collective-permute-start.31 = (bf16[256,2048]{1,0:T(8,128)(2,1)S(1)}, bf16[256,2048]{1,0:T(8,128)(2,1)S(1)}, u32[]{:S(2)}, u32[]{:S(2)}) collective-permute-start(bf16[256,2048]{1,0:T(8,128)(2,1)S(1)} %dynamic-slice_add_fusion.1), channel_id=1, source_target_pairs={{0,1},{1,0},{2,3},{3,2},{4,5},{5,4},{6,7},{7,6},{8,9},{9,8},{10,11... | collective-permute-start | bytes 3145736 | tf_op jit(solution)/shard_map/ppermute | solution.py:155
  575.6 221.8 %reduce-scatter.9.cloned.1.call-start = ((), (), s32[]{:S(2)}) async-start(), calls=%async_computation.10 | async-start | bytes 12681216 | tf_op jit(solution)/shard_map/reduce_scatter | solution.py:288
  593.2 207.4 %reduce-scatter.5.cloned.1.call-start = ((), (), s32[]{:S(2)}) async-start(), calls=%async_computation.8 | async-start | bytes 7077888 | tf_op jit(solution)/shard_map/reduce_scatter | solution.py:288
  622.7 30.2 %collective-permute-start.38 = (bf16[1024,512]{1,0:T(8,128)(2,1)S(1)}, bf16[1024,512]{1,0:T(8,128)(2,1)S(1)}, u32[]{:S(2)}, u32[]{:S(2)}) collective-permute-start(bf16[1024,512]{1,0:T(8,128)(2,1)S(1)} %get-tuple-element.20), channel_id=1, source_target_pairs={{4,0},{8,4},{12,8},{20,16},{24,20},{28,24},{5,1},{9,5},{13,9},{21,... | collective-permute-start | bytes 3145736 | tf_op jit(solution)/shard_map/ppermute | solution.py:155
  723.4 67.3 %collective-permute-start.40 = (bf16[256,2048]{1,0:T(8,128)(2,1)}, bf16[256,2048]{1,0:T(8,128)(2,1)}, u32[]{:S(2)}, u32[]{:S(2)}) collective-permute-start(bf16[256,2048]{1,0:T(8,128)(2,1)} %get-tuple-element.30), channel_id=1, source_target_pairs={{1,2},{2,1},{5,6},{6,5},{9,10},{10,9},{13,14},{14,13},{17,18},{18,... | collective-permute-start | bytes 3145736 | tf_op jit(solution)/shard_map/ppermute | solution.py:155
  738.9 51.8 %collective-permute-start.43 = (bf16[256,2048]{1,0:T(8,128)(2,1)}, bf16[256,2048]{1,0:T(8,128)(2,1)}, u32[]{:S(2)}, u32[]{:S(2)}) collective-permute-start(bf16[256,2048]{1,0:T(8,128)(2,1)} %dynamic-slice_add_fusion), channel_id=1, source_target_pairs={{0,1},{1,0},{2,3},{3,2},{4,5},{5,4},{6,7},{7,6},{8,9},{9,8},{10,11... | collective-permute-start | bytes 3145736 | tf_op jit(solution)/shard_map/ppermute | solution.py:155
  (65 other events, 1541.9 us)
Sparse Core Ops, SparseCore 0:
  9.9 46.6 all-gather.4
  58.5 28.1 all-gather.6
  88.6 76.8 all-gather.8
  171.2 103.5 all-gather.10
  411.4 111.5 reduce-scatter.10
  575.7 66.6 reduce-scatter.6
  646.4 86.1 reduce-scatter.8
  736.0 61.8 reduce-scatter.4

commit v2 on v1

v2 whole, which is shorter than its diff:
```python
import functools
import math

import jax
import jax.numpy as jnp
from jax import lax
from jax.experimental import pallas as pl
from jax.experimental.pallas import tpu as pltpu
from jax.sharding import PartitionSpec as P

HEAD_DIM = 128
WINDOW = 1024
SEQ_LEN = 4096
QB = 256
SCALE = 1.0 / math.sqrt(HEAD_DIM)
LOG2E = 1.4426950408889634
EPS = 1e-06
MASKED = -1e30
VMEM_LIMIT = 60 << 20
SMALL = pl.CostEstimate(flops=1 << 20, bytes_accessed=1 << 16, transcendentals=0)
NT = (((1,), (1,)), ((), ()))
TN = (((0,), (0,)), ((), ()))


def nt(a, b):
    return lax.dot_general(a, b, NT, preferred_element_type=jnp.float32)


def nn(a, b):
    return jnp.dot(a, b, preferred_element_type=jnp.float32)


def tn(a, b):
    return lax.dot_general(a, b, TN, preferred_element_type=jnp.float32)


def masked_scores(k_j, q, j, lo):
    s = nt(k_j, q)
    row = lax.broadcasted_iota(jnp.int32, s.shape, 0) + j * QB
    ok = row >= lo
    if (j + 1) * QB > WINDOW:
        hi = lax.broadcasted_iota(jnp.int32, (1, QB), 1) + WINDOW
        ok = ok & (row <= hi)
    return jnp.where(ok, s, MASKED)


def low_bound(doc_ref, b, off):
    q_row = lax.broadcasted_iota(jnp.int32, (1, QB), 1)
    doc = doc_ref[:, b * QB : (b + 1) * QB]
    return jnp.maximum(q_row + 1, doc - off + (WINDOW - b * QB))


def block_at(index):
    return pl.ds(pl.multiple_of(index * QB, QB), QB)


def attend_kernel(place_ref, doc_ref, *refs):
    new, old = refs[:4], refs[4:8]
    o_ref, lse_ref, q_s, k_s, vt_s = refs[8:]
    h = pl.program_id(0)
    off, me = place_ref[0], place_ref[1]
    blocks = len(new)
    for slot in range(blocks):
        at = me ^ slot
        q_s[block_at(at)] = new[slot][0]
        k_s[block_at(at)] = old[slot][0]
        k_s[block_at(at + blocks)] = new[slot][1]
        vt_s[:, block_at(at)] = old[slot][1].T
        vt_s[:, block_at(at + blocks)] = new[slot][2].T
    c = SCALE * LOG2E
    n = WINDOW // QB + 1
    for b in range(blocks):
        q = q_s[b * QB : (b + 1) * QB]
        lo = low_bound(doc_ref, b, off)
        ss = [
            masked_scores(k_s[(b + j) * QB : (b + j + 1) * QB], q, j, lo) for j in range(n)
        ]
        m = functools.reduce(jnp.maximum, [jnp.max(s, axis=0, keepdims=True) for s in ss])
        total = jnp.zeros((1, QB), jnp.float32)
        acc = jnp.zeros((HEAD_DIM, QB), jnp.float32)
        for j in range(n):
            p = jnp.exp2((ss[j] - m) * c)
            total = total + jnp.sum(p, axis=0, keepdims=True)
            acc = acc + nn(vt_s[:, (b + j) * QB : (b + j + 1) * QB], p.astype(jnp.bfloat16))
        o_ref[block_at(me ^ b)] = (acc / total).T.astype(o_ref.dtype)
        lse_ref[pl.ds(h, 1), b * QB : (b + 1) * QB] = m * c + jnp.log2(total)


def back_kernel(first, place_ref, doc_ref, lse_ref, *refs):
    new, old, cot = refs[:4], refs[4:8], refs[8:12]
    dq_ref, dk_ref, dv_ref, prev_ref, q_s, do_s, k_s, v_s, kt_s, dk_s, dv_s = refs[-11:]
    h = pl.program_id(0)
    off, me = place_ref[0], place_ref[1]
    blocks = len(new)
    for slot in range(blocks):
        at = me ^ slot
        q_s[block_at(at)] = new[slot][0]
        do_s[block_at(at)] = cot[slot][...]
        k_s[block_at(at)] = old[slot][0]
        k_s[block_at(at + blocks)] = new[slot][1]
        v_s[block_at(at)] = old[slot][1]
        v_s[block_at(at + blocks)] = new[slot][2]
        kt_s[:, block_at(at)] = old[slot][0].T
        kt_s[:, block_at(at + blocks)] = new[slot][1].T
    c = SCALE * LOG2E
    n = WINDOW // QB + 1
    seen = 0
    for b in range(blocks):
        q = q_s[b * QB : (b + 1) * QB]
        do = do_s[b * QB : (b + 1) * QB]
        lse = lse_ref[pl.ds(h + first, 1), b * QB : (b + 1) * QB]
        lo = low_bound(doc_ref, b, off)
        delta = jnp.zeros((1, QB), jnp.float32)
        ps, dps = [], []
        for j in range(n):
            rows = slice((b + j) * QB, (b + j + 1) * QB)
            p = jnp.exp2(masked_scores(k_s[rows], q, j, lo) * c - lse)
            dp = nt(v_s[rows], do)
            delta = delta + jnp.sum(p * dp, axis=0, keepdims=True)
            dv = nn(p.astype(jnp.bfloat16), do)
            if b + j >= seen:
                dv_s[rows] = dv
            else:
                dv_s[rows] += dv
            ps.append(p)
            dps.append(dp)
        dqt = jnp.zeros((HEAD_DIM, QB), jnp.float32)
        for j in range(n):
            rows = slice((b + j) * QB, (b + j + 1) * QB)
            ds = (ps[j] * (dps[j] - delta)).astype(jnp.bfloat16)
            dk = nn(ds, q)
            if b + j >= seen:
                dk_s[rows] = dk
            else:
                dk_s[rows] += dk
            dqt = dqt + nn(kt_s[:, rows], ds)
        seen = b + n
        dq_ref[block_at(me ^ b)] = (dqt * SCALE).T.astype(dq_ref.dtype)
    for slot in range(blocks):
        at = me ^ slot
        rows = slice(slot * QB, (slot + 1) * QB)
        prev_ref[0, rows] = (dk_s[block_at(at)] * SCALE).astype(prev_ref.dtype)
        prev_ref[1, rows] = dv_s[block_at(at)].astype(prev_ref.dtype)
        dk_ref[rows] = dk_s[block_at(at + blocks)] * SCALE
        dv_ref[rows] = dv_s[block_at(at + blocks)]


def spec2(rows, first=0):
    return pl.BlockSpec((rows, HEAD_DIM), lambda h: (0, h + first))


def spec3(count, rows, first=0):
    return pl.BlockSpec((count, rows, HEAD_DIM), lambda h: (0, 0, h + first))


def constant(shape):
    return pl.BlockSpec(shape, lambda h: (0, 0))


def attend(place, doc, new, old):
    blocks = len(new)
    span, width = blocks * QB, new[0].shape[-1]
    heads = width // HEAD_DIM
    bf = jnp.bfloat16
    return pl.pallas_call(
        attend_kernel,
        grid=(heads,),
        in_specs=[pl.BlockSpec(memory_space=pltpu.SMEM), constant((1, span))]
        + [spec3(3, QB)] * blocks
        + [spec3(2, QB)] * blocks,
        out_specs=[spec2(span), constant((heads, span))],
        out_shape=[
            jax.ShapeDtypeStruct((span, width), bf),
            jax.ShapeDtypeStruct((heads, span), jnp.float32),
        ],
        scratch_shapes=[
            pltpu.VMEM((span, HEAD_DIM), bf),
            pltpu.VMEM((WINDOW + span, HEAD_DIM), bf),
            pltpu.VMEM((HEAD_DIM, WINDOW + span), bf),
        ],
        compiler_params=pltpu.CompilerParams(vmem_limit_bytes=VMEM_LIMIT),
        cost_estimate=SMALL,
    )(place, doc, *new, *old)


def attend_back(place, doc, lse, new, old, cot, first, heads, kept=()):
    blocks = len(new)
    span, width = blocks * QB, new[0].shape[-1]
    bf, f32 = jnp.bfloat16, jnp.float32
    fixed = 3 + 3 * blocks
    return pl.pallas_call(
        functools.partial(back_kernel, first),
        grid=(heads,),
        in_specs=[
            pl.BlockSpec(memory_space=pltpu.SMEM),
            constant((1, span)),
            constant(lse.shape),
        ]
        + [spec3(3, QB, first)] * blocks
        + [spec3(2, QB, first)] * blocks
        + [spec2(QB, first)] * blocks
        + [pl.BlockSpec(memory_space=pl.ANY)] * len(kept),
        out_specs=[spec2(span, first)] * 3 + [spec3(2, WINDOW)],
        out_shape=[
            jax.ShapeDtypeStruct((span, width), bf),
            jax.ShapeDtypeStruct((span, width), f32),
            jax.ShapeDtypeStruct((span, width), f32),
            jax.ShapeDtypeStruct((2, WINDOW, heads * HEAD_DIM), bf),
        ],
        input_output_aliases={fixed + i: i for i in range(len(kept))},
        scratch_shapes=[pltpu.VMEM((span, HEAD_DIM), bf)] * 2
        + [pltpu.VMEM((WINDOW + span, HEAD_DIM), bf)] * 2
        + [pltpu.VMEM((HEAD_DIM, WINDOW + span), bf)]
        + [pltpu.VMEM((WINDOW + span, HEAD_DIM), f32)] * 2,
        compiler_params=pltpu.CompilerParams(vmem_limit_bytes=VMEM_LIMIT),
        cost_estimate=SMALL,
    )(place, doc, lse, *new, *old, *cot, *kept)


PAIRS = [(0, 1), (1, 0), (2, 3), (3, 2)]
MIDDLE = [(1, 2), (2, 1)]
OUTWARD = [(1, 0), (2, 3)]
INWARD = [(0, 1), (3, 2)]


def send(block, route, axis="tp"):
    return lax.ppermute(block, axis, route)


def tie(*values):
    return lax.optimization_barrier(values)


def after(value, *others):
    return lax.optimization_barrier((value,) + others)[0]


def flip(bit, axis="fsdp"):
    return [(i, i ^ bit) for i in range(lax.axis_size(axis))]


def neighbour_route(distance, per_seq):
    size = lax.axis_size("fsdp")
    pairs = [(i - 1, i) for i in range(1, size) if i % per_seq]
    return pairs if distance > 0 else [(b, a) for a, b in pairs]


def pick(array, index, axis):
    return lax.dynamic_index_in_dim(array, index, axis, keepdims=False)


def normalize(values):
    inverse = lax.rsqrt(jnp.mean(values * values, axis=-1, keepdims=True) + EPS)
    return (values * inverse, inverse)


def norm_back(grad, gain, unit, inverse):
    scaled = grad * gain
    return inverse * (scaled - unit * jnp.mean(scaled * unit, axis=-1, keepdims=True))


def add(a, b):
    return (a.astype(jnp.float32) + b.astype(jnp.float32)).astype(jnp.bfloat16)


def grad_kernel(blocks, which_ref, *refs):
    lhs, rhs = refs[:blocks], refs[blocks : 2 * blocks]
    away_ref, kept_ref, lhs_s, rhs_s = refs[2 * blocks :]
    count, e = away_ref.shape[1:3]
    group, groups = pl.program_id(0), pl.num_programs(0) // 2

    @pl.when(group == 0)
    def _():
        for k in range(blocks):
            for s in range(count):
                rhs_s[s * e : (s + 1) * e, k * QB : (k + 1) * QB] = rhs[k][s].T

    for k in range(blocks):
        lhs_s[k * QB : (k + 1) * QB] = lhs[k][...]

    def product(out_ref):
        for s in range(count):
            out_ref[0, s] = nn(rhs_s[s * e : (s + 1) * e], lhs_s[...]).astype(out_ref.dtype)

    pl.when(group < groups)(lambda: product(away_ref))
    pl.when(group >= groups)(lambda: product(kept_ref))


def grad_product(own, lhs, rhs):
    blocks = len(lhs)
    e = rhs[0][0].shape[-1]
    count = rhs[0][0].shape[0] if rhs[0][1] is None else 1
    groups = lhs[0].shape[1] // (2 * QB)

    def lhs_at(j, own):
        parity = jnp.where(j < groups, 1 - own[0], own[0])
        return (0, 2 * lax.rem(j, groups) + parity)

    def rhs_at(fixed):
        if fixed is None:
            return pl.BlockSpec((count, QB, e), lambda j, own: (0, 0, 0))
        return pl.BlockSpec((1, QB, e), lambda j, own: (fixed, 0, 0))

    out = jax.ShapeDtypeStruct((groups, count, e, QB), jnp.bfloat16)
    return pl.pallas_call(
        functools.partial(grad_kernel, blocks),
        grid_spec=pltpu.PrefetchScalarGridSpec(
            num_scalar_prefetch=1,
            grid=(2 * groups,),
            in_specs=[pl.BlockSpec((QB, QB), lhs_at)] * blocks
            + [rhs_at(fixed) for _, fixed in rhs],
            out_specs=[
                pl.BlockSpec(
                    (1, count, e, QB), lambda j, own: (jnp.minimum(j, groups - 1), 0, 0, 0)
                ),
                pl.BlockSpec((1, count, e, QB), lambda j, own: (jnp.maximum(j - groups, 0), 0, 0, 0)),
            ],
            scratch_shapes=[
                pltpu.VMEM((blocks * QB, QB), jnp.bfloat16),
                pltpu.VMEM((count * e, blocks * QB), jnp.bfloat16),
            ],
        ),
        out_shape=[out, out],
        compiler_params=pltpu.CompilerParams(vmem_limit_bytes=VMEM_LIMIT),
        cost_estimate=SMALL,
    )(own.reshape(1).astype(jnp.int32), *lhs, *[r for r, _ in rhs])


def turn_kernel(where_ref, a_ref, ra_ref, b_ref, rb_ref, out_ref):
    f32 = jnp.float32
    top = a_ref[0, 0].astype(f32) + ra_ref[0].astype(f32)
    bottom = b_ref[0, 0].astype(f32) + rb_ref[0].astype(f32)
    out_ref[0] = jnp.concatenate([top, bottom]).T


def turn(one, two, a, ra, b, rb):
    count, half, width = ra.shape
    part = pl.BlockSpec((1, half, width), lambda s, where: (s, 0, 0))
    return pl.pallas_call(
        turn_kernel,
        grid_spec=pltpu.PrefetchScalarGridSpec(
            num_scalar_prefetch=1,
            grid=(count,),
            in_specs=[
                pl.BlockSpec((1, 1, half, width), lambda s, where: (where[1], s, 0, 0)),
                part,
                pl.BlockSpec((1, 1, half, width), lambda s, where: (where[0], s, 0, 0)),
                part,
            ],
            out_specs=pl.BlockSpec((1, width, 2 * half), lambda s, where: (s, 0, 0)),
        ),
        out_shape=jax.ShapeDtypeStruct((count, width, 2 * half), jnp.float32),
        compiler_params=pltpu.CompilerParams(vmem_limit_bytes=VMEM_LIMIT),
        cost_estimate=SMALL,
    )(jnp.stack([one, two]).astype(jnp.int32), a, ra, b, rb)


def rows_kernel(blocks, *refs):
    w_ref, out_ref = refs[blocks], refs[blocks + 1]
    for k in range(blocks):
        out_ref[k * QB : (k + 1) * QB] = nn(refs[k][...], w_ref[...]).astype(out_ref.dtype)


def rows_product(lhs, w):
    blocks, inner, cols = len(lhs), w.shape[0], w.shape[1]
    wide = 512
    return pl.pallas_call(
        functools.partial(rows_kernel, blocks),
        grid=(cols // wide,),
        in_specs=[pl.BlockSpec((QB, inner), lambda n: (0, 0))] * blocks
        + [pl.BlockSpec((inner, wide), lambda n: (0, n))],
        out_specs=pl.BlockSpec((blocks * QB, wide), lambda n: (0, n)),
        out_shape=jax.ShapeDtypeStruct((blocks * QB, cols), jnp.bfloat16),
        compiler_params=pltpu.CompilerParams(vmem_limit_bytes=VMEM_LIMIT),
        cost_estimate=SMALL,
    )(*lhs, w)


class GradSum:
    def __init__(self, lhs, rhs):
        me = lax.axis_index("fsdp")
        self.low, self.one, self.two = me % 2, (me // 2) % 2, me // 4
        self.lhs, self.rhs = lhs, rhs
        self.staged = lax.axis_size("fsdp") == 8
        self.ra = self.rb = jnp.zeros((), jnp.bfloat16)

    def first(self, *others):
        own = self.low if self.staged else jnp.int32(1)
        self.away, self.kept = grad_product(after(own, *others), self.lhs, self.rhs)

    def ready(self):
        return [self.away, self.kept, self.ra, self.rb]

    def set(self, values):
        self.away, self.kept, self.ra, self.rb = values

    def exchange(self, one_step):
        if not self.staged:
            return
        if one_step == 0:
            self.back = send(self.away, flip(1), "fsdp")
        else:
            self.ra = send(self.ra, flip(2 * one_step), "fsdp")
            self.rb = send(self.rb, flip(4 // one_step), "fsdp")

    def part(self, index, axis, top, *more):
        groups, s, e, width = self.kept.shape
        start, size = [0] * 5, [2, 2, s, e // 2, width]
        start[axis], size[axis] = index, 1
        start[3] = 0 if top else e // 2
        total = 0.0
        for array in (self.kept, self.back):
            cut = lax.dynamic_slice(array.reshape(2, 2, s, e, width), start, size)
            total = total + jnp.squeeze(cut, axis).astype(jnp.float32)
        for array in more:
            total = total + array.astype(jnp.float32)
        return total.astype(jnp.bfloat16)

    def second(self, *others):
        if self.staged:
            self.kept, self.back = tie(self.kept, self.back, *others)[:2]
            self.ra = self.part(1 - self.one, 1, True)
            self.rb = self.part(1 - self.two, 0, False)

    def third(self, *others):
        if self.staged:
            ra, rb = tie(self.ra, self.rb, *others)[:2]
            self.a = self.part(self.one, 1, True, ra)
            self.b = self.part(self.two, 0, False, rb)
            self.ra = pick(self.a, 1 - self.two, 0)
            self.rb = pick(self.b, 1 - self.one, 0)

    def last(self, turned, *others):
        f32 = jnp.float32
        if not self.staged:
            both = jnp.stack([self.away, self.kept], axis=1)
            groups, _, s, e, width = both.shape
            both = both.transpose(2, 3, 0, 1, 4).reshape(s, e, 2 * groups * width)
            own = lax.psum_scatter(both, "fsdp", scatter_dimension=2, tiled=True).astype(f32)
            return own.transpose(0, 2, 1) if turned else own
        ra, rb = tie(self.ra, self.rb, *others)[:2]
        if turned:
            return turn(self.one, self.two, self.a, ra, self.b, rb)
        top = pick(self.a, self.two, 0).astype(f32) + ra.astype(f32)
        bottom = pick(self.b, self.one, 0).astype(f32) + rb.astype(f32)
        return jnp.concatenate([top, bottom], axis=1)


def per_device(layer_input, norm_gains, w_qkv, w_out, w_gate_up, w_down, doc_start, out_cotangent):
    bf, f32 = jnp.bfloat16, jnp.float32
    span_len = doc_start.shape[0]
    me = lax.axis_index("tp")
    mid = (me == 1) | (me == 2)
    per_seq = SEQ_LEN // span_len
    place = jnp.stack([lax.axis_index("fsdp") * span_len, me]).astype(jnp.int32)
    doc_row = doc_start.reshape(1, span_len)
    full_qkv = lax.all_gather(w_qkv, "fsdp", axis=1, tiled=True)
    full_out = lax.all_gather(w_out, "fsdp", axis=1, tiled=True)
    forth, back = neighbour_route(1, per_seq), neighbour_route(-1, per_seq)

    input_f32 = layer_input.astype(f32)
    unit_one, inverse_one = normalize(input_f32)
    normed_one = (unit_one * norm_gains[0]).astype(bf)
    x1, xm = tie(send(normed_one, PAIRS), send(normed_one, MIDDLE))
    xf, xo = tie(send(x1, MIDDLE), send(xm, OUTWARD))
    x2 = jnp.where(mid, xf, xo)
    x3 = send(xf, OUTWARD)
    cm = send(after(out_cotangent, xf), MIDDLE)
    full_qkv = after(full_qkv, xf)

    def project(block):
        return jnp.einsum("td,sde->ste", block, full_qkv, preferred_element_type=f32).astype(bf)

    attn_rows = [normed_one, x1, x2]
    new, old = [], []
    for block in attn_rows:
        new.append(project(block))
        old.append(send(new[-1][1:], forth, "fsdp"))
    tied = tie(x3, cm, *old)
    x3, cm, old = tied[0], tied[1], list(tied[2:])
    attn_rows.append(jnp.where(mid, xm, x3))
    new.append(project(attn_rows[3]))
    old.append(send(new[3][1:], forth, "fsdp"))
    old[3], w_gate_up, w_down = tie(old[3], w_gate_up, w_down)
    full_gate_up = lax.all_gather(w_gate_up, "fsdp", axis=1, tiled=True)
    full_down = lax.all_gather(w_down, "fsdp", axis=1, tiled=True)
    c1 = send(after(out_cotangent, new[3]), PAIRS)
    heads_out, lse = attend(place, doc_row, new, old)

    def out_part(k):
        return nn(heads_out[k * QB : (k + 1) * QB], full_out).astype(bf)

    a3 = out_part(3)
    t1 = send(a3, INWARD)
    c1, cm = tie(c1, after(cm, a3))
    cf, co = send(c1, MIDDLE), send(cm, OUTWARD)
    a2, a1, a0 = out_part(2), out_part(1), out_part(0)
    t1, cf, co, a2, a1, a0 = tie(t1, cf, co, a2, a1, a0)
    t2, t3 = send(a2, INWARD), send(add(a2, t1), MIDDLE)
    c3 = send(cf, OUTWARD)
    t2, t3, c3 = tie(t2, t3, c3)
    t4, t5 = send(add(a3, t2), MIDDLE), send(add(a1, t3), PAIRS)
    cot = [out_cotangent, c1, jnp.where(mid, cf, co), jnp.where(mid, cm, c3)]
    t4, t5 = tie(t4, t5)
    residual_mid = input_f32 + (a0.astype(f32) + t4.astype(f32) + t5.astype(f32))
    unit_two, inverse_two = normalize(residual_mid)
    normed_two = (unit_two * norm_gains[1]).astype(bf)

    def up(rows):
        return jnp.einsum("td,sdf->stf", rows, full_gate_up, preferred_element_type=f32)

    def down(gate_up, cot_rows):
        gate_pre, up_pre = gate_up[0], gate_up[1]
        sig = jax.nn.sigmoid(gate_pre)
        act = (gate_pre * sig * up_pre).astype(bf)
        grad_act = nt(cot_rows, full_down)
        grad_up = grad_act * gate_pre * sig
        grad_gate = grad_act * up_pre * sig * (1.0 + gate_pre * (1.0 - sig))
        grads = jnp.stack([grad_gate, grad_up]).astype(bf)
        back_part = jnp.einsum("stf,sdf->td", grads, full_gate_up, preferred_element_type=f32)
        return act, grads, back_part.astype(bf)

    m1, mm = send(normed_two, PAIRS), send(normed_two, MIDDLE)
    u0 = up(normed_two)
    m1, mm, u0 = tie(m1, mm, u0)
    mf, mo = send(m1, MIDDLE), send(mm, OUTWARD)
    u1 = up(m1)
    f0 = down(after(u0, u1), cot[0])
    mf, mo, u1, f0 = tie(mf, mo, u1, f0)
    m2 = jnp.where(mid, mf, mo)
    m3 = send(mf, OUTWARD)
    f1 = down(u1, cot[1])
    f2 = down(up(m2), cot[2])
    m3, f1, f2 = tie(m3, f1, f2)
    m3 = jnp.where(mid, mm, m3)
    f3 = down(up(m3), cot[3])
    g3, g2, g1, g0 = f3[2], f2[2], f1[2], f0[2]

    feed = (f0, f1, f2, f3)

    def join(sums, *values):
        count = len(values)
        tied = tie(*values, *[r for s in sums for r in s.ready()])
        for i, s in enumerate(sums):
            s.set(tied[count + 4 * i : count + 4 * i + 4])
        return tied[:count]

    t1 = send(g3, INWARD)
    mlp_rows = [normed_two, m1, m2, m3]
    up_sum = GradSum(mlp_rows, [(f[1], None) for f in feed])
    up_sum.first(g3)
    (t1,) = join([up_sum], t1)
    t2, t3 = send(after(g2, t1), INWARD), send(add(g2, t1), MIDDLE)
    up_sum.exchange(0)
    down_sum = GradSum(cot, [(f[0][None], None) for f in feed])
    down_sum.first(t1)
    down_part = rows_product([f[0] for f in feed[:3]] + [after(f3[0], t1)], full_down)
    t2, t3, down_part = join([down_sum], t2, t3, down_part)
    t4, t5 = send(add(g3, t2), MIDDLE), send(add(g1, t3), PAIRS)
    down_sum.exchange(0)
    up_sum.second(t2)
    t4, t5 = join([up_sum], t4, t5)
    grad_normed_two = g0.astype(f32) + t4.astype(f32) + t5.astype(f32)
    grad_mid = out_cotangent.astype(f32) + norm_back(
        grad_normed_two, norm_gains[1], unit_two, inverse_two
    )
    grad_branch = grad_mid.astype(bf)

    def heads_back(block):
        return nt(block, full_out).astype(bf)

    d3, d2, d1, d0 = [down_part[k * QB : (k + 1) * QB] for k in (3, 2, 1, 0)]
    b1, bm = send(grad_branch, PAIRS), send(grad_branch, MIDDLE)
    up_sum.exchange(1)
    down_sum.second(grad_branch)
    h0 = heads_back(grad_branch)
    b1, bm, h0 = join([down_sum], b1, bm, h0)
    bfar, bo = send(b1, MIDDLE), send(bm, OUTWARD)
    r1 = send(after(d3, b1), INWARD)
    h1 = heads_back(b1)
    up_sum.third(b1)
    bfar, bo, r1, h1 = join([up_sum], bfar, bo, r1, h1)
    b2 = jnp.where(mid, bfar, bo)
    b3 = send(bfar, OUTWARD)
    r2, r3 = send(after(d2, bfar), INWARD), send(add(d2, r1), MIDDLE)
    up_sum.exchange(2)
    down_sum.exchange(1)
    h2 = heads_back(b2)
    b3, r2, r3, h2 = tie(b3, r2, r3, h2)
    b3 = jnp.where(mid, bm, b3)
    h3 = heads_back(b3)
    r4, r5 = send(add(d3, r2), MIDDLE), send(add(d1, r3), PAIRS)
    cots = [h0, h1, h2, h3]
    half = heads_out.shape[1] // HEAD_DIM // 2
    *kept, prev_a = attend_back(place, doc_row, lse, new, old, cots, 0, half)
    n_a = send(prev_a, back, "fsdp")
    down_sum.third(prev_a)
    down_sum.exchange(2)
    *kept, prev_b = attend_back(place, doc_row, lse, new, old, cots, half, half, kept)
    n_b = send(prev_b, back, "fsdp")
    grad_q, own_k, own_v = kept
    head_blocks = heads_out.reshape(4, QB, -1)
    out_sum = GradSum([grad_branch, b1, b2, b3], [(head_blocks, k) for k in range(4)])
    out_sum.first(prev_b)
    up_own = up_sum.last(True, prev_b)
    n_a, n_b, r4, r5, up_own = join([out_sum], n_a, n_b, r4, r5, up_own)

    def piece(k):
        rows = slice(k * QB, (k + 1) * QB)
        arrived = jnp.concatenate([n_a[:, rows], n_b[:, rows]], axis=2)
        return jnp.stack([grad_q[rows], add(own_k[rows], arrived[0]), add(own_v[rows], arrived[1])])

    def first_back(grad):
        return jnp.einsum("ste,sde->td", grad, full_qkv, preferred_element_type=f32).astype(bf)

    q3 = piece(3)
    p3 = first_back(q3)
    t1 = send(p3, INWARD)
    out_sum.exchange(0)
    q2, q1, q0 = after(piece(2), p3), after(piece(1), p3), after(piece(0), p3)
    p2, p1, p0 = first_back(q2), first_back(q1), first_back(q0)
    qkv_sum = GradSum(attn_rows, [(q, None) for q in (q0, q1, q2, q3)])
    qkv_sum.first(p3)
    t1, p2, p1, p0 = join([qkv_sum], t1, p2, p1, p0)
    t2, t3 = send(p2, INWARD), send(add(p2, t1), MIDDLE)
    qkv_sum.exchange(0)
    gain_one = functools.reduce(
        jnp.add,
        [
            jnp.sum(p.astype(f32) * r.astype(f32), axis=0)
            for p, r in zip((p0, p1, p2, p3), attn_rows)
        ],
    )
    gain_two = jnp.sum(grad_normed_two * unit_two, axis=0)
    gains = jnp.stack([gain_one / norm_gains[0], gain_two])
    step = 1
    while step < lax.axis_size("fsdp"):
        gains = gains + send(gains, flip(step), "fsdp")
        step *= 2
    qkv_sum.second(t1)
    out_sum.second(t1)
    t2, t3, gains = join([qkv_sum, out_sum], t2, t3, gains)
    s1 = send(gains, INWARD)
    t4, t5 = send(add(p3, t2), MIDDLE), send(add(p1, t3), PAIRS)
    qkv_sum.exchange(1)
    out_sum.exchange(1)
    layer_output = (
        residual_mid + (d0.astype(f32) + r4.astype(f32) + after(r5, t2).astype(f32))
    ).astype(bf)
    down_own = down_sum.last(False, t2)
    gains = gains + s1
    s2 = send(gains, MIDDLE)
    qkv_sum.third(down_own)
    qkv_sum.exchange(2)
    out_sum.third(down_own)
    out_sum.exchange(2)
    gains = gains + s2
    s3 = send(gains, OUTWARD)
    grad_normed_one = p0.astype(f32) + t4.astype(f32) + t5.astype(f32)
    input_grad = (
        grad_mid + norm_back(grad_normed_one, norm_gains[0], unit_one, inverse_one)
    ).astype(bf)
    out_own = out_sum.last(False)
    qkv_own = qkv_sum.last(True)
    gains = jnp.where(mid, gains, s3)
    return (layer_output, input_grad, gains, qkv_own, out_own[0], up_own, down_own[0])


def solution(mesh):
    in_specs = (
        P(("fsdp", "tp"), None),
        P(),
        P(None, "fsdp", "tp"),
        P("tp", "fsdp"),
        P(None, "fsdp", "tp"),
        P("tp", "fsdp"),
        P("fsdp"),
        P(("fsdp", "tp"), None),
    )
    out_specs = (
        P(("fsdp", "tp"), None),
        P(("fsdp", "tp"), None),
        P(),
        P(None, "fsdp", "tp"),
        P("tp", "fsdp"),
        P(None, "fsdp", "tp"),
        P("tp", "fsdp"),
    )
    return jax.shard_map(
        per_device, mesh=mesh, in_specs=in_specs, out_specs=out_specs, check_vma=False
    )
```

time: 818 us -> 725 us (0.89)
  waiting for transfers between devices: 438 us -> 221 us
  Pallas kernels: 35.6 us -> 115 us
  other arithmetic: 53.7 us -> 92.7 us
  starting transfers between devices: 112 us -> 149 us
  matrix products: 132 us -> 102 us
    ppermute x49 -> x72, waiting for transfers between devices: 436 us -> 220 us  [send(): return lax.ppermute(block, axis, route)]
    pallas_call x1 -> x9, Pallas kernels: 22.6 us -> 101 us  [the longest x4 55.9 us: grad_product(): pl.pallas_call(functools.partial(grad_kernel, blocks), grid_spec=pltpu.Pr...]
    convert_element_type x3 -> x29, other arithmetic: 7.42 us -> 53.2 us  [the longest x14 28.1 us: part(): return total.astype(jnp.bfloat16)]
    ppermute x49 -> x72, starting transfers between devices: 111 us -> 149 us  [send(): return lax.ppermute(block, axis, route)]
    dot_general x5 -> x4, matrix products: 27.1 us -> 4.99 us  [nn(): return jnp.dot(a, b, preferred_element_type=jnp.float32)]
    add x17 -> x10, other arithmetic: 18 us -> 1.32 us  [the longest x2 1.11 us: last(): top = pick(self.a, self.two, 0).astype(f32) + ra.astype(f32)]
    dynamic_update_slice x11 -> x0, other arithmetic: 13.4 us -> none  [gather_rows(): lax.dynamic_update_slice_in_dim(whole_rows, part, (me ^ k) * rows, 0)]
    select_n x0 -> x9, other arithmetic: none -> 13.4 us  [the longest x2 3.56 us: per_device(): cot = [out_cotangent, c1, jnp.where(mid, cf, co), jnp.where(mid, cm, c3)]]
  transfers between devices with their start and end apart: 57 -> 76, of which waited for: 34 -> 32; matrix products, arithmetic and copies ran while one was open for 22% -> 27% of each run, Pallas kernels for 4% -> 15%
where the time goes in v2:
time: 725 us; the launch traced here: 714 us
  waiting for transfers between devices  221 us (30%)
  starting transfers between devices  149 us (21%)
  Pallas kernels  115 us (16%)
  matrix products  102 us (14%)
  other arithmetic  92.7 us (13%)
  local copies, waits for them, and re-layouts  18.2 us (3%)
  between operations  15.8 us (2%)
    ppermute x72, waiting for transfers between devices, send(): return lax.ppermute(block, axis, route)  220 us
    ppermute x72, starting transfers between devices, send(): return lax.ppermute(block, axis, route)  149 us
    pallas_call x4, Pallas kernels, grad_product(): pl.pallas_call(functools.partial(grad_kernel, blocks), grid_spec=pltpu.Pr...  55.9 us
    convert_element_type x14, other arithmetic, part(): return total.astype(jnp.bfloat16)  28.1 us
    pallas_call x2, Pallas kernels, attend_back(): pl.pallas_call(functools.partial(back_kernel, first), grid=(heads,), in_s...  26.4 us
    dot_general x8, matrix products, nt(): return lax.dot_general(a, b, NT, preferred_element_type=jnp.float32)  26 us
    dot_general x4, matrix products, up(): jnp.einsum('td,sdf->stf', rows, full_gate_up, preferred_element_type=f32)  21.6 us
    dot_general x4, matrix products, down(): jnp.einsum('stf,sdf->td', grads, full_gate_up, preferred_element_type=f32)  20.9 us
  transfers between devices with their start and end apart: 76, of which 32 were waited for; matrix products, arithmetic and copies ran while one was open for 27% of the time, Pallas kernels for 15%

profile of v2, /device:TPU:8, one launch (start us, length us, event | category | flops | bytes accessed | tf_op | source)
XLA Modules:
  0.0 714.3 jit_solution(6899434717956467676)
XLA Ops:
  14.5 23.3 %collective-permute-done.1 = bf16[256,2048]{1,0:T(8,128)(2,1)} collective-permute-done((bf16[256,2048]{1,0:T(8,128)(2,1)S(1)}, bf16[256,2048]{1,0:T(8,128)(2,1)}, u32[]{:S(2)}, u32[]{:S(2)}) %collective-permute-start.1) | collective-permute-done | bytes 1048608 | tf_op jit(solution)/shard_map/ppermute | solution.py:227
  45.5 17.6 %collective-permute-done.3 = bf16[256,2048]{1,0:T(8,128)(2,1)} collective-permute-done((bf16[256,2048]{1,0:T(8,128)(2,1)}, bf16[256,2048]{1,0:T(8,128)(2,1)}, u32[]{:S(2)}, u32[]{:S(2)}) %collective-permute-start.3) | collective-permute-done | bytes 1048608 | tf_op jit(solution)/shard_map/ppermute | solution.py:227
  99.4 7.7 %collective-permute-start.9 = (bf16[2,256,512]{2,1,0:T(8,128)(2,1)S(1)}, bf16[2,256,512]{2,1,0:T(8,128)(2,1)S(1)}, u32[]{:S(2)}, u32[]{:S(2)}) collective-permute-start(bf16[2,256,512]{2,1,0:T(8,128)(2,1)S(1)} %slice.206), channel_id=1, source_target_pairs={{0,4},{4,8},{8,12},{16,20},{20,24},{24,28},{1,5},{5,9},{9,13},{17,... | collective-permute-start | bytes 1572872 | tf_op jit(solution)/shard_map/ppermute | solution.py:227
  109.9 13.7 %shard_map.135 = (bf16[1024,512]{1,0:T(8,128)(2,1)}, f32[4,1024]{1,0:T(4,128)}) custom-call(s32[2]{0:T(128)} %pad_add_fusion.place_ref, s32[1,1024]{1,0:T(1,128)} %bitcast.527, bf16[3,256,512]{2,1,0:T(8,128)(2,1)} %copy-done.8, bf16[3,256,512]{2,1,0:T(8,128)(2,1)} %copy-done.9, bf16[3,256,512]{2,1,0:T(8,128)(2,1)} %copy-done.10, ...), custom_call_target="tpu_custom_call" | custom-call | flops 1048576 | bytes 65536 | tf_op jit(solution)/shard_map/pallas_call | solution.py:165
  137.8 16.8 %collective-permute-done.10 = bf16[256,2048]{1,0:T(8,128)(2,1)S(1)} collective-permute-done((bf16[256,2048]{1,0:T(8,128)(2,1)S(1)}, bf16[256,2048]{1,0:T(8,128)(2,1)S(1)}, u32[]{:S(2)}, u32[]{:S(2)}) %collective-permute-start.10) | collective-permute-done | bytes 1048608 | tf_op jit(solution)/shard_map/ppermute | solution.py:227
  161.6 17.1 %collective-permute-done.15 = bf16[256,2048]{1,0:T(8,128)(2,1)S(1)} collective-permute-done((bf16[256,2048]{1,0:T(8,128)(2,1)S(1)}, bf16[256,2048]{1,0:T(8,128)(2,1)S(1)}, u32[]{:S(2)}, u32[]{:S(2)}) %collective-permute-start.15) | collective-permute-done | bytes 1048608 | tf_op jit(solution)/shard_map/ppermute | solution.py:227
  187.2 16.1 %collective-permute-done.18 = bf16[256,2048]{1,0:T(8,128)(2,1)S(1)} collective-permute-done((bf16[256,2048]{1,0:T(8,128)(2,1)S(1)}, bf16[256,2048]{1,0:T(8,128)(2,1)S(1)}, u32[]{:S(2)}, u32[]{:S(2)}) %collective-permute-start.18) | collective-permute-done | bytes 1048608 | tf_op jit(solution)/shard_map/ppermute | solution.py:227
  212.8 9.2 %convolution_bitcast_fusion.3 = f32[2,256,1376]{2,1,0:T(8,128)} fusion(bf16[2,2048,1376]{1,2,0:T(8,128)(2,1)} %all-gather.9.cloned.1.call-done, bf16[256,2048]{1,0:T(8,128)(2,1)S(1)} %multiply_convert_fusion.refs_0_), kind=kOutput, calls=%fused_computation.3 | convolution fusion | flops 2885681152 | bytes 15138816 | tf_op jit(solution)/shard_map/td,sdf->stf/dot_general | solution.py:510
  222.0 9.8 %collective-permute-done.20 = bf16[256,2048]{1,0:T(8,128)(2,1)} collective-permute-done((bf16[256,2048]{1,0:T(8,128)(2,1)S(1)}, bf16[256,2048]{1,0:T(8,128)(2,1)}, u32[]{:S(2)}, u32[]{:S(2)}) %collective-permute-start.20) | collective-permute-done | bytes 1048608 | tf_op jit(solution)/shard_map/ppermute | solution.py:227
  253.2 7.9 %fusion.5 = bf16[256,2048]{1,0:T(8,128)(2,1)S(1)} fusion(bf16[2,2048,1376]{1,2,0:T(8,128)(2,1)} %all-gather.9.cloned.1.call-done, bf16[1,256,1376]{2,1,0:T(8,128)(2,1)S(1)} %get-tuple-element.340, bf16[1,256,1376]{2,1,0:T(8,128)(2,1)S(1)} %get-tuple-element.339), kind=kOutput, calls=%fused_computation.33 | convolution fusion | flops 2886909952 | bytes 13729792 | tf_op jit(solution)/shard_map/stf,sdf->td/dot_general | solution.py:520
  304.4 20.3 %shard_map.136 = (bf16[4,2,1376,256]{3,2,1,0:T(8,128)(2,1)}, bf16[4,2,1376,256]{3,2,1,0:T(8,128)(2,1)}) custom-call(s32[1]{0:T(128)} %bitcast.42.which_ref, bf16[256,2048]{1,0:T(8,128)(2,1)} %copy-done.29, bf16[256,2048]{1,0:T(8,128)(2,1)} %collective-permute-done.19.refs_1_, bf16[256,2048]{1,0:T(8,128)(2,1)} %copy-done.34, bf16[256,2048]{1,0:T(8,128)(2,1)} %copy-done.35, ...), custom_call_target="tpu_custom_call" | custom-call | flops 1048576 | bytes 65536 | tf_op jit(solution)/shard_map/pallas_call | solution.py:305
  336.7 12.9 %shard_map.138 = (bf16[4,1,1376,256]{3,2,1,0:T(8,128)(2,1)}, bf16[4,1,1376,256]{3,2,1,0:T(8,128)(2,1)}) custom-call(s32[1]{0:T(128)} %bitcast.43.which_ref, bf16[256,2048]{1,0:T(8,128)(2,1)} %refs_0_.1, bf16[256,2048]{1,0:T(8,128)(2,1)} %collective-permute-done.11.refs_1_, bf16[256,2048]{1,0:T(8,128)(2,1)} %broadcast_select_fusion.4.refs_2_, ...), custom_call_target="tpu_custom_call" | custom-call | flops 1048576 | bytes 65536 | tf_op jit(solution)/shard_map/pallas_call | solution.py:305
  349.6 10.5 %shard_map.137 = bf16[1024,2048]{1,0:T(8,128)(2,1)} custom-call(bf16[256,1376]{1,0:T(8,128)(2,1)} %get-tuple-element.205.refs_0_, bf16[256,1376]{1,0:T(8,128)(2,1)} %get-tuple-element.206.refs_1_, bf16[256,1376]{1,0:T(8,128)(2,1)} %get-tuple-element.207.refs_2_, bf16[256,1376]{1,0:T(8,128)(2,1)} %get-tuple-element.208.refs_3_, ...), custom_call_target="tpu_custom_call" | custom-call | flops 1048576 | bytes 65536 | tf_op jit(solution)/shard_map/pallas_call | solution.py:367
  378.9 13.5 %collective-permute-done.28 = bf16[256,2048]{1,0:T(8,128)(2,1)} collective-permute-done((bf16[256,2048]{1,0:T(8,128)(2,1)}, bf16[256,2048]{1,0:T(8,128)(2,1)}, u32[]{:S(2)}, u32[]{:S(2)}) %collective-permute-start.28) | collective-permute-done | bytes 1048608 | tf_op jit(solution)/shard_map/ppermute | solution.py:227
  415.9 12.4 %collective-permute-done.31 = bf16[256,2048]{1,0:T(8,128)(2,1)} collective-permute-done((bf16[256,2048]{1,0:T(8,128)(2,1)S(1)}, bf16[256,2048]{1,0:T(8,128)(2,1)}, u32[]{:S(2)}, u32[]{:S(2)}) %collective-permute-start.31) | collective-permute-done | bytes 1048608 | tf_op jit(solution)/shard_map/ppermute | solution.py:227
  475.5 7.9 %collective-permute-done.39 = bf16[256,2048]{1,0:T(8,128)(2,1)S(1)} collective-permute-done((bf16[256,2048]{1,0:T(8,128)(2,1)S(1)}, bf16[256,2048]{1,0:T(8,128)(2,1)S(1)}, u32[]{:S(2)}, u32[]{:S(2)}) %collective-permute-start.39) | collective-permute-done | bytes 1048608 | tf_op jit(solution)/shard_map/ppermute | solution.py:227
  494.9 13.4 %shard_map.139 = (bf16[1024,512]{1,0:T(8,128)(2,1)}, f32[1024,512]{1,0:T(8,128)}, f32[1024,512]{1,0:T(8,128)}, bf16[2,1024,256]{2,1,0:T(8,128)(2,1)}) custom-call(s32[2]{0:T(128)} %pad_add_fusion.place_ref, s32[1,1024]{1,0:T(1,128)} %bitcast.528, f32[4,1024]{1,0:T(4,128)} %get-tuple-element.213.lse_ref, bf16[3,256,512]{2,1,0:T(8,128)(2,1)} %copy-done.8, ...), custom_call_target="tpu_custom_call" | custom-call | flops 1048576 | bytes 65536 | tf_op jit(solution)/shard_map/pallas_call | solution.py:191
  508.3 12.9 %shard_map.140 = (bf16[1024,512]{1,0:T(8,128)(2,1)}, f32[1024,512]{1,0:T(8,128)}, f32[1024,512]{1,0:T(8,128)}, bf16[2,1024,256]{2,1,0:T(8,128)(2,1)}) custom-call(s32[2]{0:T(128)} %pad_add_fusion.place_ref, s32[1,1024]{1,0:T(1,128)} %bitcast.529, ...), custom_call_target="tpu_custom_call", output_to_operand_aliasing={{0}: (15, {}), {1}: (16, {}), {2}: (17, {})} | custom-call | flops 1048576 | bytes 65536 | tf_op jit(solution)/shard_map/pallas_call | solution.py:191
  532.1 8.8 %shard_map.142 = (bf16[4,1,512,256]{3,2,1,0:T(8,128)(2,1)}, bf16[4,1,512,256]{3,2,1,0:T(8,128)(2,1)}) custom-call(s32[1]{0:T(128)} %bitcast.64.which_ref, bf16[256,2048]{1,0:T(8,128)(2,1)} %copy-done.26, bf16[256,2048]{1,0:T(8,128)(2,1)} %collective-permute-done.30.refs_1_, bf16[256,2048]{1,0:T(8,128)(2,1)} %copy-done.30, bf16[256,2048]{1,0:T(8,128)(2,1)} %copy-done.33, ...), custom_call_target="tpu_custom_call" | custom-call | flops 1048576 | bytes 65536 | tf_op jit(solution)/shard_map/pallas_call | solution.py:305
  563.1 13.9 %shard_map.143 = (bf16[4,3,512,256]{3,2,1,0:T(8,128)(2,1)}, bf16[4,3,512,256]{3,2,1,0:T(8,128)(2,1)}) custom-call(s32[1]{0:T(128)} %bitcast.90.which_ref, bf16[256,2048]{1,0:T(8,128)(2,1)} %copy-done.42, bf16[256,2048]{1,0:T(8,128)(2,1)} %copy-done.36, bf16[256,2048]{1,0:T(8,128)(2,1)} %broadcast_select_fusion.7.refs_2_, bf16[256,2048]{1,0:T(8,128)(2,1)} %copy-done.39, ...), custom_call_target="tpu_custom_call" | custom-call | flops 1048576 | bytes 65536 | tf_op jit(solution)/shard_map/pallas_call | solution.py:305
  586.7 7.5 %collective-permute-start.53 = (bf16[4,3,512,256]{3,2,1,0:T(8,128)(2,1)}, bf16[4,3,512,256]{3,2,1,0:T(8,128)(2,1)}, u32[]{:S(2)}, u32[]{:S(2)}) collective-permute-start(bf16[4,3,512,256]{3,2,1,0:T(8,128)(2,1)} %get-tuple-element.275), channel_id=1, source_target_pairs={{0,4},{4,0},{8,12},{12,8},{16,20},{20,16},{24,28},{28,24},{1,5},{5... | collective-permute-start | bytes 9437192 | tf_op jit(solution)/shard_map/ppermute | solution.py:227
  620.8 13.2 %collective-permute-done.49 = bf16[256,2048]{1,0:T(8,128)(2,1)S(1)} collective-permute-done((bf16[256,2048]{1,0:T(8,128)(2,1)}, bf16[256,2048]{1,0:T(8,128)(2,1)S(1)}, u32[]{:S(2)}, u32[]{:S(2)}) %collective-permute-start.49) | collective-permute-done | bytes 1048608 | tf_op jit(solution)/shard_map/ppermute | solution.py:227
  658.7 14.3 %collective-permute-done.59 = f32[2,2048]{1,0:T(2,128)S(1)} collective-permute-done((f32[2,2048]{1,0:T(2,128)S(1)}, f32[2,2048]{1,0:T(2,128)S(1)}, u32[]{:S(2)}, u32[]{:S(2)}) %collective-permute-start.59) | collective-permute-done | bytes 16416 | tf_op jit(solution)/shard_map/ppermute | solution.py:227
  683.0 15.8 %collective-permute-done.55 = bf16[256,2048]{1,0:T(8,128)(2,1)S(1)} collective-permute-done((bf16[256,2048]{1,0:T(8,128)(2,1)S(1)}, bf16[256,2048]{1,0:T(8,128)(2,1)S(1)}, u32[]{:S(2)}, u32[]{:S(2)}) %collective-permute-start.55) | collective-permute-done | bytes 1048608 | tf_op jit(solution)/shard_map/ppermute | solution.py:227
  (422 shorter events, 382.2 us)
Async XLA Ops:
  7.2 68.6 %all-gather.5.cloned.1.call-start = ((), (), s32[]{:S(2)}) async-start(), calls=%async_computation | async-start | bytes 7077888 | tf_op jit(solution)/shard_map/all_gather | solution.py:457
  7.9 115.7 %all-gather.7.cloned.1.call-start = ((), (), s32[]{:S(2)}) async-start(), calls=%async_computation.1 | async-start | bytes 2359296 | tf_op jit(solution)/shard_map/all_gather | solution.py:458
  45.4 167.4 %all-gather.9.cloned.1.call-start = ((), (), s32[]{:S(2)}) async-start(), calls=%async_computation.2 | async-start | bytes 12681216 | tf_op jit(solution)/shard_map/all_gather | solution.py:485
  108.6 136.6 %all-gather.11.cloned.1.call-start = ((), (), s32[]{:S(2)}) async-start(), calls=%async_computation.3 | async-start | bytes 6340608 | tf_op jit(solution)/shard_map/all_gather | solution.py:486
  126.5 28.0 %collective-permute-start.10 = (bf16[256,2048]{1,0:T(8,128)(2,1)S(1)}, bf16[256,2048]{1,0:T(8,128)(2,1)S(1)}, u32[]{:S(2)}, u32[]{:S(2)}) collective-permute-start(bf16[256,2048]{1,0:T(8,128)(2,1)S(1)} %convolution_convert_fusion.3), channel_id=1, source_target_pairs={{0,1},{3,2},{4,5},{7,6},{8,9},{11,10},{12,13},{15,14},{16,17},{19,... | collective-permute-start | bytes 3145736 | tf_op jit(solution)/shard_map/ppermute | solution.py:227
  233.1 28.1 %collective-permute-start.22 = (bf16[256,2048]{1,0:T(8,128)(2,1)}, bf16[256,2048]{1,0:T(8,128)(2,1)}, u32[]{:S(2)}, u32[]{:S(2)}) collective-permute-start(bf16[256,2048]{1,0:T(8,128)(2,1)} %collective-permute-done.20), channel_id=1, source_target_pairs={{1,0},{2,3},{5,4},{6,7},{9,8},{10,11},{13,12},{14,15},{17,16},{18,... | collective-permute-start | bytes 3145736 | tf_op jit(solution)/shard_map/ppermute | solution.py:227
  326.5 46.0 %collective-permute-start.29 = (bf16[4,2,1376,256]{3,2,1,0:T(8,128)(2,1)}, bf16[4,2,1376,256]{3,2,1,0:T(8,128)(2,1)}, u32[]{:S(2)}, u32[]{:S(2)}) collective-permute-start(bf16[4,2,1376,256]{3,2,1,0:T(8,128)(2,1)} %get-tuple-element.218), channel_id=1, source_target_pairs={{0,4},{4,0},{8,12},{12,8},{16,20},{20,16},{24,28},{28,24},{1,5},{5... | collective-permute-start | bytes 16908296 | tf_op jit(solution)/shard_map/ppermute | solution.py:227
  331.1 29.1 %collective-permute-start.26 = (bf16[256,2048]{1,0:T(8,128)(2,1)}, bf16[256,2048]{1,0:T(8,128)(2,1)}, u32[]{:S(2)}, u32[]{:S(2)}) collective-permute-start(bf16[256,2048]{1,0:T(8,128)(2,1)} %add_convert_fusion.8), channel_id=1, source_target_pairs={{1,2},{2,1},{5,6},{6,5},{9,10},{10,9},{13,14},{14,13},{17,18},{18,... | collective-permute-start | bytes 3145736 | tf_op jit(solution)/shard_map/ppermute | solution.py:227
  372.3 37.6 %collective-permute-start.32 = (bf16[4,1,1376,256]{3,2,1,0:T(8,128)(2,1)}, bf16[4,1,1376,256]{3,2,1,0:T(8,128)(2,1)}, u32[]{:S(2)}, u32[]{:S(2)}) collective-permute-start(bf16[4,1,1376,256]{3,2,1,0:T(8,128)(2,1)} %get-tuple-element.224), channel_id=1, source_target_pairs={{0,4},{4,0},{8,12},{12,8},{16,20},{20,16},{24,28},{28,24},{1,5},{5... | collective-permute-start | bytes 8454152 | tf_op jit(solution)/shard_map/ppermute | solution.py:227
  405.9 37.2 %collective-permute-start.36 = (bf16[2,2,688,256]{3,2,1,0:T(8,128)(2,1)}, bf16[2,2,688,256]{3,2,1,0:T(8,128)(2,1)S(1)}, u32[]{:S(2)}, u32[]{:S(2)}) collective-permute-start(bf16[2,2,688,256]{3,2,1,0:T(8,128)(2,1)} %fusion.62), channel_id=1, source_target_pairs={{0,8},{4,12},{8,0},{12,4},{16,24},{20,28},{24,16},{28,20},{1,9},{5... | collective-permute-start | bytes 4227080 | tf_op jit(solution)/shard_map/ppermute | solution.py:227
  407.1 36.1 %collective-permute-start.37 = (bf16[2,2,688,256]{3,2,1,0:T(8,128)(2,1)}, bf16[2,2,688,256]{3,2,1,0:T(8,128)(2,1)}, u32[]{:S(2)}, u32[]{:S(2)}) collective-permute-start(bf16[2,2,688,256]{3,2,1,0:T(8,128)(2,1)} %fusion.63), channel_id=1, source_target_pairs={{0,16},{4,20},{8,24},{12,28},{16,0},{20,4},{24,8},{28,12},{1,17},{... | collective-permute-start | bytes 4227080 | tf_op jit(solution)/shard_map/ppermute | solution.py:227
  469.3 52.0 %collective-permute-start.62 = (bf16[2,1,688,256]{3,2,1,0:T(8,128)(2,1)}, bf16[2,1,688,256]{3,2,1,0:T(8,128)(2,1)}, u32[]{:S(2)}, u32[]{:S(2)}) collective-permute-start(bf16[2,1,688,256]{3,2,1,0:T(8,128)(2,1)} %fusion.88), channel_id=1, source_target_pairs={{0,8},{4,12},{8,0},{12,4},{16,24},{20,28},{24,16},{28,20},{1,9},{5... | collective-permute-start | bytes 2113544 | tf_op jit(solution)/shard_map/ppermute | solution.py:227
  471.7 55.5 %collective-permute-start.63 = (bf16[2,1,688,256]{3,2,1,0:T(8,128)(2,1)}, bf16[2,1,688,256]{3,2,1,0:T(8,128)(2,1)}, u32[]{:S(2)}, u32[]{:S(2)}) collective-permute-start(bf16[2,1,688,256]{3,2,1,0:T(8,128)(2,1)} %fusion.89), channel_id=1, source_target_pairs={{0,16},{4,20},{8,24},{12,28},{16,0},{20,4},{24,8},{28,12},{1,17},{... | collective-permute-start | bytes 2113544 | tf_op jit(solution)/shard_map/ppermute | solution.py:227
  483.4 40.6 %collective-permute-start.45 = (bf16[2,688,256]{2,1,0:T(8,128)(2,1)}, bf16[2,688,256]{2,1,0:T(8,128)(2,1)S(1)}, u32[]{:S(2)}, u32[]{:S(2)}) collective-permute-start(bf16[2,688,256]{2,1,0:T(8,128)(2,1)} %dynamic-slice_bitcast_fusion.1), channel_id=1, source_target_pairs={{0,16},{4,20},{8,24},{12,28},{16,0},{20,4},{24,8},{28,12},{1,17},{... | collective-permute-start | bytes 2113544 | tf_op jit(solution)/shard_map/ppermute | solution.py:227
  486.5 38.8 %collective-permute-start.46 = (bf16[2,688,256]{2,1,0:T(8,128)(2,1)}, bf16[2,688,256]{2,1,0:T(8,128)(2,1)}, u32[]{:S(2)}, u32[]{:S(2)}) collective-permute-start(bf16[2,688,256]{2,1,0:T(8,128)(2,1)} %dynamic-slice_bitcast_fusion), channel_id=1, source_target_pairs={{0,8},{4,12},{8,0},{12,4},{16,24},{20,28},{24,16},{28,20},{1,9},{5... | collective-permute-start | bytes 2113544 | tf_op jit(solution)/shard_map/ppermute | solution.py:227
  491.7 53.5 %collective-permute-start.44 = (bf16[256,2048]{1,0:T(8,128)(2,1)}, bf16[256,2048]{1,0:T(8,128)(2,1)}, u32[]{:S(2)}, u32[]{:S(2)}) collective-permute-start(bf16[256,2048]{1,0:T(8,128)(2,1)} %get-tuple-element.341), channel_id=1, source_target_pairs={{0,1},{1,0},{2,3},{3,2},{4,5},{5,4},{6,7},{7,6},{8,9},{9,8},{10,11... | collective-permute-start | bytes 3145736 | tf_op jit(solution)/shard_map/ppermute | solution.py:227
  530.6 105.5 %collective-permute-start.64 = (bf16[1,688,256]{2,1,0:T(8,128)(2,1)}, bf16[1,688,256]{2,1,0:T(8,128)(2,1)}, u32[]{:S(2)}, u32[]{:S(2)}) collective-permute-start(bf16[1,688,256]{2,1,0:T(8,128)(2,1)} %dynamic-slice_bitcast_fusion.5), channel_id=1, source_target_pairs={{0,16},{4,20},{8,24},{12,28},{16,0},{20,4},{24,8},{28,12},{1,17},{... | collective-permute-start | bytes 1056776 | tf_op jit(solution)/shard_map/ppermute | solution.py:227
  556.9 29.8 %collective-permute-start.47 = (bf16[256,2048]{1,0:T(8,128)(2,1)}, bf16[256,2048]{1,0:T(8,128)(2,1)}, u32[]{:S(2)}, u32[]{:S(2)}) collective-permute-start(bf16[256,2048]{1,0:T(8,128)(2,1)} %get-tuple-element.374), channel_id=1, source_target_pairs={{0,1},{3,2},{4,5},{7,6},{8,9},{11,10},{12,13},{15,14},{16,17},{19,... | collective-permute-start | bytes 3145736 | tf_op jit(solution)/shard_map/ppermute | solution.py:227
  586.7 31.1 %collective-permute-start.53 = (bf16[4,3,512,256]{3,2,1,0:T(8,128)(2,1)}, bf16[4,3,512,256]{3,2,1,0:T(8,128)(2,1)}, u32[]{:S(2)}, u32[]{:S(2)}) collective-permute-start(bf16[4,3,512,256]{3,2,1,0:T(8,128)(2,1)} %get-tuple-element.275), channel_id=1, source_target_pairs={{0,4},{4,0},{8,12},{12,8},{16,20},{20,16},{24,28},{28,24},{1,5},{5... | collective-permute-start | bytes 9437192 | tf_op jit(solution)/shard_map/ppermute | solution.py:227
  604.9 29.1 %collective-permute-start.48 = (bf16[256,2048]{1,0:T(8,128)(2,1)}, bf16[256,2048]{1,0:T(8,128)(2,1)S(1)}, u32[]{:S(2)}, u32[]{:S(2)}) collective-permute-start(bf16[256,2048]{1,0:T(8,128)(2,1)} %fusion.10), channel_id=1, source_target_pairs={{0,1},{3,2},{4,5},{7,6},{8,9},{11,10},{12,13},{15,14},{16,17},{19,... | collective-permute-start | bytes 3145736 | tf_op jit(solution)/shard_map/ppermute | solution.py:227
  606.5 27.5 %collective-permute-start.49 = (bf16[256,2048]{1,0:T(8,128)(2,1)}, bf16[256,2048]{1,0:T(8,128)(2,1)S(1)}, u32[]{:S(2)}, u32[]{:S(2)}) collective-permute-start(bf16[256,2048]{1,0:T(8,128)(2,1)} %get-tuple-element.358), channel_id=1, source_target_pairs={{1,2},{2,1},{5,6},{6,5},{9,10},{10,9},{13,14},{14,13},{17,18},{18,... | collective-permute-start | bytes 3145736 | tf_op jit(solution)/shard_map/ppermute | solution.py:227
  648.4 30.5 %collective-permute-start.60 = (bf16[2,3,256,256]{3,2,1,0:T(8,128)(2,1)S(1)}, bf16[2,3,256,256]{3,2,1,0:T(8,128)(2,1)S(1)}, u32[]{:S(2)}, u32[]{:S(2)}) collective-permute-start(bf16[2,3,256,256]{3,2,1,0:T(8,128)(2,1)S(1)} %fusion.78), channel_id=1, source_target_pairs={{0,8},{4,12},{8,0},{12,4},{16,24},{20,28},{24,16},{28,20},{1,9},{5... | collective-permute-start | bytes 2359304 | tf_op jit(solution)/shard_map/ppermute | solution.py:227
  650.4 28.5 %collective-permute-start.61 = (bf16[2,3,256,256]{3,2,1,0:T(8,128)(2,1)S(1)}, bf16[2,3,256,256]{3,2,1,0:T(8,128)(2,1)S(1)}, u32[]{:S(2)}, u32[]{:S(2)}) collective-permute-start(bf16[2,3,256,256]{3,2,1,0:T(8,128)(2,1)S(1)} %fusion.79), channel_id=1, source_target_pairs={{0,16},{4,20},{8,24},{12,28},{16,0},{20,4},{24,8},{28,12},{1,17},{... | collective-permute-start | bytes 2359304 | tf_op jit(solution)/shard_map/ppermute | solution.py:227
  651.6 31.4 %collective-permute-start.56 = (bf16[256,2048]{1,0:T(8,128)(2,1)S(1)}, bf16[256,2048]{1,0:T(8,128)(2,1)S(1)}, u32[]{:S(2)}, u32[]{:S(2)}) collective-permute-start(bf16[256,2048]{1,0:T(8,128)(2,1)S(1)} %fusion.19), channel_id=1, source_target_pairs={{0,1},{1,0},{2,3},{3,2},{4,5},{5,4},{6,7},{7,6},{8,9},{9,8},{10,11... | collective-permute-start | bytes 3145736 | tf_op jit(solution)/shard_map/ppermute | solution.py:227
  (130 other events, 1747.5 us)
Sparse Core Ops, SparseCore 0:
  9.9 46.6 all-gather.4
  58.5 28.1 all-gather.6
  108.7 76.1 all-gather.8
  186.6 43.7 all-gather.10

commit v3 on v2

--- a/solution.py
+++ b/solution.py
@@ -16,7 +16,8 @@
 LOG2E = 1.4426950408889634
 EPS = 1e-06
 MASKED = -1e30
-VMEM_LIMIT = 60 << 20
+VMEM_LIMIT = 36 << 20
+ATTEND_LIMIT = 60 << 20
 SMALL = pl.CostEstimate(flops=1 << 20, bytes_accessed=1 << 16, transcendentals=0)
 NT = (((1,), (1,)), ((), ()))
 TN = (((0,), (0,)), ((), ()))
@@ -178,7 +179,7 @@
             pltpu.VMEM((WINDOW + span, HEAD_DIM), bf),
             pltpu.VMEM((HEAD_DIM, WINDOW + span), bf),
         ],
-        compiler_params=pltpu.CompilerParams(vmem_limit_bytes=VMEM_LIMIT),
+        compiler_params=pltpu.CompilerParams(vmem_limit_bytes=ATTEND_LIMIT),
         cost_estimate=SMALL,
     )(place, doc, *new, *old)
 
@@ -212,7 +213,7 @@
         + [pltpu.VMEM((WINDOW + span, HEAD_DIM), bf)] * 2
         + [pltpu.VMEM((HEAD_DIM, WINDOW + span), bf)]
         + [pltpu.VMEM((WINDOW + span, HEAD_DIM), f32)] * 2,
-        compiler_params=pltpu.CompilerParams(vmem_limit_bytes=VMEM_LIMIT),
+        compiler_params=pltpu.CompilerParams(vmem_limit_bytes=ATTEND_LIMIT),
         cost_estimate=SMALL,
     )(place, doc, lse, *new, *old, *cot, *kept)
 
@@ -249,14 +250,82 @@
     return lax.dynamic_index_in_dim(array, index, axis, keepdims=False)
 
 
-def normalize(values):
-    inverse = lax.rsqrt(jnp.mean(values * values, axis=-1, keepdims=True) + EPS)
-    return (values * inverse, inverse)
-
-
-def norm_back(grad, gain, unit, inverse):
-    scaled = grad * gain
-    return inverse * (scaled - unit * jnp.mean(scaled * unit, axis=-1, keepdims=True))
+NORM_ROWS = 64
+
+
+def row_mean(values):
+    return jnp.mean(values, axis=-1, keepdims=True)
+
+
+def total_of(first, *more):
+    total = first.astype(jnp.float32)
+    for array in more:
+        total = total + array.astype(jnp.float32)
+    return total
+
+
+def norm_kernel(parts, gain_ref, *refs):
+    total = total_of(*[ref[...] for ref in refs[:parts]])
+    inverse = lax.rsqrt(row_mean(total * total) + EPS)
+    refs[parts][...] = (total * inverse * gain_ref[...]).astype(jnp.bfloat16)
+    refs[parts + 1][...] = jnp.broadcast_to(inverse, refs[parts + 1].shape)
+    if len(refs) > parts + 2:
+        refs[parts + 2][...] = total
+
+
+def row_call(kernel, gain, arrays, outs, sums=0):
+    rows, width = arrays[0].shape
+    block = lambda w: pl.BlockSpec((NORM_ROWS, w), lambda r: (r, 0))
+    one = pl.BlockSpec((1, width), lambda r: (0, 0))
+    return pl.pallas_call(
+        kernel,
+        grid=(rows // NORM_ROWS,),
+        in_specs=[one] + [block(a.shape[1]) for a in arrays],
+        out_specs=[block(w) for w, _ in outs] + [one] * sums,
+        out_shape=[jax.ShapeDtypeStruct((rows, w), t) for w, t in outs]
+        + [jax.ShapeDtypeStruct((1, width), jnp.float32)] * sums,
+        compiler_params=pltpu.CompilerParams(vmem_limit_bytes=VMEM_LIMIT),
+        cost_estimate=SMALL,
+    )(gain[None], *arrays)
+
+
+def norm(gain, parts, keep):
+    width = parts[0].shape[1]
+    outs = [(width, jnp.bfloat16), (128, jnp.float32)] + [(width, jnp.float32)] * keep
+    return row_call(functools.partial(norm_kernel, len(parts)), gain, parts, outs)
+
+
+def norm_back_kernel(parts, gain_ref, *refs):
+    grad = total_of(*[ref[...] for ref in refs[:parts]])
+    value_ref, inverse_ref, more_ref = refs[parts : parts + 3]
+    outs = refs[parts + 3 :]
+    inverse = inverse_ref[:, :1]
+    unit = value_ref[...].astype(jnp.float32) * inverse
+    scaled = grad * gain_ref[...]
+    result = more_ref[...].astype(jnp.float32) + inverse * (
+        scaled - unit * row_mean(scaled * unit)
+    )
+    outs[0][...] = result.astype(jnp.bfloat16)
+    if len(outs) == 3:
+        outs[1][...] = result
+
+        @pl.when(pl.program_id(0) == 0)
+        def _():
+            outs[2][...] = jnp.zeros_like(outs[2])
+
+        outs[2][...] += jnp.sum(grad * unit, axis=0, keepdims=True)
+
+
+def norm_back(gain, parts, value, inverse, more, keep):
+    width = value.shape[1]
+    outs = [(width, jnp.bfloat16)] + [(width, jnp.float32)] * keep
+    return row_call(
+        functools.partial(norm_back_kernel, len(parts)),
+        gain,
+        [*parts, value, inverse, more],
+        outs,
+        sums=int(keep),
+    )
 
 
 def add(a, b):
@@ -289,17 +358,16 @@
 def grad_product(own, lhs, rhs):
     blocks = len(lhs)
     e = rhs[0][0].shape[-1]
-    count = rhs[0][0].shape[0] if rhs[0][1] is None else 1
+    count = rhs[0][1]
     groups = lhs[0].shape[1] // (2 * QB)
 
     def lhs_at(j, own):
         parity = jnp.where(j < groups, 1 - own[0], own[0])
         return (0, 2 * lax.rem(j, groups) + parity)
 
-    def rhs_at(fixed):
-        if fixed is None:
-            return pl.BlockSpec((count, QB, e), lambda j, own: (0, 0, 0))
-        return pl.BlockSpec((1, QB, e), lambda j, own: (fixed, 0, 0))
+    def rhs_at(array, k):
+        at = (0, k, 0) if array.shape[0] == count else (k, 0, 0)
+        return pl.BlockSpec((count, QB, e), lambda j, own: at)
 
     out = jax.ShapeDtypeStruct((groups, count, e, QB), jnp.bfloat16)
     return pl.pallas_call(
@@ -308,7 +376,7 @@
             num_scalar_prefetch=1,
             grid=(2 * groups,),
             in_specs=[pl.BlockSpec((QB, QB), lhs_at)] * blocks
-            + [rhs_at(fixed) for _, fixed in rhs],
+            + [rhs_at(array, k) for array, _, k in rhs],
             out_specs=[
                 pl.BlockSpec(
                     (1, count, e, QB), lambda j, own: (jnp.minimum(j, groups - 1), 0, 0, 0)
@@ -323,36 +391,32 @@
         out_shape=[out, out],
         compiler_params=pltpu.CompilerParams(vmem_limit_bytes=VMEM_LIMIT),
         cost_estimate=SMALL,
-    )(own.reshape(1).astype(jnp.int32), *lhs, *[r for r, _ in rhs])
-
-
-def turn_kernel(where_ref, a_ref, ra_ref, b_ref, rb_ref, out_ref):
-    f32 = jnp.float32
-    top = a_ref[0, 0].astype(f32) + ra_ref[0].astype(f32)
-    bottom = b_ref[0, 0].astype(f32) + rb_ref[0].astype(f32)
-    out_ref[0] = jnp.concatenate([top, bottom]).T
-
-
-def turn(one, two, a, ra, b, rb):
-    count, half, width = ra.shape
-    part = pl.BlockSpec((1, half, width), lambda s, where: (s, 0, 0))
+    )(own.reshape(1).astype(jnp.int32), *lhs, *[r[0] for r in rhs])
+
+
+def turn_kernel(group_ref, kept_ref, back_ref, *refs):
+    total = kept_ref[0, 0].astype(jnp.float32) + back_ref[0, 0].astype(jnp.float32)
+    for ref in refs[:-1]:
+        total = total + ref[0].astype(jnp.float32)
+    refs[-1][0] = total.T
+
+
+def turn(group, kept, back, parts):
+    groups, count, e, width = kept.shape
+    mine = pl.BlockSpec((1, 1, e, width), lambda s, group: (group[0], s, 0, 0))
     return pl.pallas_call(
         turn_kernel,
         grid_spec=pltpu.PrefetchScalarGridSpec(
             num_scalar_prefetch=1,
             grid=(count,),
-            in_specs=[
-                pl.BlockSpec((1, 1, half, width), lambda s, where: (where[1], s, 0, 0)),
-                part,
-                pl.BlockSpec((1, 1, half, width), lambda s, where: (where[0], s, 0, 0)),
-                part,
-            ],
-            out_specs=pl.BlockSpec((1, width, 2 * half), lambda s, where: (s, 0, 0)),
+            in_specs=[mine, mine]
+            + [pl.BlockSpec((1, e, width), lambda s, group: (s, 0, 0))] * len(parts),
+            out_specs=pl.BlockSpec((1, width, e), lambda s, group: (s, 0, 0)),
         ),
-        out_shape=jax.ShapeDtypeStruct((count, width, 2 * half), jnp.float32),
+        out_shape=jax.ShapeDtypeStruct((count, width, e), jnp.float32),
         compiler_params=pltpu.CompilerParams(vmem_limit_bytes=VMEM_LIMIT),
         cost_estimate=SMALL,
-    )(jnp.stack([one, two]).astype(jnp.int32), a, ra, b, rb)
+    )(group.reshape(1).astype(jnp.int32), kept, back, *parts)
 
 
 def rows_kernel(blocks, *refs):
@@ -377,73 +441,83 @@
 
 
 class GradSum:
-    def __init__(self, lhs, rhs):
+    def __init__(self, lhs, rhs, direct):
         me = lax.axis_index("fsdp")
         self.low, self.one, self.two = me % 2, (me // 2) % 2, me // 4
-        self.lhs, self.rhs = lhs, rhs
+        self.group = me // 2
+        self.lhs, self.rhs, self.direct = lhs, rhs, direct
         self.staged = lax.axis_size("fsdp") == 8
-        self.ra = self.rb = jnp.zeros((), jnp.bfloat16)
-
-    def first(self, *others):
+        self.back, self.parts = jnp.zeros((), jnp.bfloat16), []
+
+    def product(self, *others):
         own = self.low if self.staged else jnp.int32(1)
         self.away, self.kept = grad_product(after(own, *others), self.lhs, self.rhs)
 
-    def ready(self):
-        return [self.away, self.kept, self.ra, self.rb]
-
-    def set(self, values):
-        self.away, self.kept, self.ra, self.rb = values
-
-    def exchange(self, one_step):
-        if not self.staged:
-            return
-        if one_step == 0:
+    def swap(self):
+        if self.staged:
             self.back = send(self.away, flip(1), "fsdp")
-        else:
-            self.ra = send(self.ra, flip(2 * one_step), "fsdp")
-            self.rb = send(self.rb, flip(4 // one_step), "fsdp")
-
-    def part(self, index, axis, top, *more):
+
+    def half(self, index, axis, top, *more):
         groups, s, e, width = self.kept.shape
         start, size = [0] * 5, [2, 2, s, e // 2, width]
         start[axis], size[axis] = index, 1
         start[3] = 0 if top else e // 2
-        total = 0.0
-        for array in (self.kept, self.back):
-            cut = lax.dynamic_slice(array.reshape(2, 2, s, e, width), start, size)
-            total = total + jnp.squeeze(cut, axis).astype(jnp.float32)
-        for array in more:
-            total = total + array.astype(jnp.float32)
-        return total.astype(jnp.bfloat16)
-
-    def second(self, *others):
+        cuts = [
+            jnp.squeeze(lax.dynamic_slice(a.reshape(2, 2, s, e, width), start, size), axis)
+            for a in (self.kept, self.back)
+        ]
+        return total_of(*cuts, *more).astype(jnp.bfloat16)
+
+    def split(self):
+        if self.staged and self.direct:
+            self.parts = [
+                total_of(pick(self.kept, self.group ^ k, 0), pick(self.back, self.group ^ k, 0))
+                for k in (1, 2, 3)
+            ]
+            self.parts = [part.astype(jnp.bfloat16) for part in self.parts]
+        elif self.staged:
+            self.parts = [self.half(1 - self.one, 1, True), self.half(1 - self.two, 0, False)]
+
+    def spread(self):
+        routes = (2, 4, 6) if self.direct else (2, 4)
+        self.parts = [send(p, flip(r), "fsdp") for p, r in zip(self.parts, routes)]
+
+    def refine(self):
         if self.staged:
-            self.kept, self.back = tie(self.kept, self.back, *others)[:2]
-            self.ra = self.part(1 - self.one, 1, True)
-            self.rb = self.part(1 - self.two, 0, False)
-
-    def third(self, *others):
-        if self.staged:
-            ra, rb = tie(self.ra, self.rb, *others)[:2]
-            self.a = self.part(self.one, 1, True, ra)
-            self.b = self.part(self.two, 0, False, rb)
-            self.ra = pick(self.a, 1 - self.two, 0)
-            self.rb = pick(self.b, 1 - self.one, 0)
-
-    def last(self, turned, *others):
-        f32 = jnp.float32
+            self.a = self.half(self.one, 1, True, self.parts[0])
+            self.b = self.half(self.two, 0, False, self.parts[1])
+            self.parts = [pick(self.a, 1 - self.two, 0), pick(self.b, 1 - self.one, 0)]
+
+    def finish(self):
+        self.parts = [send(p, flip(r), "fsdp") for p, r in zip(self.parts, (4, 2))]
+
+    def own(self, turned, *others):
         if not self.staged:
             both = jnp.stack([self.away, self.kept], axis=1)
             groups, _, s, e, width = both.shape
             both = both.transpose(2, 3, 0, 1, 4).reshape(s, e, 2 * groups * width)
-            own = lax.psum_scatter(both, "fsdp", scatter_dimension=2, tiled=True).astype(f32)
+            own = lax.psum_scatter(both, "fsdp", scatter_dimension=2, tiled=True)
+            own = own.astype(jnp.float32)
             return own.transpose(0, 2, 1) if turned else own
-        ra, rb = tie(self.ra, self.rb, *others)[:2]
+        parts = tie(*self.parts, *others)[: len(self.parts)]
+        if not self.direct:
+            top = total_of(pick(self.a, self.two, 0), parts[0])
+            bottom = total_of(pick(self.b, self.one, 0), parts[1])
+            own = jnp.concatenate([top, bottom], axis=1)
+            return own.transpose(0, 2, 1) if turned else own
         if turned:
-            return turn(self.one, self.two, self.a, ra, self.b, rb)
-        top = pick(self.a, self.two, 0).astype(f32) + ra.astype(f32)
-        bottom = pick(self.b, self.one, 0).astype(f32) + rb.astype(f32)
-        return jnp.concatenate([top, bottom], axis=1)
+            return turn(self.group, self.kept, self.back, parts)
+        return total_of(pick(self.kept, self.group, 0), pick(self.back, self.group, 0), *parts)
+
+
+def join(sums, *values):
+    held = [[s.away, s.kept, s.back, *s.parts] for s in sums]
+    tied = list(tie(*values, *[h for hs in held for h in hs]))
+    out, tied = tied[: len(values)], tied[len(values) :]
+    for s, hs in zip(sums, held):
+        s.away, s.kept, s.back, *s.parts = tied[: len(hs)]
+        tied = tied[len(hs) :]
+    return out
 
 
 def per_device(layer_input, norm_gains, w_qkv, w_out, w_gate_up, w_down, doc_start, out_cotangent):
@@ -458,53 +532,50 @@
     full_out = lax.all_gather(w_out, "fsdp", axis=1, tiled=True)
     forth, back = neighbour_route(1, per_seq), neighbour_route(-1, per_seq)
 
-    input_f32 = layer_input.astype(f32)
-    unit_one, inverse_one = normalize(input_f32)
-    normed_one = (unit_one * norm_gains[0]).astype(bf)
-    x1, xm = tie(send(normed_one, PAIRS), send(normed_one, MIDDLE))
-    xf, xo = tie(send(x1, MIDDLE), send(xm, OUTWARD))
+    normed_one, inverse_one = norm(norm_gains[0], [layer_input], False)
+    xm, x1 = send(normed_one, MIDDLE), send(normed_one, PAIRS)
+    xo, xf = send(xm, OUTWARD), send(x1, MIDDLE)
+    full_qkv = after(full_qkv, x1)
+
+    def project(block):
+        return jnp.einsum("td,sde->ste", block, full_qkv, preferred_element_type=f32).astype(bf)
+
+    first = project(normed_one)
+    xf, xo, first = tie(xf, xo, first)
     x2 = jnp.where(mid, xf, xo)
     x3 = send(xf, OUTWARD)
-    cm = send(after(out_cotangent, xf), MIDDLE)
-    full_qkv = after(full_qkv, xf)
-
-    def project(block):
-        return jnp.einsum("td,sde->ste", block, full_qkv, preferred_element_type=f32).astype(bf)
-
     attn_rows = [normed_one, x1, x2]
-    new, old = [], []
-    for block in attn_rows:
-        new.append(project(block))
-        old.append(send(new[-1][1:], forth, "fsdp"))
-    tied = tie(x3, cm, *old)
-    x3, cm, old = tied[0], tied[1], list(tied[2:])
+    new = [first, project(x1), project(x2)]
+    old = [send(n[1:], forth, "fsdp") for n in new]
+    x3, *old = tie(x3, *old)
     attn_rows.append(jnp.where(mid, xm, x3))
     new.append(project(attn_rows[3]))
     old.append(send(new[3][1:], forth, "fsdp"))
     old[3], w_gate_up, w_down = tie(old[3], w_gate_up, w_down)
     full_gate_up = lax.all_gather(w_gate_up, "fsdp", axis=1, tiled=True)
     full_down = lax.all_gather(w_down, "fsdp", axis=1, tiled=True)
-    c1 = send(after(out_cotangent, new[3]), PAIRS)
+    late_cot = after(out_cotangent, new[3])
+    c1, cm = send(late_cot, PAIRS), send(late_cot, MIDDLE)
     heads_out, lse = attend(place, doc_row, new, old)
 
     def out_part(k):
         return nn(heads_out[k * QB : (k + 1) * QB], full_out).astype(bf)
 
+    def cross(middle, end):
+        return send(jnp.where(mid, middle, end), PAIRS)
+
     a3 = out_part(3)
-    t1 = send(a3, INWARD)
-    c1, cm = tie(c1, after(cm, a3))
-    cf, co = send(c1, MIDDLE), send(cm, OUTWARD)
+    y1 = cross(after(cm, a3), a3)
+    c1 = after(c1, a3)
+    cf = send(c1, MIDDLE)
     a2, a1, a0 = out_part(2), out_part(1), out_part(0)
-    t1, cf, co, a2, a1, a0 = tie(t1, cf, co, a2, a1, a0)
-    t2, t3 = send(a2, INWARD), send(add(a2, t1), MIDDLE)
-    c3 = send(cf, OUTWARD)
-    t2, t3, c3 = tie(t2, t3, c3)
-    t4, t5 = send(add(a3, t2), MIDDLE), send(add(a1, t3), PAIRS)
-    cot = [out_cotangent, c1, jnp.where(mid, cf, co), jnp.where(mid, cm, c3)]
+    y1, cf, a2, a1, a0 = tie(y1, cf, a2, a1, a0)
+    y2, t3 = cross(cf, a2), send(add(a2, y1), MIDDLE)
+    y2, t3 = tie(y2, t3)
+    t4, t5 = send(add(a3, y2), MIDDLE), send(add(a1, t3), PAIRS)
+    cot = [out_cotangent, c1, jnp.where(mid, cf, y1), jnp.where(mid, cm, y2)]
     t4, t5 = tie(t4, t5)
-    residual_mid = input_f32 + (a0.astype(f32) + t4.astype(f32) + t5.astype(f32))
-    unit_two, inverse_two = normalize(residual_mid)
-    normed_two = (unit_two * norm_gains[1]).astype(bf)
+    normed_two, inverse_two, residual_mid = norm(norm_gains[1], [layer_input, a0, t4, t5], True)
 
     def up(rows):
         return jnp.einsum("td,sdf->stf", rows, full_gate_up, preferred_element_type=f32)
@@ -516,14 +587,15 @@
         grad_act = nt(cot_rows, full_down)
         grad_up = grad_act * gate_pre * sig
         grad_gate = grad_act * up_pre * sig * (1.0 + gate_pre * (1.0 - sig))
-        grads = jnp.stack([grad_gate, grad_up]).astype(bf)
-        back_part = jnp.einsum("stf,sdf->td", grads, full_gate_up, preferred_element_type=f32)
-        return act, grads, back_part.astype(bf)
+        return act, jnp.stack([grad_gate, grad_up]).astype(bf)
+
+    def second_back(grads):
+        return jnp.einsum("stf,sdf->td", grads, full_gate_up, preferred_element_type=f32).astype(bf)
 
     m1, mm = send(normed_two, PAIRS), send(normed_two, MIDDLE)
     u0 = up(normed_two)
     m1, mm, u0 = tie(m1, mm, u0)
-    mf, mo = send(m1, MIDDLE), send(mm, OUTWARD)
+    mo, mf = send(mm, OUTWARD), send(m1, MIDDLE)
     u1 = up(m1)
     f0 = down(after(u0, u1), cot[0])
     mf, mo, u1, f0 = tie(mf, mo, u1, f0)
@@ -531,138 +603,120 @@
     m3 = send(mf, OUTWARD)
     f1 = down(u1, cot[1])
     f2 = down(up(m2), cot[2])
-    m3, f1, f2 = tie(m3, f1, f2)
+    g0, g1, g2 = second_back(f0[1]), second_back(f1[1]), second_back(f2[1])
+    m3, f1, f2, g0, g1, g2 = tie(m3, f1, f2, g0, g1, g2)
     m3 = jnp.where(mid, mm, m3)
     f3 = down(up(m3), cot[3])
-    g3, g2, g1, g0 = f3[2], f2[2], f1[2], f0[2]
+    g3 = second_back(f3[1])
 
     feed = (f0, f1, f2, f3)
-
-    def join(sums, *values):
-        count = len(values)
-        tied = tie(*values, *[r for s in sums for r in s.ready()])
-        for i, s in enumerate(sums):
-            s.set(tied[count + 4 * i : count + 4 * i + 4])
-        return tied[:count]
-
     t1 = send(g3, INWARD)
-    mlp_rows = [normed_two, m1, m2, m3]
-    up_sum = GradSum(mlp_rows, [(f[1], None) for f in feed])
-    up_sum.first(g3)
+    up_sum = GradSum([normed_two, m1, m2, m3], [(f[1], 2, 0) for f in feed], False)
+    up_sum.product(g3)
     (t1,) = join([up_sum], t1)
     t2, t3 = send(after(g2, t1), INWARD), send(add(g2, t1), MIDDLE)
-    up_sum.exchange(0)
-    down_sum = GradSum(cot, [(f[0][None], None) for f in feed])
-    down_sum.first(t1)
-    down_part = rows_product([f[0] for f in feed[:3]] + [after(f3[0], t1)], full_down)
-    t2, t3, down_part = join([down_sum], t2, t3, down_part)
+    up_sum.swap()
+    down_sum = GradSum(cot, [(f[0][None], 1, 0) for f in feed], False)
+    down_sum.product(t1)
+    t2, t3 = join([up_sum, down_sum], t2, t3)
     t4, t5 = send(add(g3, t2), MIDDLE), send(add(g1, t3), PAIRS)
-    down_sum.exchange(0)
-    up_sum.second(t2)
-    t4, t5 = join([up_sum], t4, t5)
-    grad_normed_two = g0.astype(f32) + t4.astype(f32) + t5.astype(f32)
-    grad_mid = out_cotangent.astype(f32) + norm_back(
-        grad_normed_two, norm_gains[1], unit_two, inverse_two
+    down_sum.swap()
+    up_sum.split()
+    down_part = rows_product([f[0] for f in feed[:3]] + [after(f3[0], t2)], full_down)
+    t4, t5, down_part = join([up_sum, down_sum], t4, t5, down_part)
+    grad_branch, grad_mid, gain_two = norm_back(
+        norm_gains[1], [g0, t4, t5], residual_mid, inverse_two, out_cotangent, True
     )
-    grad_branch = grad_mid.astype(bf)
 
     def heads_back(block):
         return nt(block, full_out).astype(bf)
 
     d3, d2, d1, d0 = [down_part[k * QB : (k + 1) * QB] for k in (3, 2, 1, 0)]
     b1, bm = send(grad_branch, PAIRS), send(grad_branch, MIDDLE)
-    up_sum.exchange(1)
-    down_sum.second(grad_branch)
+    up_sum.spread()
+    down_sum.kept = after(down_sum.kept, grad_branch)
+    down_sum.split()
     h0 = heads_back(grad_branch)
     b1, bm, h0 = join([down_sum], b1, bm, h0)
-    bfar, bo = send(b1, MIDDLE), send(bm, OUTWARD)
-    r1 = send(after(d3, b1), INWARD)
+    y1, bfar = cross(bm, d3), send(b1, MIDDLE)
+    down_sum.spread()
     h1 = heads_back(b1)
-    up_sum.third(b1)
-    bfar, bo, r1, h1 = join([up_sum], bfar, bo, r1, h1)
-    b2 = jnp.where(mid, bfar, bo)
-    b3 = send(bfar, OUTWARD)
-    r2, r3 = send(after(d2, bfar), INWARD), send(add(d2, r1), MIDDLE)
-    up_sum.exchange(2)
-    down_sum.exchange(1)
+    y1, bfar, h1 = join([up_sum], y1, bfar, h1)
+    b2 = jnp.where(mid, bfar, y1)
+    y2, r3 = cross(bfar, d2), send(add(d2, y1), MIDDLE)
+    up_sum.refine()
     h2 = heads_back(b2)
-    b3, r2, r3, h2 = tie(b3, r2, r3, h2)
-    b3 = jnp.where(mid, bm, b3)
+    y2, r3, h2 = join([up_sum, down_sum], y2, r3, h2)
+    b3 = jnp.where(mid, bm, y2)
     h3 = heads_back(b3)
-    r4, r5 = send(add(d3, r2), MIDDLE), send(add(d1, r3), PAIRS)
+    r4, r5 = send(add(d3, y2), MIDDLE), send(add(d1, r3), PAIRS)
+    up_sum.finish()
     cots = [h0, h1, h2, h3]
     half = heads_out.shape[1] // HEAD_DIM // 2
     *kept, prev_a = attend_back(place, doc_row, lse, new, old, cots, 0, half)
+    head_blocks = heads_out.reshape(4, QB, -1)
+    gb_blocks = [grad_branch, b1, b2, b3]
+    out_sum = GradSum(gb_blocks, [(head_blocks, 1, k) for k in range(4)], True)
+    out_sum.product(h3)
+    r4, r5, prev_a, *kept = join([out_sum, up_sum, down_sum], r4, r5, prev_a, *kept)
     n_a = send(prev_a, back, "fsdp")
-    down_sum.third(prev_a)
-    down_sum.exchange(2)
+    out_sum.swap()
     *kept, prev_b = attend_back(place, doc_row, lse, new, old, cots, half, half, kept)
+    n_a, prev_b, *kept = join([out_sum, down_sum], n_a, prev_b, *kept)
     n_b = send(prev_b, back, "fsdp")
     grad_q, own_k, own_v = kept
-    head_blocks = heads_out.reshape(4, QB, -1)
-    out_sum = GradSum([grad_branch, b1, b2, b3], [(head_blocks, k) for k in range(4)])
-    out_sum.first(prev_b)
-    up_own = up_sum.last(True, prev_b)
-    n_a, n_b, r4, r5, up_own = join([out_sum], n_a, n_b, r4, r5, up_own)
-
-    def piece(k):
-        rows = slice(k * QB, (k + 1) * QB)
+    out_sum.split()
+    down_sum.refine()
+    up_own = up_sum.own(True, prev_b)
+    n_b, up_own = join([out_sum, down_sum], n_b, up_own)
+
+    def piece(rows):
         arrived = jnp.concatenate([n_a[:, rows], n_b[:, rows]], axis=2)
         return jnp.stack([grad_q[rows], add(own_k[rows], arrived[0]), add(own_v[rows], arrived[1])])
 
     def first_back(grad):
         return jnp.einsum("ste,sde->td", grad, full_qkv, preferred_element_type=f32).astype(bf)
 
-    q3 = piece(3)
+    last = slice(3 * QB, 4 * QB)
+    q3 = piece(last)
     p3 = first_back(q3)
     t1 = send(p3, INWARD)
-    out_sum.exchange(0)
-    q2, q1, q0 = after(piece(2), p3), after(piece(1), p3), after(piece(0), p3)
-    p2, p1, p0 = first_back(q2), first_back(q1), first_back(q0)
-    qkv_sum = GradSum(attn_rows, [(q, None) for q in (q0, q1, q2, q3)])
-    qkv_sum.first(p3)
-    t1, p2, p1, p0 = join([qkv_sum], t1, p2, p1, p0)
+    out_sum.spread()
+    down_sum.finish()
+    q012 = after(piece(slice(0, 3 * QB)), p3)
+    p012 = first_back(q012)
+    qkv_sum = GradSum(attn_rows, [(q012, 3, k) for k in range(3)] + [(q3, 3, 0)], True)
+    qkv_sum.product(p3)
+    t1, p012, p3 = join([qkv_sum, out_sum, down_sum], t1, p012, p3)
+    p0, p1, p2 = [p012[k * QB : (k + 1) * QB] for k in range(3)]
     t2, t3 = send(p2, INWARD), send(add(p2, t1), MIDDLE)
-    qkv_sum.exchange(0)
+    qkv_sum.swap()
+    qkv_sum.split()
+    qkv_sum.spread()
+    late = tie(p0, p1, p2, p3, qkv_sum.back)[:4]
     gain_one = functools.reduce(
         jnp.add,
-        [
-            jnp.sum(p.astype(f32) * r.astype(f32), axis=0)
-            for p, r in zip((p0, p1, p2, p3), attn_rows)
-        ],
+        [jnp.sum(p.astype(f32) * r.astype(f32), axis=0) for p, r in zip(late, attn_rows)],
     )
-    gain_two = jnp.sum(grad_normed_two * unit_two, axis=0)
-    gains = jnp.stack([gain_one / norm_gains[0], gain_two])
-    step = 1
-    while step < lax.axis_size("fsdp"):
-        gains = gains + send(gains, flip(step), "fsdp")
-        step *= 2
-    qkv_sum.second(t1)
-    out_sum.second(t1)
-    t2, t3, gains = join([qkv_sum, out_sum], t2, t3, gains)
-    s1 = send(gains, INWARD)
+    gains = jnp.stack([gain_one / norm_gains[0], gain_two[0]])
+    if lax.axis_size("fsdp") == 8:
+        gains = [gains] + [send(gains, flip(k), "fsdp") for k in range(1, 8)]
+    else:
+        gains = [lax.psum(gains, "fsdp")]
+    down_own = down_sum.own(False)
+    t2, t3, down_own, *gains = tie(t2, t3, down_own, *gains)
     t4, t5 = send(add(p3, t2), MIDDLE), send(add(p1, t3), PAIRS)
-    qkv_sum.exchange(1)
-    out_sum.exchange(1)
+    gains = total_of(*gains)
+    out_own = out_sum.own(False, t2)
     layer_output = (
         residual_mid + (d0.astype(f32) + r4.astype(f32) + after(r5, t2).astype(f32))
     ).astype(bf)
-    down_own = down_sum.last(False, t2)
-    gains = gains + s1
-    s2 = send(gains, MIDDLE)
-    qkv_sum.third(down_own)
-    qkv_sum.exchange(2)
-    out_sum.third(down_own)
-    out_sum.exchange(2)
-    gains = gains + s2
-    s3 = send(gains, OUTWARD)
-    grad_normed_one = p0.astype(f32) + t4.astype(f32) + t5.astype(f32)
-    input_grad = (
-        grad_mid + norm_back(grad_normed_one, norm_gains[0], unit_one, inverse_one)
-    ).astype(bf)
-    out_own = out_sum.last(False)
-    qkv_own = qkv_sum.last(True)
-    gains = jnp.where(mid, gains, s3)
+    t4, t5, gains, layer_output, out_own = tie(t4, t5, gains, layer_output, out_own)
+    gains = total_of(gains, *[send(gains, flip(k, "tp"), "tp") for k in (1, 2, 3)])
+    (input_grad,) = norm_back(
+        norm_gains[0], [p0, t4, t5], layer_input, inverse_one, grad_mid, False
+    )
+    qkv_own = qkv_sum.own(True, t5)
     return (layer_output, input_grad, gains, qkv_own, out_own[0], up_own, down_own[0])
 
 

time: 725 us -> 690 us (0.952)
  waiting for transfers between devices: 221 us -> 263 us
  starting transfers between devices: 149 us -> 109 us
  other arithmetic: 92.7 us -> 68.4 us
  matrix products: 102 us -> 87.9 us
  local copies, waits for them, and re-layouts: 18.2 us -> 28.9 us
  Pallas kernels: 115 us -> 106 us
    ppermute x72 -> x70, starting transfers between devices: 149 us -> 109 us  [send(): return lax.ppermute(block, axis, route)]
    ppermute x72 -> x70, waiting for transfers between devices: 220 us -> 249 us  [send(): return lax.ppermute(block, axis, route)]
    convert_element_type x18 -> x9, other arithmetic: 35.1 us -> 21.3 us  [the longest x7 17.7 us: half(): return total_of(*cuts, *more).astype(jnp.bfloat16)]
    all_gather x1, waiting for transfers between devices: 0.01 us -> 13.2 us  [per_device(): full_qkv = lax.all_gather(w_qkv, 'fsdp', axis=1, tiled=True)]
    unnamed x157 -> x238, local copies, waits for them, and re-layouts: 10.3 us -> 21.2 us
    pallas_call x4, Pallas kernels: 55.9 us -> 45.7 us  [grad_product(): pl.pallas_call(functools.partial(grad_kernel, blocks), grid_spec=pltpu.Pr...]
    pallas_call x0 -> x4, Pallas kernels: none -> 8.86 us  [row_call(): pl.pallas_call(kernel, grid=(rows // NORM_ROWS,), in_specs=[one] + [block...]
    dot_general x4 -> x2, matrix products: 18.5 us -> 11.3 us  [first_back(): jnp.einsum('ste,sde->td', grad, full_qkv, preferred_element_type=f32)]
  transfers between devices with their start and end apart: 76 -> 74, of which waited for: 32 -> 39; matrix products, arithmetic and copies ran while one was open for 27% -> 21% of each run, Pallas kernels for 15% -> 15%
where the time goes in v3:
time: 690 us; the launch traced here: 679 us
  waiting for transfers between devices  263 us (38%)
  starting transfers between devices  109 us (16%)
  Pallas kernels  106 us (15%)
  matrix products  87.9 us (13%)
  other arithmetic  68.4 us (10%)
  local copies, waits for them, and re-layouts  28.9 us (4%)
  between operations  16.2 us (2%)
    ppermute x70, waiting for transfers between devices, send(): return lax.ppermute(block, axis, route)  249 us
    ppermute x70, starting transfers between devices, send(): return lax.ppermute(block, axis, route)  109 us
    pallas_call x4, Pallas kernels, grad_product(): pl.pallas_call(functools.partial(grad_kernel, blocks), grid_spec=pltpu.Pr...  45.7 us
    pallas_call x2, Pallas kernels, attend_back(): pl.pallas_call(functools.partial(back_kernel, first), grid=(heads,), in_s...  26 us
    dot_general x8, matrix products, nt(): return lax.dot_general(a, b, NT, preferred_element_type=jnp.float32)  22.8 us
    dot_general x4, matrix products, up(): jnp.einsum('td,sdf->stf', rows, full_gate_up, preferred_element_type=f32)  21.9 us
    unnamed x238, local copies, waits for them, and re-layouts  21.2 us
    convert_element_type x7, other arithmetic, half(): return total_of(*cuts, *more).astype(jnp.bfloat16)  17.7 us
  transfers between devices with their start and end apart: 74, of which 39 were waited for; matrix products, arithmetic and copies ran while one was open for 21% of the time, Pallas kernels for 15%

profile of v3, /device:TPU:8, one launch (start us, length us, event | category | flops | bytes accessed | tf_op | source)
XLA Modules:
  0.0 679.3 jit_solution(6104576182038051119)
XLA Ops:
  14.4 23.2 %collective-permute-done.1 = bf16[256,2048]{1,0:T(8,128)(2,1)} collective-permute-done((bf16[256,2048]{1,0:T(8,128)(2,1)S(1)}, bf16[256,2048]{1,0:T(8,128)(2,1)}, u32[]{:S(2)}, u32[]{:S(2)}) %collective-permute-start.1) | collective-permute-done | bytes 1048608 | tf_op jit(solution)/shard_map/ppermute | solution.py:228
  43.4 13.2 %all-gather.5.cloned.1.call-done = bf16[3,2048,512]{2,1,0:T(8,128)(2,1)} async-done(((bf16[3,256,512]{2,1,0:T(8,128)(2,1)}), bf16[3,2048,512]{2,1,0:T(8,128)(2,1)}) %all-gather.5.cloned.1.call-update) | async-done | bytes 6291472 | tf_op jit(solution)/shard_map/all_gather | solution.py:531
  77.9 16.4 %collective-permute-done.4 = bf16[256,2048]{1,0:T(8,128)(2,1)S(1)} collective-permute-done((bf16[256,2048]{1,0:T(8,128)(2,1)}, bf16[256,2048]{1,0:T(8,128)(2,1)S(1)}, u32[]{:S(2)}, u32[]{:S(2)}) %collective-permute-start.4) | collective-permute-done | bytes 1048608 | tf_op jit(solution)/shard_map/ppermute | solution.py:228
  107.4 13.7 %shard_map.136 = (bf16[1024,512]{1,0:T(8,128)(2,1)}, f32[4,1024]{1,0:T(4,128)}) custom-call(s32[2]{0:T(128)} %pad_add_fusion.place_ref, s32[1,1024]{1,0:T(1,128)} %bitcast.425, bf16[3,256,512]{2,1,0:T(8,128)(2,1)} %copy-done.63, bf16[3,256,512]{2,1,0:T(8,128)(2,1)} %copy-done.62, bf16[3,256,512]{2,1,0:T(8,128)(2,1)} %copy-done.64, ...), custom_call_target="tpu_custom_call" | custom-call | flops 1048576 | bytes 65536 | tf_op jit(solution)/shard_map/pallas_call | solution.py:166
  135.5 16.2 %collective-permute-done.10 = bf16[256,2048]{1,0:T(8,128)(2,1)S(1)} collective-permute-done((bf16[256,2048]{1,0:T(8,128)(2,1)S(1)}, bf16[256,2048]{1,0:T(8,128)(2,1)S(1)}, u32[]{:S(2)}, u32[]{:S(2)}) %collective-permute-start.10) | collective-permute-done | bytes 1048608 | tf_op jit(solution)/shard_map/ppermute | solution.py:228
  159.7 19.6 %collective-permute-done.13 = bf16[256,2048]{1,0:T(8,128)(2,1)S(1)} collective-permute-done((bf16[256,2048]{1,0:T(8,128)(2,1)S(1)}, bf16[256,2048]{1,0:T(8,128)(2,1)S(1)}, u32[]{:S(2)}, u32[]{:S(2)}) %collective-permute-start.13) | collective-permute-done | bytes 1048608 | tf_op jit(solution)/shard_map/ppermute | solution.py:228
  186.7 22.4 %collective-permute-done.15.refs_2_ = bf16[256,2048]{1,0:T(8,128)(2,1)S(1)} collective-permute-done((bf16[256,2048]{1,0:T(8,128)(2,1)S(1)}, bf16[256,2048]{1,0:T(8,128)(2,1)S(1)}, u32[]{:S(2)}, u32[]{:S(2)}) %collective-permute-start.15) | collective-permute-done | bytes 1048608 | tf_op jit(solution)/shard_map/ppermute | solution.py:228
  218.8 9.5 %convolution_bitcast_fusion.3 = f32[2,256,1376]{2,1,0:T(8,128)} fusion(bf16[2,2048,1376]{1,2,0:T(8,128)(2,1)} %all-gather.11.cloned.1.call-done, bf16[256,2048]{1,0:T(8,128)(2,1)} %get-tuple-element.224.refs_0_), kind=kOutput, calls=%fused_computation.4 | convolution fusion | flops 2885681152 | bytes 15138816 | tf_op jit(solution)/shard_map/td,sdf->stf/dot_general | solution.py:581
  228.3 14.1 %collective-permute-done.18 = bf16[256,2048]{1,0:T(8,128)(2,1)} collective-permute-done((bf16[256,2048]{1,0:T(8,128)(2,1)}, bf16[256,2048]{1,0:T(8,128)(2,1)}, u32[]{:S(2)}, u32[]{:S(2)}) %collective-permute-start.18) | collective-permute-done | bytes 1048608 | tf_op jit(solution)/shard_map/ppermute | solution.py:228
  249.3 6.0 convolution_bitcast_fusion.2
  255.4 7.0 %fusion.69 = (bf16[1,256,1376]{2,1,0:T(8,128)(2,1)S(1)}, bf16[1,256,1376]{2,1,0:T(8,128)(2,1)S(1)}, bf16[256,1376]{1,0:T(8,128)(2,1)}) fusion(f32[2,256,1376]{2,1,0:T(8,128)} %convolution_bitcast_fusion.3, bf16[1376,2048]{1,0:T(8,128)(2,1)} %all-gather.9.cloned.1.call-done.refs_4_, bf16[256,2048]{1,0:T(8,128)(2,1)} %refs_5_.1), kind=kOutput, calls=%fused_computation.172 | convolution fusion | flops 1448476672 | bytes 11616256 | tf_op jit(solution)/shard_map/dot_general | solution.py:27
  321.2 18.0 %shard_map.138 = (bf16[4,2,1376,256]{3,2,1,0:T(8,128)(2,1)S(1)}, bf16[4,2,1376,256]{3,2,1,0:T(8,128)(2,1)}) custom-call(s32[1]{0:T(128)} %bitcast.40.which_ref, bf16[256,2048]{1,0:T(8,128)(2,1)} %get-tuple-element.224.refs_0_, bf16[256,2048]{1,0:T(8,128)(2,1)} %collective-permute-done.17.refs_1_, bf16[256,2048]{1,0:T(8,128)(2,1)S(1)} %copy-done.32, ...), custom_call_target="tpu_custom_call" | custom-call | flops 1048576 | bytes 65536 | tf_op jit(solution)/shard_map/pallas_call | solution.py:373
  347.6 10.4 %shard_map.139 = (bf16[4,1,1376,256]{3,2,1,0:T(8,128)(2,1)}, bf16[4,1,1376,256]{3,2,1,0:T(8,128)(2,1)S(1)}) custom-call(s32[1]{0:T(128)} %bitcast.41.which_ref, bf16[256,2048]{1,0:T(8,128)(2,1)S(1)} %copy-done.21, bf16[256,2048]{1,0:T(8,128)(2,1)S(1)} %copy-done.50, bf16[256,2048]{1,0:T(8,128)(2,1)S(1)} %copy-done.36, bf16[256,2048]{1,0:T(8,128)(2,1)S(1)} %copy-done.30, ...), custom_call_target="tpu_custom_call" | custom-call | flops 1048576 | bytes 65536 | tf_op jit(solution)/shard_map/pallas_call | solution.py:373
  357.9 12.4 %collective-permute-done.24 = bf16[256,2048]{1,0:T(8,128)(2,1)S(1)} collective-permute-done((bf16[256,2048]{1,0:T(8,128)(2,1)}, bf16[256,2048]{1,0:T(8,128)(2,1)S(1)}, u32[]{:S(2)}, u32[]{:S(2)}) %collective-permute-start.24) | collective-permute-done | bytes 1048608 | tf_op jit(solution)/shard_map/ppermute | solution.py:228
  386.8 7.9 %shard_map.140 = bf16[1024,2048]{1,0:T(8,128)(2,1)S(1)} custom-call(bf16[256,1376]{1,0:T(8,128)(2,1)S(1)} %copy-done.38, bf16[256,1376]{1,0:T(8,128)(2,1)S(1)} %copy-done.40, bf16[256,1376]{1,0:T(8,128)(2,1)S(1)} %copy-done.42, bf16[256,1376]{1,0:T(8,128)(2,1)S(1)} %copy-done.56, bf16[1376,2048]{1,0:T(8,128)(2,1)S(1)} %copy-done.19), custom_call_target="tpu_custom_call" | custom-call | flops 1048576 | bytes 65536 | tf_op jit(solution)/shard_map/pallas_call | solution.py:431
  417.8 17.2 %collective-permute-done.30 = bf16[256,2048]{1,0:T(8,128)(2,1)S(1)} collective-permute-done((bf16[256,2048]{1,0:T(8,128)(2,1)S(1)}, bf16[256,2048]{1,0:T(8,128)(2,1)S(1)}, u32[]{:S(2)}, u32[]{:S(2)}) %collective-permute-start.30) | collective-permute-done | bytes 1048608 | tf_op jit(solution)/shard_map/ppermute | solution.py:228
  443.8 15.9 %collective-permute-done.31 = bf16[256,2048]{1,0:T(8,128)(2,1)S(1)} collective-permute-done((bf16[256,2048]{1,0:T(8,128)(2,1)S(1)}, bf16[256,2048]{1,0:T(8,128)(2,1)S(1)}, u32[]{:S(2)}, u32[]{:S(2)}) %collective-permute-start.31) | collective-permute-done | bytes 1048608 | tf_op jit(solution)/shard_map/ppermute | solution.py:228
  498.4 6.1 shard_map.143
  505.4 13.0 %shard_map.142 = (bf16[1024,512]{1,0:T(8,128)(2,1)}, f32[1024,512]{1,0:T(8,128)}, f32[1024,512]{1,0:T(8,128)}, bf16[2,1024,256]{2,1,0:T(8,128)(2,1)}) custom-call(s32[2]{0:T(128)} %pad_add_fusion.place_ref, s32[1,1024]{1,0:T(1,128)} %bitcast.426, f32[4,1024]{1,0:T(4,128)} %get-tuple-element.286.lse_ref, bf16[3,256,512]{2,1,0:T(8,128)(2,1)} %copy-done.63, ...), custom_call_target="tpu_custom_call" | custom-call | flops 1048576 | bytes 65536 | tf_op jit(solution)/shard_map/pallas_call | solution.py:192
  521.1 13.0 %shard_map.144 = (bf16[1024,512]{1,0:T(8,128)(2,1)}, f32[1024,512]{1,0:T(8,128)}, f32[1024,512]{1,0:T(8,128)}, bf16[2,1024,256]{2,1,0:T(8,128)(2,1)}) custom-call(s32[2]{0:T(128)} %pad_add_fusion.place_ref, s32[1,1024]{1,0:T(1,128)} %bitcast.427, ...), custom_call_target="tpu_custom_call", output_to_operand_aliasing={{0}: (15, {}), {1}: (16, {}), {2}: (17, {})} | custom-call | flops 1048576 | bytes 65536 | tf_op jit(solution)/shard_map/pallas_call | solution.py:192
  568.5 6.6 bitcast_convert_fusion
  576.3 11.3 %shard_map.145 = (bf16[4,3,512,256]{3,2,1,0:T(8,128)(2,1)}, bf16[4,3,512,256]{3,2,1,0:T(8,128)(2,1)S(1)}) custom-call(s32[1]{0:T(128)} %bitcast.89.which_ref, bf16[256,2048]{1,0:T(8,128)(2,1)S(1)} %copy-done.24, bf16[256,2048]{1,0:T(8,128)(2,1)S(1)} %copy-done.27, bf16[256,2048]{1,0:T(8,128)(2,1)S(1)} %copy-done.4, bf16[256,2048]{1,0:T(8,128)(2,1)S(1)} %copy-done.7, ...), custom_call_target="tpu_custom_call" | custom-call | flops 1048576 | bytes 65536 | tf_op jit(solution)/shard_map/pallas_call | solution.py:373
  606.6 15.3 %collective-permute-done.53 = bf16[256,2048]{1,0:T(8,128)(2,1)S(1)} collective-permute-done((bf16[256,2048]{1,0:T(8,128)(2,1)S(1)}, bf16[256,2048]{1,0:T(8,128)(2,1)S(1)}, u32[]{:S(2)}, u32[]{:S(2)}) %collective-permute-start.53) | collective-permute-done | bytes 1048608 | tf_op jit(solution)/shard_map/ppermute | solution.py:228
  642.6 15.2 %collective-permute-done.63.refs_2_ = bf16[256,2048]{1,0:T(8,128)(2,1)S(1)} collective-permute-done((bf16[256,2048]{1,0:T(8,128)(2,1)S(1)}, bf16[256,2048]{1,0:T(8,128)(2,1)S(1)}, u32[]{:S(2)}, u32[]{:S(2)}) %collective-permute-start.63) | collective-permute-done | bytes 1048608 | tf_op jit(solution)/shard_map/ppermute | solution.py:228
  (480 shorter events, 339.4 us)
Async XLA Ops:
  7.2 49.5 %all-gather.5.cloned.1.call-start = ((), (), s32[]{:S(2)}) async-start(), calls=%async_computation | async-start | bytes 7077888 | tf_op jit(solution)/shard_map/all_gather | solution.py:531
  7.9 113.1 %all-gather.7.cloned.1.call-start = ((), (), s32[]{:S(2)}) async-start(), calls=%async_computation.1 | async-start | bytes 2359296 | tf_op jit(solution)/shard_map/all_gather | solution.py:532
  14.3 204.5 %all-gather.11.cloned.1.call-start = ((), (), s32[]{:S(2)}) async-start(), calls=%async_computation.3 | async-start | bytes 12681216 | tf_op jit(solution)/shard_map/all_gather | solution.py:555
  37.6 27.9 %collective-permute-start.3 = (bf16[256,2048]{1,0:T(8,128)(2,1)}, bf16[256,2048]{1,0:T(8,128)(2,1)}, u32[]{:S(2)}, u32[]{:S(2)}) collective-permute-start(bf16[256,2048]{1,0:T(8,128)(2,1)} %collective-permute-done.1), channel_id=1, source_target_pairs={{1,0},{2,3},{5,4},{6,7},{9,8},{10,11},{13,12},{14,15},{17,16},{18,... | collective-permute-start | bytes 3145736 | tf_op jit(solution)/shard_map/ppermute | solution.py:228
  100.6 154.7 %all-gather.9.cloned.1.call-start = ((), (), s32[]{:S(2)}) async-start(), calls=%async_computation.2 | async-start | bytes 6340608 | tf_op jit(solution)/shard_map/all_gather | solution.py:556
  181.9 27.2 %collective-permute-start.15 = (bf16[256,2048]{1,0:T(8,128)(2,1)S(1)}, bf16[256,2048]{1,0:T(8,128)(2,1)S(1)}, u32[]{:S(2)}, u32[]{:S(2)}) collective-permute-start(bf16[256,2048]{1,0:T(8,128)(2,1)S(1)} %add_convert_fusion.13), channel_id=1, source_target_pairs={{1,2},{2,1},{5,6},{6,5},{9,10},{10,9},{13,14},{14,13},{17,18},{18,... | collective-permute-start | bytes 3145736 | tf_op jit(solution)/shard_map/ppermute | solution.py:228
  214.4 27.9 %collective-permute-start.18 = (bf16[256,2048]{1,0:T(8,128)(2,1)}, bf16[256,2048]{1,0:T(8,128)(2,1)}, u32[]{:S(2)}, u32[]{:S(2)}) collective-permute-start(bf16[256,2048]{1,0:T(8,128)(2,1)} %get-tuple-element.224.refs_0_), channel_id=1, source_target_pairs={{1,2},{2,1},{5,6},{6,5},{9,10},{10,9},{13,14},{14,13},{17,18},{18,... | collective-permute-start | bytes 3145736 | tf_op jit(solution)/shard_map/ppermute | solution.py:228
  272.7 27.6 %collective-permute-start.21 = (bf16[256,2048]{1,0:T(8,128)(2,1)}, bf16[256,2048]{1,0:T(8,128)(2,1)S(1)}, u32[]{:S(2)}, u32[]{:S(2)}) collective-permute-start(bf16[256,2048]{1,0:T(8,128)(2,1)} %collective-permute-done.19), channel_id=1, source_target_pairs={{1,0},{2,3},{5,4},{6,7},{9,8},{10,11},{13,12},{14,15},{17,16},{18,... | collective-permute-start | bytes 3145736 | tf_op jit(solution)/shard_map/ppermute | solution.py:228
  339.7 33.3 %collective-permute-start.25 = (bf16[4,2,1376,256]{3,2,1,0:T(8,128)(2,1)S(1)}, bf16[4,2,1376,256]{3,2,1,0:T(8,128)(2,1)}, u32[]{:S(2)}, u32[]{:S(2)}) collective-permute-start(bf16[4,2,1376,256]{3,2,1,0:T(8,128)(2,1)S(1)} %get-tuple-element.242), channel_id=1, source_target_pairs={{0,4},{4,0},{8,12},{12,8},{16,20},{20,16},{24,28},{28,24},{1,5},{5... | collective-permute-start | bytes 16908296 | tf_op jit(solution)/shard_map/ppermute | solution.py:228
  342.5 27.9 %collective-permute-start.24 = (bf16[256,2048]{1,0:T(8,128)(2,1)}, bf16[256,2048]{1,0:T(8,128)(2,1)S(1)}, u32[]{:S(2)}, u32[]{:S(2)}) collective-permute-start(bf16[256,2048]{1,0:T(8,128)(2,1)} %add_convert_fusion.11), channel_id=1, source_target_pairs={{1,2},{2,1},{5,6},{6,5},{9,10},{10,9},{13,14},{14,13},{17,18},{18,... | collective-permute-start | bytes 3145736 | tf_op jit(solution)/shard_map/ppermute | solution.py:228
  345.8 27.2 %collective-permute-start.23 = (bf16[256,2048]{1,0:T(8,128)(2,1)S(1)}, bf16[256,2048]{1,0:T(8,128)(2,1)S(1)}, u32[]{:S(2)}, u32[]{:S(2)}) collective-permute-start(bf16[256,2048]{1,0:T(8,128)(2,1)S(1)} %copy-done.91), channel_id=1, source_target_pairs={{0,1},{3,2},{4,5},{7,6},{8,9},{11,10},{12,13},{15,14},{16,17},{19,... | collective-permute-start | bytes 3145736 | tf_op jit(solution)/shard_map/ppermute | solution.py:228
  372.9 31.7 %collective-permute-start.28 = (bf16[4,1,1376,256]{3,2,1,0:T(8,128)(2,1)}, bf16[4,1,1376,256]{3,2,1,0:T(8,128)(2,1)}, u32[]{:S(2)}, u32[]{:S(2)}) collective-permute-start(bf16[4,1,1376,256]{3,2,1,0:T(8,128)(2,1)} %get-tuple-element.256), channel_id=1, source_target_pairs={{0,4},{4,0},{8,12},{12,8},{16,20},{20,16},{24,28},{28,24},{1,5},{5... | collective-permute-start | bytes 8454152 | tf_op jit(solution)/shard_map/ppermute | solution.py:228
  376.9 27.8 %collective-permute-start.26 = (bf16[256,2048]{1,0:T(8,128)(2,1)}, bf16[256,2048]{1,0:T(8,128)(2,1)}, u32[]{:S(2)}, u32[]{:S(2)}) collective-permute-start(bf16[256,2048]{1,0:T(8,128)(2,1)} %add_convert_fusion.10), channel_id=1, source_target_pairs={{1,2},{2,1},{5,6},{6,5},{9,10},{10,9},{13,14},{14,13},{17,18},{18,... | collective-permute-start | bytes 3145736 | tf_op jit(solution)/shard_map/ppermute | solution.py:228
  411.4 32.3 %collective-permute-start.33 = (bf16[2,2,688,256]{3,2,1,0:T(8,128)(2,1)S(1)}, bf16[2,2,688,256]{3,2,1,0:T(8,128)(2,1)S(1)}, u32[]{:S(2)}, u32[]{:S(2)}) collective-permute-start(bf16[2,2,688,256]{3,2,1,0:T(8,128)(2,1)S(1)} %fusion.40), channel_id=1, source_target_pairs={{0,8},{4,12},{8,0},{12,4},{16,24},{20,28},{24,16},{28,20},{1,9},{5... | collective-permute-start | bytes 4227080 | tf_op jit(solution)/shard_map/ppermute | solution.py:228
  411.5 32.3 %collective-permute-start.34 = (bf16[2,2,688,256]{3,2,1,0:T(8,128)(2,1)S(1)}, bf16[2,2,688,256]{3,2,1,0:T(8,128)(2,1)S(1)}, u32[]{:S(2)}, u32[]{:S(2)}) collective-permute-start(bf16[2,2,688,256]{3,2,1,0:T(8,128)(2,1)S(1)} %fusion.41), channel_id=1, source_target_pairs={{0,16},{4,20},{8,24},{12,28},{16,0},{20,4},{24,8},{28,12},{1,17},{... | collective-permute-start | bytes 4227080 | tf_op jit(solution)/shard_map/ppermute | solution.py:228
  555.3 32.3 %collective-permute-start.48 = (bf16[1,512,256]{2,1,0:T(8,128)(2,1)S(1)}, bf16[1,512,256]{2,1,0:T(8,128)(2,1)S(1)}, u32[]{:S(2)}, u32[]{:S(2)}) collective-permute-start(bf16[1,512,256]{2,1,0:T(8,128)(2,1)S(1)} %get-tuple-element.340), channel_id=1, source_target_pairs={{0,16},{4,20},{8,24},{12,28},{16,0},{20,4},{24,8},{28,12},{1,17},{... | collective-permute-start | bytes 786440 | tf_op jit(solution)/shard_map/ppermute | solution.py:228
  556.8 30.8 %collective-permute-start.49 = (bf16[1,512,256]{2,1,0:T(8,128)(2,1)S(1)}, bf16[1,512,256]{2,1,0:T(8,128)(2,1)S(1)}, u32[]{:S(2)}, u32[]{:S(2)}) collective-permute-start(bf16[1,512,256]{2,1,0:T(8,128)(2,1)S(1)} %get-tuple-element.341), channel_id=1, source_target_pairs={{0,24},{4,28},{8,16},{12,20},{16,8},{20,12},{24,0},{28,4},{1,25},{... | collective-permute-start | bytes 786440 | tf_op jit(solution)/shard_map/ppermute | solution.py:228
  556.9 30.8 %collective-permute-start.50 = (bf16[1,688,256]{2,1,0:T(8,128)(2,1)S(1)}, bf16[1,688,256]{2,1,0:T(8,128)(2,1)S(1)}, u32[]{:S(2)}, u32[]{:S(2)}) collective-permute-start(bf16[1,688,256]{2,1,0:T(8,128)(2,1)S(1)} %dynamic-slice_bitcast_fusion.3), channel_id=1, source_target_pairs={{0,16},{4,20},{8,24},{12,28},{16,0},{20,4},{24,8},{28,12},{1,17},{... | collective-permute-start | bytes 1056776 | tf_op jit(solution)/shard_map/ppermute | solution.py:228
  563.3 27.8 %collective-permute-start.46 = (bf16[256,2048]{1,0:T(8,128)(2,1)S(1)}, bf16[256,2048]{1,0:T(8,128)(2,1)S(1)}, u32[]{:S(2)}, u32[]{:S(2)}) collective-permute-start(bf16[256,2048]{1,0:T(8,128)(2,1)S(1)} %fusion.6), channel_id=1, source_target_pairs={{0,1},{3,2},{4,5},{7,6},{8,9},{11,10},{12,13},{15,14},{16,17},{19,... | collective-permute-start | bytes 3145736 | tf_op jit(solution)/shard_map/ppermute | solution.py:228
  594.4 27.5 %collective-permute-start.53 = (bf16[256,2048]{1,0:T(8,128)(2,1)S(1)}, bf16[256,2048]{1,0:T(8,128)(2,1)S(1)}, u32[]{:S(2)}, u32[]{:S(2)}) collective-permute-start(bf16[256,2048]{1,0:T(8,128)(2,1)S(1)} %add_convert_fusion.5), channel_id=1, source_target_pairs={{1,2},{2,1},{5,6},{6,5},{9,10},{10,9},{13,14},{14,13},{17,18},{18,... | collective-permute-start | bytes 3145736 | tf_op jit(solution)/shard_map/ppermute | solution.py:228
  597.8 27.2 %collective-permute-start.52 = (bf16[256,2048]{1,0:T(8,128)(2,1)S(1)}, bf16[256,2048]{1,0:T(8,128)(2,1)S(1)}, u32[]{:S(2)}, u32[]{:S(2)}) collective-permute-start(bf16[256,2048]{1,0:T(8,128)(2,1)S(1)} %get-tuple-element.354), channel_id=1, source_target_pairs={{0,1},{3,2},{4,5},{7,6},{8,9},{11,10},{12,13},{15,14},{16,17},{19,... | collective-permute-start | bytes 3145736 | tf_op jit(solution)/shard_map/ppermute | solution.py:228
  629.1 32.1 %collective-permute-start.69 = (bf16[3,512,256]{2,1,0:T(8,128)(2,1)S(1)}, bf16[3,512,256]{2,1,0:T(8,128)(2,1)S(1)}, u32[]{:S(2)}, u32[]{:S(2)}) collective-permute-start(bf16[3,512,256]{2,1,0:T(8,128)(2,1)S(1)} %get-tuple-element.393), channel_id=1, source_target_pairs={{0,24},{4,28},{8,16},{12,20},{16,8},{20,12},{24,0},{28,4},{1,25},{... | collective-permute-start | bytes 2359304 | tf_op jit(solution)/shard_map/ppermute | solution.py:228
  629.7 36.2 %collective-permute-start.68 = (bf16[3,512,256]{2,1,0:T(8,128)(2,1)S(1)}, bf16[3,512,256]{2,1,0:T(8,128)(2,1)S(1)}, u32[]{:S(2)}, u32[]{:S(2)}) collective-permute-start(bf16[3,512,256]{2,1,0:T(8,128)(2,1)S(1)} %get-tuple-element.394), channel_id=1, source_target_pairs={{0,16},{4,20},{8,24},{12,28},{16,0},{20,4},{24,8},{28,12},{1,17},{... | collective-permute-start | bytes 2359304 | tf_op jit(solution)/shard_map/ppermute | solution.py:228
  631.2 34.7 %collective-permute-start.67 = (bf16[3,512,256]{2,1,0:T(8,128)(2,1)S(1)}, bf16[3,512,256]{2,1,0:T(8,128)(2,1)S(1)}, u32[]{:S(2)}, u32[]{:S(2)}) collective-permute-start(bf16[3,512,256]{2,1,0:T(8,128)(2,1)S(1)} %get-tuple-element.395), channel_id=1, source_target_pairs={{0,8},{4,12},{8,0},{12,4},{16,24},{20,28},{24,16},{28,20},{1,9},{5... | collective-permute-start | bytes 2359304 | tf_op jit(solution)/shard_map/ppermute | solution.py:228
  (170 other events, 2306.3 us)
Sparse Core Ops, SparseCore 0:
  9.9 46.6 all-gather.4
  58.5 29.4 all-gather.6
  100.7 74.8 all-gather.10
  177.3 43.7 all-gather.8

commit v4 on v3

--- a/solution.py
+++ b/solution.py
@@ -667,8 +667,7 @@
     grad_q, own_k, own_v = kept
     out_sum.split()
     down_sum.refine()
-    up_own = up_sum.own(True, prev_b)
-    n_b, up_own = join([out_sum, down_sum], n_b, up_own)
+    (n_b,) = join([out_sum, down_sum], n_b)
 
     def piece(rows):
         arrived = jnp.concatenate([n_a[:, rows], n_b[:, rows]], axis=2)
@@ -681,6 +680,8 @@
     q3 = piece(last)
     p3 = first_back(q3)
     t1 = send(p3, INWARD)
+    out_sum.parts = [after(p, p3) for p in out_sum.parts]
+    down_sum.parts = [after(p, p3) for p in down_sum.parts]
     out_sum.spread()
     down_sum.finish()
     q012 = after(piece(slice(0, 3 * QB)), p3)
@@ -704,7 +705,8 @@
     else:
         gains = [lax.psum(gains, "fsdp")]
     down_own = down_sum.own(False)
-    t2, t3, down_own, *gains = tie(t2, t3, down_own, *gains)
+    up_own = up_sum.own(True, qkv_sum.back)
+    t2, t3, down_own, up_own, *gains = tie(t2, t3, down_own, up_own, *gains)
     t4, t5 = send(add(p3, t2), MIDDLE), send(add(p1, t3), PAIRS)
     gains = total_of(*gains)
     out_own = out_sum.own(False, t2)

time: 690 us -> 688 us (level)
    unnamed x238 -> x236, local copies, waits for them, and re-layouts: 21.2 us -> 24 us
  transfers between devices with their start and end apart: 74 -> 74, of which waited for: 39 -> 40; matrix products, arithmetic and copies ran while one was open for 21% -> 20% of each run, Pallas kernels for 15% -> 15%
where the time goes in v4:
time: 688 us; the launch traced here: 677 us
  waiting for transfers between devices  257 us (37%)
  starting transfers between devices  112 us (16%)
  Pallas kernels  106 us (15%)
  matrix products  88 us (13%)
  other arithmetic  68.8 us (10%)
  local copies, waits for them, and re-layouts  29.4 us (4%)
  between operations  15.9 us (2%)
    ppermute x70, waiting for transfers between devices, send(): return lax.ppermute(block, axis, route)  243 us
    ppermute x70, starting transfers between devices, send(): return lax.ppermute(block, axis, route)  112 us
    pallas_call x4, Pallas kernels, grad_product(): pl.pallas_call(functools.partial(grad_kernel, blocks), grid_spec=pltpu.Pr...  45.7 us
    pallas_call x2, Pallas kernels, attend_back(): pl.pallas_call(functools.partial(back_kernel, first), grid=(heads,), in_s...  26 us
    unnamed x236, local copies, waits for them, and re-layouts  24 us
    dot_general x8, matrix products, nt(): return lax.dot_general(a, b, NT, preferred_element_type=jnp.float32)  22.8 us
    dot_general x4, matrix products, up(): jnp.einsum('td,sdf->stf', rows, full_gate_up, preferred_element_type=f32)  21.9 us
    convert_element_type x7, other arithmetic, half(): return total_of(*cuts, *more).astype(jnp.bfloat16)  17.9 us
  transfers between devices with their start and end apart: 74, of which 40 were waited for; matrix products, arithmetic and copies ran while one was open for 20% of the time, Pallas kernels for 15%

profile of v4, /device:TPU:8, one launch (start us, length us, event | category | flops | bytes accessed | tf_op | source)
XLA Modules:
  0.0 677.3 jit_solution(7911563414522546477)
XLA Ops:
  14.4 23.2 %collective-permute-done.1 = bf16[256,2048]{1,0:T(8,128)(2,1)} collective-permute-done((bf16[256,2048]{1,0:T(8,128)(2,1)S(1)}, bf16[256,2048]{1,0:T(8,128)(2,1)}, u32[]{:S(2)}, u32[]{:S(2)}) %collective-permute-start.1) | collective-permute-done | bytes 1048608 | tf_op jit(solution)/shard_map/ppermute | solution.py:228
  43.4 13.3 %all-gather.5.cloned.1.call-done = bf16[3,2048,512]{2,1,0:T(8,128)(2,1)} async-done(((bf16[3,256,512]{2,1,0:T(8,128)(2,1)}), bf16[3,2048,512]{2,1,0:T(8,128)(2,1)}) %all-gather.5.cloned.1.call-update) | async-done | bytes 6291472 | tf_op jit(solution)/shard_map/all_gather | solution.py:531
  77.9 16.4 %collective-permute-done.4 = bf16[256,2048]{1,0:T(8,128)(2,1)S(1)} collective-permute-done((bf16[256,2048]{1,0:T(8,128)(2,1)}, bf16[256,2048]{1,0:T(8,128)(2,1)S(1)}, u32[]{:S(2)}, u32[]{:S(2)}) %collective-permute-start.4) | collective-permute-done | bytes 1048608 | tf_op jit(solution)/shard_map/ppermute | solution.py:228
  107.3 13.7 %shard_map.136 = (bf16[1024,512]{1,0:T(8,128)(2,1)}, f32[4,1024]{1,0:T(4,128)}) custom-call(s32[2]{0:T(128)} %pad_add_fusion.place_ref, s32[1,1024]{1,0:T(1,128)} %bitcast.425, bf16[3,256,512]{2,1,0:T(8,128)(2,1)} %copy-done.63, bf16[3,256,512]{2,1,0:T(8,128)(2,1)} %copy-done.62, bf16[3,256,512]{2,1,0:T(8,128)(2,1)} %copy-done.64, ...), custom_call_target="tpu_custom_call" | custom-call | flops 1048576 | bytes 65536 | tf_op jit(solution)/shard_map/pallas_call | solution.py:166
  135.2 16.4 %collective-permute-done.10 = bf16[256,2048]{1,0:T(8,128)(2,1)S(1)} collective-permute-done((bf16[256,2048]{1,0:T(8,128)(2,1)S(1)}, bf16[256,2048]{1,0:T(8,128)(2,1)S(1)}, u32[]{:S(2)}, u32[]{:S(2)}) %collective-permute-start.10) | collective-permute-done | bytes 1048608 | tf_op jit(solution)/shard_map/ppermute | solution.py:228
  159.7 19.6 %collective-permute-done.13 = bf16[256,2048]{1,0:T(8,128)(2,1)S(1)} collective-permute-done((bf16[256,2048]{1,0:T(8,128)(2,1)S(1)}, bf16[256,2048]{1,0:T(8,128)(2,1)S(1)}, u32[]{:S(2)}, u32[]{:S(2)}) %collective-permute-start.13) | collective-permute-done | bytes 1048608 | tf_op jit(solution)/shard_map/ppermute | solution.py:228
  186.7 22.4 %collective-permute-done.15.refs_2_ = bf16[256,2048]{1,0:T(8,128)(2,1)S(1)} collective-permute-done((bf16[256,2048]{1,0:T(8,128)(2,1)S(1)}, bf16[256,2048]{1,0:T(8,128)(2,1)S(1)}, u32[]{:S(2)}, u32[]{:S(2)}) %collective-permute-start.15) | collective-permute-done | bytes 1048608 | tf_op jit(solution)/shard_map/ppermute | solution.py:228
  218.8 9.5 %convolution_bitcast_fusion.3 = f32[2,256,1376]{2,1,0:T(8,128)} fusion(bf16[2,2048,1376]{1,2,0:T(8,128)(2,1)} %all-gather.11.cloned.1.call-done, bf16[256,2048]{1,0:T(8,128)(2,1)} %get-tuple-element.229.refs_0_), kind=kOutput, calls=%fused_computation.4 | convolution fusion | flops 2885681152 | bytes 15138816 | tf_op jit(solution)/shard_map/td,sdf->stf/dot_general | solution.py:581
  228.3 14.1 %collective-permute-done.18 = bf16[256,2048]{1,0:T(8,128)(2,1)} collective-permute-done((bf16[256,2048]{1,0:T(8,128)(2,1)}, bf16[256,2048]{1,0:T(8,128)(2,1)}, u32[]{:S(2)}, u32[]{:S(2)}) %collective-permute-start.18) | collective-permute-done | bytes 1048608 | tf_op jit(solution)/shard_map/ppermute | solution.py:228
  255.3 7.0 %fusion.69 = (bf16[1,256,1376]{2,1,0:T(8,128)(2,1)S(1)}, bf16[1,256,1376]{2,1,0:T(8,128)(2,1)S(1)}, bf16[256,1376]{1,0:T(8,128)(2,1)}) fusion(f32[2,256,1376]{2,1,0:T(8,128)} %convolution_bitcast_fusion.3, bf16[1376,2048]{1,0:T(8,128)(2,1)} %all-gather.9.cloned.1.call-done.refs_4_, bf16[256,2048]{1,0:T(8,128)(2,1)} %refs_5_.1), kind=kOutput, calls=%fused_computation.172 | convolution fusion | flops 1448476672 | bytes 11616256 | tf_op jit(solution)/shard_map/dot_general | solution.py:27
  321.1 18.0 %shard_map.138 = (bf16[4,2,1376,256]{3,2,1,0:T(8,128)(2,1)S(1)}, bf16[4,2,1376,256]{3,2,1,0:T(8,128)(2,1)}) custom-call(s32[1]{0:T(128)} %bitcast.40.which_ref, bf16[256,2048]{1,0:T(8,128)(2,1)} %get-tuple-element.229.refs_0_, bf16[256,2048]{1,0:T(8,128)(2,1)} %collective-permute-done.17.refs_1_, bf16[256,2048]{1,0:T(8,128)(2,1)S(1)} %copy-done.32, ...), custom_call_target="tpu_custom_call" | custom-call | flops 1048576 | bytes 65536 | tf_op jit(solution)/shard_map/pallas_call | solution.py:373
  347.7 10.4 %shard_map.139 = (bf16[4,1,1376,256]{3,2,1,0:T(8,128)(2,1)}, bf16[4,1,1376,256]{3,2,1,0:T(8,128)(2,1)S(1)}) custom-call(s32[1]{0:T(128)} %bitcast.41.which_ref, bf16[256,2048]{1,0:T(8,128)(2,1)S(1)} %copy-done.21, bf16[256,2048]{1,0:T(8,128)(2,1)S(1)} %copy-done.50, bf16[256,2048]{1,0:T(8,128)(2,1)S(1)} %copy-done.36, bf16[256,2048]{1,0:T(8,128)(2,1)S(1)} %copy-done.30, ...), custom_call_target="tpu_custom_call" | custom-call | flops 1048576 | bytes 65536 | tf_op jit(solution)/shard_map/pallas_call | solution.py:373
  358.1 12.4 %collective-permute-done.24 = bf16[256,2048]{1,0:T(8,128)(2,1)S(1)} collective-permute-done((bf16[256,2048]{1,0:T(8,128)(2,1)}, bf16[256,2048]{1,0:T(8,128)(2,1)S(1)}, u32[]{:S(2)}, u32[]{:S(2)}) %collective-permute-start.24) | collective-permute-done | bytes 1048608 | tf_op jit(solution)/shard_map/ppermute | solution.py:228
  386.9 7.9 %shard_map.140 = bf16[1024,2048]{1,0:T(8,128)(2,1)S(1)} custom-call(bf16[256,1376]{1,0:T(8,128)(2,1)S(1)} %copy-done.38, bf16[256,1376]{1,0:T(8,128)(2,1)S(1)} %copy-done.40, bf16[256,1376]{1,0:T(8,128)(2,1)S(1)} %copy-done.42, bf16[256,1376]{1,0:T(8,128)(2,1)S(1)} %copy-done.56, bf16[1376,2048]{1,0:T(8,128)(2,1)S(1)} %copy-done.19), custom_call_target="tpu_custom_call" | custom-call | flops 1048576 | bytes 65536 | tf_op jit(solution)/shard_map/pallas_call | solution.py:431
  417.9 17.2 %collective-permute-done.30 = bf16[256,2048]{1,0:T(8,128)(2,1)S(1)} collective-permute-done((bf16[256,2048]{1,0:T(8,128)(2,1)S(1)}, bf16[256,2048]{1,0:T(8,128)(2,1)S(1)}, u32[]{:S(2)}, u32[]{:S(2)}) %collective-permute-start.30) | collective-permute-done | bytes 1048608 | tf_op jit(solution)/shard_map/ppermute | solution.py:228
  443.9 15.9 %collective-permute-done.31 = bf16[256,2048]{1,0:T(8,128)(2,1)S(1)} collective-permute-done((bf16[256,2048]{1,0:T(8,128)(2,1)S(1)}, bf16[256,2048]{1,0:T(8,128)(2,1)S(1)}, u32[]{:S(2)}, u32[]{:S(2)}) %collective-permute-start.31) | collective-permute-done | bytes 1048608 | tf_op jit(solution)/shard_map/ppermute | solution.py:228
  498.8 6.1 shard_map.143
  505.9 13.0 %shard_map.142 = (bf16[1024,512]{1,0:T(8,128)(2,1)}, f32[1024,512]{1,0:T(8,128)}, f32[1024,512]{1,0:T(8,128)}, bf16[2,1024,256]{2,1,0:T(8,128)(2,1)}) custom-call(s32[2]{0:T(128)} %pad_add_fusion.place_ref, s32[1,1024]{1,0:T(1,128)} %bitcast.426, f32[4,1024]{1,0:T(4,128)} %get-tuple-element.291.lse_ref, bf16[3,256,512]{2,1,0:T(8,128)(2,1)} %copy-done.63, ...), custom_call_target="tpu_custom_call" | custom-call | flops 1048576 | bytes 65536 | tf_op jit(solution)/shard_map/pallas_call | solution.py:192
  521.9 13.0 %shard_map.144 = (bf16[1024,512]{1,0:T(8,128)(2,1)}, f32[1024,512]{1,0:T(8,128)}, f32[1024,512]{1,0:T(8,128)}, bf16[2,1024,256]{2,1,0:T(8,128)(2,1)}) custom-call(s32[2]{0:T(128)} %pad_add_fusion.place_ref, s32[1,1024]{1,0:T(1,128)} %bitcast.427, ...), custom_call_target="tpu_custom_call", output_to_operand_aliasing={{0}: (15, {}), {1}: (16, {}), {2}: (17, {})} | custom-call | flops 1048576 | bytes 65536 | tf_op jit(solution)/shard_map/pallas_call | solution.py:192
  553.2 6.5 collective-permute-start.47
  569.5 6.5 bitcast_convert_fusion
  577.3 11.3 %shard_map.145 = (bf16[4,3,512,256]{3,2,1,0:T(8,128)(2,1)}, bf16[4,3,512,256]{3,2,1,0:T(8,128)(2,1)S(1)}) custom-call(s32[1]{0:T(128)} %bitcast.86.which_ref, bf16[256,2048]{1,0:T(8,128)(2,1)S(1)} %copy-done.24, bf16[256,2048]{1,0:T(8,128)(2,1)S(1)} %copy-done.27, bf16[256,2048]{1,0:T(8,128)(2,1)S(1)} %copy-done.4, bf16[256,2048]{1,0:T(8,128)(2,1)S(1)} %copy-done.7, ...), custom_call_target="tpu_custom_call" | custom-call | flops 1048576 | bytes 65536 | tf_op jit(solution)/shard_map/pallas_call | solution.py:373
  609.4 10.4 %collective-permute-done.53 = bf16[256,2048]{1,0:T(8,128)(2,1)S(1)} collective-permute-done((bf16[256,2048]{1,0:T(8,128)(2,1)S(1)}, bf16[256,2048]{1,0:T(8,128)(2,1)S(1)}, u32[]{:S(2)}, u32[]{:S(2)}) %collective-permute-start.53) | collective-permute-done | bytes 1048608 | tf_op jit(solution)/shard_map/ppermute | solution.py:228
  640.3 15.1 %collective-permute-done.63.refs_2_ = bf16[256,2048]{1,0:T(8,128)(2,1)S(1)} collective-permute-done((bf16[256,2048]{1,0:T(8,128)(2,1)S(1)}, bf16[256,2048]{1,0:T(8,128)(2,1)S(1)}, u32[]{:S(2)}, u32[]{:S(2)}) %collective-permute-start.63) | collective-permute-done | bytes 1048608 | tf_op jit(solution)/shard_map/ppermute | solution.py:228
  (478 shorter events, 341.9 us)
Async XLA Ops:
  7.2 49.5 %all-gather.5.cloned.1.call-start = ((), (), s32[]{:S(2)}) async-start(), calls=%async_computation | async-start | bytes 7077888 | tf_op jit(solution)/shard_map/all_gather | solution.py:531
  7.9 113.1 %all-gather.7.cloned.1.call-start = ((), (), s32[]{:S(2)}) async-start(), calls=%async_computation.1 | async-start | bytes 2359296 | tf_op jit(solution)/shard_map/all_gather | solution.py:532
  10.7 26.9 %collective-permute-start.1 = (bf16[256,2048]{1,0:T(8,128)(2,1)S(1)}, bf16[256,2048]{1,0:T(8,128)(2,1)}, u32[]{:S(2)}, u32[]{:S(2)}) collective-permute-start(bf16[256,2048]{1,0:T(8,128)(2,1)S(1)} %get-tuple-element.204.refs_0_), channel_id=1, source_target_pairs={{1,2},{2,1},{5,6},{6,5},{9,10},{10,9},{13,14},{14,13},{17,18},{18,... | collective-permute-start | bytes 3145736 | tf_op jit(solution)/shard_map/ppermute | solution.py:228
  14.3 204.5 %all-gather.11.cloned.1.call-start = ((), (), s32[]{:S(2)}) async-start(), calls=%async_computation.3 | async-start | bytes 12681216 | tf_op jit(solution)/shard_map/all_gather | solution.py:555
  37.6 27.9 %collective-permute-start.3 = (bf16[256,2048]{1,0:T(8,128)(2,1)}, bf16[256,2048]{1,0:T(8,128)(2,1)}, u32[]{:S(2)}, u32[]{:S(2)}) collective-permute-start(bf16[256,2048]{1,0:T(8,128)(2,1)} %collective-permute-done.1), channel_id=1, source_target_pairs={{1,0},{2,3},{5,4},{6,7},{9,8},{10,11},{13,12},{14,15},{17,16},{18,... | collective-permute-start | bytes 3145736 | tf_op jit(solution)/shard_map/ppermute | solution.py:228
  100.6 154.6 %all-gather.9.cloned.1.call-start = ((), (), s32[]{:S(2)}) async-start(), calls=%async_computation.2 | async-start | bytes 6340608 | tf_op jit(solution)/shard_map/all_gather | solution.py:556
  181.9 27.2 %collective-permute-start.15 = (bf16[256,2048]{1,0:T(8,128)(2,1)S(1)}, bf16[256,2048]{1,0:T(8,128)(2,1)S(1)}, u32[]{:S(2)}, u32[]{:S(2)}) collective-permute-start(bf16[256,2048]{1,0:T(8,128)(2,1)S(1)} %add_convert_fusion.13), channel_id=1, source_target_pairs={{1,2},{2,1},{5,6},{6,5},{9,10},{10,9},{13,14},{14,13},{17,18},{18,... | collective-permute-start | bytes 3145736 | tf_op jit(solution)/shard_map/ppermute | solution.py:228
  214.4 27.9 %collective-permute-start.18 = (bf16[256,2048]{1,0:T(8,128)(2,1)}, bf16[256,2048]{1,0:T(8,128)(2,1)}, u32[]{:S(2)}, u32[]{:S(2)}) collective-permute-start(bf16[256,2048]{1,0:T(8,128)(2,1)} %get-tuple-element.229.refs_0_), channel_id=1, source_target_pairs={{1,2},{2,1},{5,6},{6,5},{9,10},{10,9},{13,14},{14,13},{17,18},{18,... | collective-permute-start | bytes 3145736 | tf_op jit(solution)/shard_map/ppermute | solution.py:228
  245.6 27.1 %collective-permute-start.19 = (bf16[256,2048]{1,0:T(8,128)(2,1)}, bf16[256,2048]{1,0:T(8,128)(2,1)}, u32[]{:S(2)}, u32[]{:S(2)}) collective-permute-start(bf16[256,2048]{1,0:T(8,128)(2,1)} %collective-permute-done.17.refs_1_), channel_id=1, source_target_pairs={{1,2},{2,1},{5,6},{6,5},{9,10},{10,9},{13,14},{14,13},{17,18},{18,... | collective-permute-start | bytes 3145736 | tf_op jit(solution)/shard_map/ppermute | solution.py:228
  272.7 27.8 %collective-permute-start.21 = (bf16[256,2048]{1,0:T(8,128)(2,1)}, bf16[256,2048]{1,0:T(8,128)(2,1)S(1)}, u32[]{:S(2)}, u32[]{:S(2)}) collective-permute-start(bf16[256,2048]{1,0:T(8,128)(2,1)} %collective-permute-done.19), channel_id=1, source_target_pairs={{1,0},{2,3},{5,4},{6,7},{9,8},{10,11},{13,12},{14,15},{17,16},{18,... | collective-permute-start | bytes 3145736 | tf_op jit(solution)/shard_map/ppermute | solution.py:228
  339.8 33.3 %collective-permute-start.25 = (bf16[4,2,1376,256]{3,2,1,0:T(8,128)(2,1)S(1)}, bf16[4,2,1376,256]{3,2,1,0:T(8,128)(2,1)}, u32[]{:S(2)}, u32[]{:S(2)}) collective-permute-start(bf16[4,2,1376,256]{3,2,1,0:T(8,128)(2,1)S(1)} %get-tuple-element.247), channel_id=1, source_target_pairs={{0,4},{4,0},{8,12},{12,8},{16,20},{20,16},{24,28},{28,24},{1,5},{5... | collective-permute-start | bytes 16908296 | tf_op jit(solution)/shard_map/ppermute | solution.py:228
  342.6 27.9 %collective-permute-start.24 = (bf16[256,2048]{1,0:T(8,128)(2,1)}, bf16[256,2048]{1,0:T(8,128)(2,1)S(1)}, u32[]{:S(2)}, u32[]{:S(2)}) collective-permute-start(bf16[256,2048]{1,0:T(8,128)(2,1)} %add_convert_fusion.11), channel_id=1, source_target_pairs={{1,2},{2,1},{5,6},{6,5},{9,10},{10,9},{13,14},{14,13},{17,18},{18,... | collective-permute-start | bytes 3145736 | tf_op jit(solution)/shard_map/ppermute | solution.py:228
  345.9 27.2 %collective-permute-start.23 = (bf16[256,2048]{1,0:T(8,128)(2,1)S(1)}, bf16[256,2048]{1,0:T(8,128)(2,1)S(1)}, u32[]{:S(2)}, u32[]{:S(2)}) collective-permute-start(bf16[256,2048]{1,0:T(8,128)(2,1)S(1)} %copy-done.92), channel_id=1, source_target_pairs={{0,1},{3,2},{4,5},{7,6},{8,9},{11,10},{12,13},{15,14},{16,17},{19,... | collective-permute-start | bytes 3145736 | tf_op jit(solution)/shard_map/ppermute | solution.py:228
  373.1 31.7 %collective-permute-start.28 = (bf16[4,1,1376,256]{3,2,1,0:T(8,128)(2,1)}, bf16[4,1,1376,256]{3,2,1,0:T(8,128)(2,1)}, u32[]{:S(2)}, u32[]{:S(2)}) collective-permute-start(bf16[4,1,1376,256]{3,2,1,0:T(8,128)(2,1)} %get-tuple-element.261), channel_id=1, source_target_pairs={{0,4},{4,0},{8,12},{12,8},{16,20},{20,16},{24,28},{28,24},{1,5},{5... | collective-permute-start | bytes 8454152 | tf_op jit(solution)/shard_map/ppermute | solution.py:228
  377.0 27.8 %collective-permute-start.26 = (bf16[256,2048]{1,0:T(8,128)(2,1)}, bf16[256,2048]{1,0:T(8,128)(2,1)}, u32[]{:S(2)}, u32[]{:S(2)}) collective-permute-start(bf16[256,2048]{1,0:T(8,128)(2,1)} %add_convert_fusion.10), channel_id=1, source_target_pairs={{1,2},{2,1},{5,6},{6,5},{9,10},{10,9},{13,14},{14,13},{17,18},{18,... | collective-permute-start | bytes 3145736 | tf_op jit(solution)/shard_map/ppermute | solution.py:228
  411.6 32.3 %collective-permute-start.33 = (bf16[2,2,688,256]{3,2,1,0:T(8,128)(2,1)S(1)}, bf16[2,2,688,256]{3,2,1,0:T(8,128)(2,1)S(1)}, u32[]{:S(2)}, u32[]{:S(2)}) collective-permute-start(bf16[2,2,688,256]{3,2,1,0:T(8,128)(2,1)S(1)} %fusion.40), channel_id=1, source_target_pairs={{0,8},{4,12},{8,0},{12,4},{16,24},{20,28},{24,16},{28,20},{1,9},{5... | collective-permute-start | bytes 4227080 | tf_op jit(solution)/shard_map/ppermute | solution.py:228
  411.6 32.3 %collective-permute-start.34 = (bf16[2,2,688,256]{3,2,1,0:T(8,128)(2,1)S(1)}, bf16[2,2,688,256]{3,2,1,0:T(8,128)(2,1)S(1)}, u32[]{:S(2)}, u32[]{:S(2)}) collective-permute-start(bf16[2,2,688,256]{3,2,1,0:T(8,128)(2,1)S(1)} %fusion.41), channel_id=1, source_target_pairs={{0,16},{4,20},{8,24},{12,28},{16,0},{20,4},{24,8},{28,12},{1,17},{... | collective-permute-start | bytes 4227080 | tf_op jit(solution)/shard_map/ppermute | solution.py:228
  551.7 37.0 %collective-permute-start.46 = (bf16[256,2048]{1,0:T(8,128)(2,1)S(1)}, bf16[256,2048]{1,0:T(8,128)(2,1)S(1)}, u32[]{:S(2)}, u32[]{:S(2)}) collective-permute-start(bf16[256,2048]{1,0:T(8,128)(2,1)S(1)} %fusion.6), channel_id=1, source_target_pairs={{0,1},{3,2},{4,5},{7,6},{8,9},{11,10},{12,13},{15,14},{16,17},{19,... | collective-permute-start | bytes 3145736 | tf_op jit(solution)/shard_map/ppermute | solution.py:228
  560.6 28.0 %collective-permute-start.48 = (bf16[1,512,256]{2,1,0:T(8,128)(2,1)S(1)}, bf16[1,512,256]{2,1,0:T(8,128)(2,1)S(1)}, u32[]{:S(2)}, u32[]{:S(2)}) collective-permute-start(bf16[1,512,256]{2,1,0:T(8,128)(2,1)S(1)} %get-tuple-element.343), channel_id=1, source_target_pairs={{0,16},{4,20},{8,24},{12,28},{16,0},{20,4},{24,8},{28,12},{1,17},{... | collective-permute-start | bytes 786440 | tf_op jit(solution)/shard_map/ppermute | solution.py:228
  592.2 27.6 %collective-permute-start.53 = (bf16[256,2048]{1,0:T(8,128)(2,1)S(1)}, bf16[256,2048]{1,0:T(8,128)(2,1)S(1)}, u32[]{:S(2)}, u32[]{:S(2)}) collective-permute-start(bf16[256,2048]{1,0:T(8,128)(2,1)S(1)} %add_convert_fusion.5), channel_id=1, source_target_pairs={{1,2},{2,1},{5,6},{6,5},{9,10},{10,9},{13,14},{14,13},{17,18},{18,... | collective-permute-start | bytes 3145736 | tf_op jit(solution)/shard_map/ppermute | solution.py:228
  595.3 27.2 %collective-permute-start.52 = (bf16[256,2048]{1,0:T(8,128)(2,1)S(1)}, bf16[256,2048]{1,0:T(8,128)(2,1)S(1)}, u32[]{:S(2)}, u32[]{:S(2)}) collective-permute-start(bf16[256,2048]{1,0:T(8,128)(2,1)S(1)} %get-tuple-element.364), channel_id=1, source_target_pairs={{0,1},{3,2},{4,5},{7,6},{8,9},{11,10},{12,13},{15,14},{16,17},{19,... | collective-permute-start | bytes 3145736 | tf_op jit(solution)/shard_map/ppermute | solution.py:228
  626.5 32.4 %collective-permute-start.69 = (bf16[3,512,256]{2,1,0:T(8,128)(2,1)S(1)}, bf16[3,512,256]{2,1,0:T(8,128)(2,1)S(1)}, u32[]{:S(2)}, u32[]{:S(2)}) collective-permute-start(bf16[3,512,256]{2,1,0:T(8,128)(2,1)S(1)} %get-tuple-element.403), channel_id=1, source_target_pairs={{0,24},{4,28},{8,16},{12,20},{16,8},{20,12},{24,0},{28,4},{1,25},{... | collective-permute-start | bytes 2359304 | tf_op jit(solution)/shard_map/ppermute | solution.py:228
  628.3 35.6 %collective-permute-start.68 = (bf16[3,512,256]{2,1,0:T(8,128)(2,1)S(1)}, bf16[3,512,256]{2,1,0:T(8,128)(2,1)S(1)}, u32[]{:S(2)}, u32[]{:S(2)}) collective-permute-start(bf16[3,512,256]{2,1,0:T(8,128)(2,1)S(1)} %get-tuple-element.404), channel_id=1, source_target_pairs={{0,16},{4,20},{8,24},{12,28},{16,0},{20,4},{24,8},{28,12},{1,17},{... | collective-permute-start | bytes 2359304 | tf_op jit(solution)/shard_map/ppermute | solution.py:228
  628.6 35.5 %collective-permute-start.67 = (bf16[3,512,256]{2,1,0:T(8,128)(2,1)S(1)}, bf16[3,512,256]{2,1,0:T(8,128)(2,1)S(1)}, u32[]{:S(2)}, u32[]{:S(2)}) collective-permute-start(bf16[3,512,256]{2,1,0:T(8,128)(2,1)S(1)} %get-tuple-element.405), channel_id=1, source_target_pairs={{0,8},{4,12},{8,0},{12,4},{16,24},{20,28},{24,16},{28,20},{1,9},{5... | collective-permute-start | bytes 2359304 | tf_op jit(solution)/shard_map/ppermute | solution.py:228
  (169 other events, 2296.8 us)
Sparse Core Ops, SparseCore 0:
  9.9 46.6 all-gather.4
  58.5 29.4 all-gather.6
  100.7 74.8 all-gather.10
  177.4 43.7 all-gather.8

commit v5 on v4

--- a/solution.py
+++ b/solution.py
@@ -680,12 +680,12 @@
     q3 = piece(last)
     p3 = first_back(q3)
     t1 = send(p3, INWARD)
-    out_sum.parts = [after(p, p3) for p in out_sum.parts]
-    down_sum.parts = [after(p, p3) for p in down_sum.parts]
+    q012 = after(piece(slice(0, 3 * QB)), p3)
+    p012 = first_back(q012)
+    out_sum.parts = [after(p, p012) for p in out_sum.parts]
+    down_sum.parts = [after(p, p012) for p in down_sum.parts]
     out_sum.spread()
     down_sum.finish()
-    q012 = after(piece(slice(0, 3 * QB)), p3)
-    p012 = first_back(q012)
     qkv_sum = GradSum(attn_rows, [(q012, 3, k) for k in range(3)] + [(q3, 3, 0)], True)
     qkv_sum.product(p3)
     t1, p012, p3 = join([qkv_sum, out_sum, down_sum], t1, p012, p3)

time: 688 us -> 688 us (level)
  transfers between devices with their start and end apart: 74 -> 74, of which waited for: 40 -> 39; matrix products, arithmetic and copies ran while one was open for 20% -> 20% of each run, Pallas kernels for 15% -> 15%
where the time goes in v5:
time: 688 us; the launch traced here: 678 us
  waiting for transfers between devices  260 us (38%)
  starting transfers between devices  111 us (16%)
  Pallas kernels  106 us (15%)
  matrix products  88 us (13%)
  other arithmetic  68.8 us (10%)
  local copies, waits for them, and re-layouts  28.3 us (4%)
  between operations  16 us (2%)
    ppermute x70, waiting for transfers between devices, send(): return lax.ppermute(block, axis, route)  246 us
    ppermute x70, starting transfers between devices, send(): return lax.ppermute(block, axis, route)  111 us
    pallas_call x4, Pallas kernels, grad_product(): pl.pallas_call(functools.partial(grad_kernel, blocks), grid_spec=pltpu.Pr...  45.8 us
    pallas_call x2, Pallas kernels, attend_back(): pl.pallas_call(functools.partial(back_kernel, first), grid=(heads,), in_s...  26 us
    unnamed x236, local copies, waits for them, and re-layouts  22.9 us
    dot_general x8, matrix products, nt(): return lax.dot_general(a, b, NT, preferred_element_type=jnp.float32)  22.8 us
    dot_general x4, matrix products, up(): jnp.einsum('td,sdf->stf', rows, full_gate_up, preferred_element_type=f32)  21.9 us
    convert_element_type x7, other arithmetic, half(): return total_of(*cuts, *more).astype(jnp.bfloat16)  17.9 us
  transfers between devices with their start and end apart: 74, of which 39 were waited for; matrix products, arithmetic and copies ran while one was open for 20% of the time, Pallas kernels for 15%

profile of v5, /device:TPU:8, one launch (start us, length us, event | category | flops | bytes accessed | tf_op | source)
XLA Modules:
  0.0 677.7 jit_solution(7898487097674820486)
XLA Ops:
  14.4 23.2 %collective-permute-done.1 = bf16[256,2048]{1,0:T(8,128)(2,1)} collective-permute-done((bf16[256,2048]{1,0:T(8,128)(2,1)S(1)}, bf16[256,2048]{1,0:T(8,128)(2,1)}, u32[]{:S(2)}, u32[]{:S(2)}) %collective-permute-start.1) | collective-permute-done | bytes 1048608 | tf_op jit(solution)/shard_map/ppermute | solution.py:228
  43.4 13.3 %all-gather.5.cloned.1.call-done = bf16[3,2048,512]{2,1,0:T(8,128)(2,1)} async-done(((bf16[3,256,512]{2,1,0:T(8,128)(2,1)}), bf16[3,2048,512]{2,1,0:T(8,128)(2,1)}) %all-gather.5.cloned.1.call-update) | async-done | bytes 6291472 | tf_op jit(solution)/shard_map/all_gather | solution.py:531
  77.9 16.4 %collective-permute-done.4 = bf16[256,2048]{1,0:T(8,128)(2,1)S(1)} collective-permute-done((bf16[256,2048]{1,0:T(8,128)(2,1)}, bf16[256,2048]{1,0:T(8,128)(2,1)S(1)}, u32[]{:S(2)}, u32[]{:S(2)}) %collective-permute-start.4) | collective-permute-done | bytes 1048608 | tf_op jit(solution)/shard_map/ppermute | solution.py:228
  107.3 13.7 %shard_map.136 = (bf16[1024,512]{1,0:T(8,128)(2,1)}, f32[4,1024]{1,0:T(4,128)}) custom-call(s32[2]{0:T(128)} %pad_add_fusion.place_ref, s32[1,1024]{1,0:T(1,128)} %bitcast.425, bf16[3,256,512]{2,1,0:T(8,128)(2,1)} %copy-done.63, bf16[3,256,512]{2,1,0:T(8,128)(2,1)} %copy-done.62, bf16[3,256,512]{2,1,0:T(8,128)(2,1)} %copy-done.64, ...), custom_call_target="tpu_custom_call" | custom-call | flops 1048576 | bytes 65536 | tf_op jit(solution)/shard_map/pallas_call | solution.py:166
  135.2 16.4 %collective-permute-done.10 = bf16[256,2048]{1,0:T(8,128)(2,1)S(1)} collective-permute-done((bf16[256,2048]{1,0:T(8,128)(2,1)S(1)}, bf16[256,2048]{1,0:T(8,128)(2,1)S(1)}, u32[]{:S(2)}, u32[]{:S(2)}) %collective-permute-start.10) | collective-permute-done | bytes 1048608 | tf_op jit(solution)/shard_map/ppermute | solution.py:228
  159.7 19.6 %collective-permute-done.13 = bf16[256,2048]{1,0:T(8,128)(2,1)S(1)} collective-permute-done((bf16[256,2048]{1,0:T(8,128)(2,1)S(1)}, bf16[256,2048]{1,0:T(8,128)(2,1)S(1)}, u32[]{:S(2)}, u32[]{:S(2)}) %collective-permute-start.13) | collective-permute-done | bytes 1048608 | tf_op jit(solution)/shard_map/ppermute | solution.py:228
  186.7 22.4 %collective-permute-done.15.refs_2_ = bf16[256,2048]{1,0:T(8,128)(2,1)S(1)} collective-permute-done((bf16[256,2048]{1,0:T(8,128)(2,1)S(1)}, bf16[256,2048]{1,0:T(8,128)(2,1)S(1)}, u32[]{:S(2)}, u32[]{:S(2)}) %collective-permute-start.15) | collective-permute-done | bytes 1048608 | tf_op jit(solution)/shard_map/ppermute | solution.py:228
  218.8 9.5 %convolution_bitcast_fusion.3 = f32[2,256,1376]{2,1,0:T(8,128)} fusion(bf16[2,2048,1376]{1,2,0:T(8,128)(2,1)} %all-gather.11.cloned.1.call-done, bf16[256,2048]{1,0:T(8,128)(2,1)} %get-tuple-element.229.refs_0_), kind=kOutput, calls=%fused_computation.4 | convolution fusion | flops 2885681152 | bytes 15138816 | tf_op jit(solution)/shard_map/td,sdf->stf/dot_general | solution.py:581
  228.3 14.1 %collective-permute-done.18 = bf16[256,2048]{1,0:T(8,128)(2,1)} collective-permute-done((bf16[256,2048]{1,0:T(8,128)(2,1)}, bf16[256,2048]{1,0:T(8,128)(2,1)}, u32[]{:S(2)}, u32[]{:S(2)}) %collective-permute-start.18) | collective-permute-done | bytes 1048608 | tf_op jit(solution)/shard_map/ppermute | solution.py:228
  255.3 7.0 %fusion.69 = (bf16[1,256,1376]{2,1,0:T(8,128)(2,1)S(1)}, bf16[1,256,1376]{2,1,0:T(8,128)(2,1)S(1)}, bf16[256,1376]{1,0:T(8,128)(2,1)}) fusion(f32[2,256,1376]{2,1,0:T(8,128)} %convolution_bitcast_fusion.3, bf16[1376,2048]{1,0:T(8,128)(2,1)} %all-gather.9.cloned.1.call-done.refs_4_, bf16[256,2048]{1,0:T(8,128)(2,1)} %refs_5_.1), kind=kOutput, calls=%fused_computation.172 | convolution fusion | flops 1448476672 | bytes 11616256 | tf_op jit(solution)/shard_map/dot_general | solution.py:27
  321.1 18.0 %shard_map.138 = (bf16[4,2,1376,256]{3,2,1,0:T(8,128)(2,1)S(1)}, bf16[4,2,1376,256]{3,2,1,0:T(8,128)(2,1)}) custom-call(s32[1]{0:T(128)} %bitcast.40.which_ref, bf16[256,2048]{1,0:T(8,128)(2,1)} %get-tuple-element.229.refs_0_, bf16[256,2048]{1,0:T(8,128)(2,1)} %collective-permute-done.17.refs_1_, bf16[256,2048]{1,0:T(8,128)(2,1)S(1)} %copy-done.32, ...), custom_call_target="tpu_custom_call" | custom-call | flops 1048576 | bytes 65536 | tf_op jit(solution)/shard_map/pallas_call | solution.py:373
  347.7 10.4 %shard_map.139 = (bf16[4,1,1376,256]{3,2,1,0:T(8,128)(2,1)}, bf16[4,1,1376,256]{3,2,1,0:T(8,128)(2,1)S(1)}) custom-call(s32[1]{0:T(128)} %bitcast.41.which_ref, bf16[256,2048]{1,0:T(8,128)(2,1)S(1)} %copy-done.21, bf16[256,2048]{1,0:T(8,128)(2,1)S(1)} %copy-done.50, bf16[256,2048]{1,0:T(8,128)(2,1)S(1)} %copy-done.36, bf16[256,2048]{1,0:T(8,128)(2,1)S(1)} %copy-done.30, ...), custom_call_target="tpu_custom_call" | custom-call | flops 1048576 | bytes 65536 | tf_op jit(solution)/shard_map/pallas_call | solution.py:373
  358.1 12.4 %collective-permute-done.24 = bf16[256,2048]{1,0:T(8,128)(2,1)S(1)} collective-permute-done((bf16[256,2048]{1,0:T(8,128)(2,1)}, bf16[256,2048]{1,0:T(8,128)(2,1)S(1)}, u32[]{:S(2)}, u32[]{:S(2)}) %collective-permute-start.24) | collective-permute-done | bytes 1048608 | tf_op jit(solution)/shard_map/ppermute | solution.py:228
  386.9 7.9 %shard_map.140 = bf16[1024,2048]{1,0:T(8,128)(2,1)S(1)} custom-call(bf16[256,1376]{1,0:T(8,128)(2,1)S(1)} %copy-done.38, bf16[256,1376]{1,0:T(8,128)(2,1)S(1)} %copy-done.40, bf16[256,1376]{1,0:T(8,128)(2,1)S(1)} %copy-done.42, bf16[256,1376]{1,0:T(8,128)(2,1)S(1)} %copy-done.56, bf16[1376,2048]{1,0:T(8,128)(2,1)S(1)} %copy-done.19), custom_call_target="tpu_custom_call" | custom-call | flops 1048576 | bytes 65536 | tf_op jit(solution)/shard_map/pallas_call | solution.py:431
  417.9 17.2 %collective-permute-done.30 = bf16[256,2048]{1,0:T(8,128)(2,1)S(1)} collective-permute-done((bf16[256,2048]{1,0:T(8,128)(2,1)S(1)}, bf16[256,2048]{1,0:T(8,128)(2,1)S(1)}, u32[]{:S(2)}, u32[]{:S(2)}) %collective-permute-start.30) | collective-permute-done | bytes 1048608 | tf_op jit(solution)/shard_map/ppermute | solution.py:228
  443.9 15.9 %collective-permute-done.31 = bf16[256,2048]{1,0:T(8,128)(2,1)S(1)} collective-permute-done((bf16[256,2048]{1,0:T(8,128)(2,1)S(1)}, bf16[256,2048]{1,0:T(8,128)(2,1)S(1)}, u32[]{:S(2)}, u32[]{:S(2)}) %collective-permute-start.31) | collective-permute-done | bytes 1048608 | tf_op jit(solution)/shard_map/ppermute | solution.py:228
  498.8 6.1 shard_map.143
  505.9 13.0 %shard_map.142 = (bf16[1024,512]{1,0:T(8,128)(2,1)}, f32[1024,512]{1,0:T(8,128)}, f32[1024,512]{1,0:T(8,128)}, bf16[2,1024,256]{2,1,0:T(8,128)(2,1)}) custom-call(s32[2]{0:T(128)} %pad_add_fusion.place_ref, s32[1,1024]{1,0:T(1,128)} %bitcast.426, f32[4,1024]{1,0:T(4,128)} %get-tuple-element.291.lse_ref, bf16[3,256,512]{2,1,0:T(8,128)(2,1)} %copy-done.63, ...), custom_call_target="tpu_custom_call" | custom-call | flops 1048576 | bytes 65536 | tf_op jit(solution)/shard_map/pallas_call | solution.py:192
  521.9 13.0 %shard_map.144 = (bf16[1024,512]{1,0:T(8,128)(2,1)}, f32[1024,512]{1,0:T(8,128)}, f32[1024,512]{1,0:T(8,128)}, bf16[2,1024,256]{2,1,0:T(8,128)(2,1)}) custom-call(s32[2]{0:T(128)} %pad_add_fusion.place_ref, s32[1,1024]{1,0:T(1,128)} %bitcast.427, ...), custom_call_target="tpu_custom_call", output_to_operand_aliasing={{0}: (15, {}), {1}: (16, {}), {2}: (17, {})} | custom-call | flops 1048576 | bytes 65536 | tf_op jit(solution)/shard_map/pallas_call | solution.py:192
  554.1 6.5 bitcast_convert_fusion
  560.7 6.5 collective-permute-start.47
  578.0 11.4 %shard_map.145 = (bf16[4,3,512,256]{3,2,1,0:T(8,128)(2,1)}, bf16[4,3,512,256]{3,2,1,0:T(8,128)(2,1)S(1)}) custom-call(s32[1]{0:T(128)} %bitcast.86.which_ref, bf16[256,2048]{1,0:T(8,128)(2,1)S(1)} %copy-done.24, bf16[256,2048]{1,0:T(8,128)(2,1)S(1)} %copy-done.27, bf16[256,2048]{1,0:T(8,128)(2,1)S(1)} %copy-done.4, bf16[256,2048]{1,0:T(8,128)(2,1)S(1)} %copy-done.7, ...), custom_call_target="tpu_custom_call" | custom-call | flops 1048576 | bytes 65536 | tf_op jit(solution)/shard_map/pallas_call | solution.py:373
  609.4 11.1 %collective-permute-done.53 = bf16[256,2048]{1,0:T(8,128)(2,1)S(1)} collective-permute-done((bf16[256,2048]{1,0:T(8,128)(2,1)S(1)}, bf16[256,2048]{1,0:T(8,128)(2,1)S(1)}, u32[]{:S(2)}, u32[]{:S(2)}) %collective-permute-start.53) | collective-permute-done | bytes 1048608 | tf_op jit(solution)/shard_map/ppermute | solution.py:228
  641.0 15.3 %collective-permute-done.63.refs_2_ = bf16[256,2048]{1,0:T(8,128)(2,1)S(1)} collective-permute-done((bf16[256,2048]{1,0:T(8,128)(2,1)S(1)}, bf16[256,2048]{1,0:T(8,128)(2,1)S(1)}, u32[]{:S(2)}, u32[]{:S(2)}) %collective-permute-start.63) | collective-permute-done | bytes 1048608 | tf_op jit(solution)/shard_map/ppermute | solution.py:228
  (478 shorter events, 341.4 us)
Async XLA Ops:
  7.2 49.5 %all-gather.5.cloned.1.call-start = ((), (), s32[]{:S(2)}) async-start(), calls=%async_computation | async-start | bytes 7077888 | tf_op jit(solution)/shard_map/all_gather | solution.py:531
  7.9 113.1 %all-gather.7.cloned.1.call-start = ((), (), s32[]{:S(2)}) async-start(), calls=%async_computation.1 | async-start | bytes 2359296 | tf_op jit(solution)/shard_map/all_gather | solution.py:532
  10.7 26.9 %collective-permute-start.1 = (bf16[256,2048]{1,0:T(8,128)(2,1)S(1)}, bf16[256,2048]{1,0:T(8,128)(2,1)}, u32[]{:S(2)}, u32[]{:S(2)}) collective-permute-start(bf16[256,2048]{1,0:T(8,128)(2,1)S(1)} %get-tuple-element.204.refs_0_), channel_id=1, source_target_pairs={{1,2},{2,1},{5,6},{6,5},{9,10},{10,9},{13,14},{14,13},{17,18},{18,... | collective-permute-start | bytes 3145736 | tf_op jit(solution)/shard_map/ppermute | solution.py:228
  14.3 204.5 %all-gather.11.cloned.1.call-start = ((), (), s32[]{:S(2)}) async-start(), calls=%async_computation.3 | async-start | bytes 12681216 | tf_op jit(solution)/shard_map/all_gather | solution.py:555
  37.6 27.9 %collective-permute-start.3 = (bf16[256,2048]{1,0:T(8,128)(2,1)}, bf16[256,2048]{1,0:T(8,128)(2,1)}, u32[]{:S(2)}, u32[]{:S(2)}) collective-permute-start(bf16[256,2048]{1,0:T(8,128)(2,1)} %collective-permute-done.1), channel_id=1, source_target_pairs={{1,0},{2,3},{5,4},{6,7},{9,8},{10,11},{13,12},{14,15},{17,16},{18,... | collective-permute-start | bytes 3145736 | tf_op jit(solution)/shard_map/ppermute | solution.py:228
  100.6 154.6 %all-gather.9.cloned.1.call-start = ((), (), s32[]{:S(2)}) async-start(), calls=%async_computation.2 | async-start | bytes 6340608 | tf_op jit(solution)/shard_map/all_gather | solution.py:556
  181.9 27.2 %collective-permute-start.15 = (bf16[256,2048]{1,0:T(8,128)(2,1)S(1)}, bf16[256,2048]{1,0:T(8,128)(2,1)S(1)}, u32[]{:S(2)}, u32[]{:S(2)}) collective-permute-start(bf16[256,2048]{1,0:T(8,128)(2,1)S(1)} %add_convert_fusion.13), channel_id=1, source_target_pairs={{1,2},{2,1},{5,6},{6,5},{9,10},{10,9},{13,14},{14,13},{17,18},{18,... | collective-permute-start | bytes 3145736 | tf_op jit(solution)/shard_map/ppermute | solution.py:228
  214.4 27.9 %collective-permute-start.18 = (bf16[256,2048]{1,0:T(8,128)(2,1)}, bf16[256,2048]{1,0:T(8,128)(2,1)}, u32[]{:S(2)}, u32[]{:S(2)}) collective-permute-start(bf16[256,2048]{1,0:T(8,128)(2,1)} %get-tuple-element.229.refs_0_), channel_id=1, source_target_pairs={{1,2},{2,1},{5,6},{6,5},{9,10},{10,9},{13,14},{14,13},{17,18},{18,... | collective-permute-start | bytes 3145736 | tf_op jit(solution)/shard_map/ppermute | solution.py:228
  245.6 27.1 %collective-permute-start.19 = (bf16[256,2048]{1,0:T(8,128)(2,1)}, bf16[256,2048]{1,0:T(8,128)(2,1)}, u32[]{:S(2)}, u32[]{:S(2)}) collective-permute-start(bf16[256,2048]{1,0:T(8,128)(2,1)} %collective-permute-done.17.refs_1_), channel_id=1, source_target_pairs={{1,2},{2,1},{5,6},{6,5},{9,10},{10,9},{13,14},{14,13},{17,18},{18,... | collective-permute-start | bytes 3145736 | tf_op jit(solution)/shard_map/ppermute | solution.py:228
  272.7 27.8 %collective-permute-start.21 = (bf16[256,2048]{1,0:T(8,128)(2,1)}, bf16[256,2048]{1,0:T(8,128)(2,1)S(1)}, u32[]{:S(2)}, u32[]{:S(2)}) collective-permute-start(bf16[256,2048]{1,0:T(8,128)(2,1)} %collective-permute-done.19), channel_id=1, source_target_pairs={{1,0},{2,3},{5,4},{6,7},{9,8},{10,11},{13,12},{14,15},{17,16},{18,... | collective-permute-start | bytes 3145736 | tf_op jit(solution)/shard_map/ppermute | solution.py:228
  339.8 33.3 %collective-permute-start.25 = (bf16[4,2,1376,256]{3,2,1,0:T(8,128)(2,1)S(1)}, bf16[4,2,1376,256]{3,2,1,0:T(8,128)(2,1)}, u32[]{:S(2)}, u32[]{:S(2)}) collective-permute-start(bf16[4,2,1376,256]{3,2,1,0:T(8,128)(2,1)S(1)} %get-tuple-element.247), channel_id=1, source_target_pairs={{0,4},{4,0},{8,12},{12,8},{16,20},{20,16},{24,28},{28,24},{1,5},{5... | collective-permute-start | bytes 16908296 | tf_op jit(solution)/shard_map/ppermute | solution.py:228
  342.6 27.9 %collective-permute-start.24 = (bf16[256,2048]{1,0:T(8,128)(2,1)}, bf16[256,2048]{1,0:T(8,128)(2,1)S(1)}, u32[]{:S(2)}, u32[]{:S(2)}) collective-permute-start(bf16[256,2048]{1,0:T(8,128)(2,1)} %add_convert_fusion.11), channel_id=1, source_target_pairs={{1,2},{2,1},{5,6},{6,5},{9,10},{10,9},{13,14},{14,13},{17,18},{18,... | collective-permute-start | bytes 3145736 | tf_op jit(solution)/shard_map/ppermute | solution.py:228
  345.9 27.2 %collective-permute-start.23 = (bf16[256,2048]{1,0:T(8,128)(2,1)S(1)}, bf16[256,2048]{1,0:T(8,128)(2,1)S(1)}, u32[]{:S(2)}, u32[]{:S(2)}) collective-permute-start(bf16[256,2048]{1,0:T(8,128)(2,1)S(1)} %copy-done.92), channel_id=1, source_target_pairs={{0,1},{3,2},{4,5},{7,6},{8,9},{11,10},{12,13},{15,14},{16,17},{19,... | collective-permute-start | bytes 3145736 | tf_op jit(solution)/shard_map/ppermute | solution.py:228
  373.1 31.7 %collective-permute-start.28 = (bf16[4,1,1376,256]{3,2,1,0:T(8,128)(2,1)}, bf16[4,1,1376,256]{3,2,1,0:T(8,128)(2,1)}, u32[]{:S(2)}, u32[]{:S(2)}) collective-permute-start(bf16[4,1,1376,256]{3,2,1,0:T(8,128)(2,1)} %get-tuple-element.261), channel_id=1, source_target_pairs={{0,4},{4,0},{8,12},{12,8},{16,20},{20,16},{24,28},{28,24},{1,5},{5... | collective-permute-start | bytes 8454152 | tf_op jit(solution)/shard_map/ppermute | solution.py:228
  377.0 27.8 %collective-permute-start.26 = (bf16[256,2048]{1,0:T(8,128)(2,1)}, bf16[256,2048]{1,0:T(8,128)(2,1)}, u32[]{:S(2)}, u32[]{:S(2)}) collective-permute-start(bf16[256,2048]{1,0:T(8,128)(2,1)} %add_convert_fusion.10), channel_id=1, source_target_pairs={{1,2},{2,1},{5,6},{6,5},{9,10},{10,9},{13,14},{14,13},{17,18},{18,... | collective-permute-start | bytes 3145736 | tf_op jit(solution)/shard_map/ppermute | solution.py:228
  408.5 26.7 %collective-permute-start.30 = (bf16[256,2048]{1,0:T(8,128)(2,1)S(1)}, bf16[256,2048]{1,0:T(8,128)(2,1)S(1)}, u32[]{:S(2)}, u32[]{:S(2)}) collective-permute-start(bf16[256,2048]{1,0:T(8,128)(2,1)S(1)} %get-tuple-element.269.refs_0_), channel_id=1, source_target_pairs={{1,2},{2,1},{5,6},{6,5},{9,10},{10,9},{13,14},{14,13},{17,18},{18,... | collective-permute-start | bytes 3145736 | tf_op jit(solution)/shard_map/ppermute | solution.py:228
  411.6 32.3 %collective-permute-start.33 = (bf16[2,2,688,256]{3,2,1,0:T(8,128)(2,1)S(1)}, bf16[2,2,688,256]{3,2,1,0:T(8,128)(2,1)S(1)}, u32[]{:S(2)}, u32[]{:S(2)}) collective-permute-start(bf16[2,2,688,256]{3,2,1,0:T(8,128)(2,1)S(1)} %fusion.40), channel_id=1, source_target_pairs={{0,8},{4,12},{8,0},{12,4},{16,24},{20,28},{24,16},{28,20},{1,9},{5... | collective-permute-start | bytes 4227080 | tf_op jit(solution)/shard_map/ppermute | solution.py:228
  411.6 32.3 %collective-permute-start.34 = (bf16[2,2,688,256]{3,2,1,0:T(8,128)(2,1)S(1)}, bf16[2,2,688,256]{3,2,1,0:T(8,128)(2,1)S(1)}, u32[]{:S(2)}, u32[]{:S(2)}) collective-permute-start(bf16[2,2,688,256]{3,2,1,0:T(8,128)(2,1)S(1)} %fusion.41), channel_id=1, source_target_pairs={{0,16},{4,20},{8,24},{12,28},{16,0},{20,4},{24,8},{28,12},{1,17},{... | collective-permute-start | bytes 4227080 | tf_op jit(solution)/shard_map/ppermute | solution.py:228
  551.7 37.8 %collective-permute-start.46 = (bf16[256,2048]{1,0:T(8,128)(2,1)S(1)}, bf16[256,2048]{1,0:T(8,128)(2,1)S(1)}, u32[]{:S(2)}, u32[]{:S(2)}) collective-permute-start(bf16[256,2048]{1,0:T(8,128)(2,1)S(1)} %fusion.6), channel_id=1, source_target_pairs={{0,1},{3,2},{4,5},{7,6},{8,9},{11,10},{12,13},{15,14},{16,17},{19,... | collective-permute-start | bytes 3145736 | tf_op jit(solution)/shard_map/ppermute | solution.py:228
  593.0 27.6 %collective-permute-start.53 = (bf16[256,2048]{1,0:T(8,128)(2,1)S(1)}, bf16[256,2048]{1,0:T(8,128)(2,1)S(1)}, u32[]{:S(2)}, u32[]{:S(2)}) collective-permute-start(bf16[256,2048]{1,0:T(8,128)(2,1)S(1)} %add_convert_fusion.5), channel_id=1, source_target_pairs={{1,2},{2,1},{5,6},{6,5},{9,10},{10,9},{13,14},{14,13},{17,18},{18,... | collective-permute-start | bytes 3145736 | tf_op jit(solution)/shard_map/ppermute | solution.py:228
  596.2 27.2 %collective-permute-start.52 = (bf16[256,2048]{1,0:T(8,128)(2,1)S(1)}, bf16[256,2048]{1,0:T(8,128)(2,1)S(1)}, u32[]{:S(2)}, u32[]{:S(2)}) collective-permute-start(bf16[256,2048]{1,0:T(8,128)(2,1)S(1)} %get-tuple-element.364), channel_id=1, source_target_pairs={{0,1},{3,2},{4,5},{7,6},{8,9},{11,10},{12,13},{15,14},{16,17},{19,... | collective-permute-start | bytes 3145736 | tf_op jit(solution)/shard_map/ppermute | solution.py:228
  627.5 32.2 %collective-permute-start.69 = (bf16[3,512,256]{2,1,0:T(8,128)(2,1)S(1)}, bf16[3,512,256]{2,1,0:T(8,128)(2,1)S(1)}, u32[]{:S(2)}, u32[]{:S(2)}) collective-permute-start(bf16[3,512,256]{2,1,0:T(8,128)(2,1)S(1)} %get-tuple-element.403), channel_id=1, source_target_pairs={{0,24},{4,28},{8,16},{12,20},{16,8},{20,12},{24,0},{28,4},{1,25},{... | collective-permute-start | bytes 2359304 | tf_op jit(solution)/shard_map/ppermute | solution.py:228
  628.2 36.4 %collective-permute-start.68 = (bf16[3,512,256]{2,1,0:T(8,128)(2,1)S(1)}, bf16[3,512,256]{2,1,0:T(8,128)(2,1)S(1)}, u32[]{:S(2)}, u32[]{:S(2)}) collective-permute-start(bf16[3,512,256]{2,1,0:T(8,128)(2,1)S(1)} %get-tuple-element.404), channel_id=1, source_target_pairs={{0,16},{4,20},{8,24},{12,28},{16,0},{20,4},{24,8},{28,12},{1,17},{... | collective-permute-start | bytes 2359304 | tf_op jit(solution)/shard_map/ppermute | solution.py:228
  629.7 34.8 %collective-permute-start.67 = (bf16[3,512,256]{2,1,0:T(8,128)(2,1)S(1)}, bf16[3,512,256]{2,1,0:T(8,128)(2,1)S(1)}, u32[]{:S(2)}, u32[]{:S(2)}) collective-permute-start(bf16[3,512,256]{2,1,0:T(8,128)(2,1)S(1)} %get-tuple-element.405), channel_id=1, source_target_pairs={{0,8},{4,12},{8,0},{12,4},{16,24},{20,28},{24,16},{28,20},{1,9},{5... | collective-permute-start | bytes 2359304 | tf_op jit(solution)/shard_map/ppermute | solution.py:228
  (169 other events, 2295.0 us)
Sparse Core Ops, SparseCore 0:
  9.9 46.6 all-gather.4
  58.5 29.4 all-gather.6
  100.7 74.8 all-gather.10
  177.4 43.7 all-gather.8

commit v6 on v4

--- a/solution.py
+++ b/solution.py
@@ -389,7 +389,7 @@
             ],
         ),
         out_shape=[out, out],
-        compiler_params=pltpu.CompilerParams(vmem_limit_bytes=VMEM_LIMIT),
+        compiler_params=pltpu.CompilerParams(vmem_limit_bytes=ATTEND_LIMIT if count == 2 else VMEM_LIMIT),
         cost_estimate=SMALL,
     )(own.reshape(1).astype(jnp.int32), *lhs, *[r[0] for r in rhs])
 

time: 688 us -> 688 us (level)
    unnamed x236 -> x226, local copies, waits for them, and re-layouts: 24 us -> 19.6 us
  transfers between devices with their start and end apart: 74 -> 74, of which waited for: 40 -> 40; matrix products, arithmetic and copies ran while one was open for 20% -> 21% of each run, Pallas kernels for 15% -> 15%
where the time goes in v6:
time: 688 us; the launch traced here: 678 us
  waiting for transfers between devices  258 us (38%)
  starting transfers between devices  112 us (16%)
  Pallas kernels  108 us (16%)
  matrix products  88.1 us (13%)
  other arithmetic  70.3 us (10%)
  local copies, waits for them, and re-layouts  25.1 us (4%)
  between operations  15.9 us (2%)
    ppermute x70, waiting for transfers between devices, send(): return lax.ppermute(block, axis, route)  244 us
    ppermute x70, starting transfers between devices, send(): return lax.ppermute(block, axis, route)  112 us
    pallas_call x4, Pallas kernels, grad_product(): pl.pallas_call(functools.partial(grad_kernel, blocks), grid_spec=pltpu.Pr...  48.1 us
    pallas_call x2, Pallas kernels, attend_back(): pl.pallas_call(functools.partial(back_kernel, first), grid=(heads,), in_s...  26 us
    dot_general x8, matrix products, nt(): return lax.dot_general(a, b, NT, preferred_element_type=jnp.float32)  22.8 us
    dot_general x4, matrix products, up(): jnp.einsum('td,sdf->stf', rows, full_gate_up, preferred_element_type=f32)  21.9 us
    unnamed x226, local copies, waits for them, and re-layouts  19.6 us
    dot_general x4, matrix products, second_back(): jnp.einsum('stf,sdf->td', grads, full_gate_up, preferred_element_type=f32)  17.4 us
  transfers between devices with their start and end apart: 74, of which 40 were waited for; matrix products, arithmetic and copies ran while one was open for 21% of the time, Pallas kernels for 15%

profile of v6, /device:TPU:8, one launch (start us, length us, event | category | flops | bytes accessed | tf_op | source)
XLA Modules:
  0.0 678.0 jit_solution(18322631220843482694)
XLA Ops:
  14.4 23.2 %collective-permute-done.1 = bf16[256,2048]{1,0:T(8,128)(2,1)} collective-permute-done((bf16[256,2048]{1,0:T(8,128)(2,1)S(1)}, bf16[256,2048]{1,0:T(8,128)(2,1)}, u32[]{:S(2)}, u32[]{:S(2)}) %collective-permute-start.1) | collective-permute-done | bytes 1048608 | tf_op jit(solution)/shard_map/ppermute | solution.py:228
  43.3 13.3 %all-gather.5.cloned.1.call-done = bf16[3,2048,512]{2,1,0:T(8,128)(2,1)} async-done(((bf16[3,256,512]{2,1,0:T(8,128)(2,1)}), bf16[3,2048,512]{2,1,0:T(8,128)(2,1)}) %all-gather.5.cloned.1.call-update) | async-done | bytes 6291472 | tf_op jit(solution)/shard_map/all_gather | solution.py:531
  77.9 16.4 %collective-permute-done.4 = bf16[256,2048]{1,0:T(8,128)(2,1)S(1)} collective-permute-done((bf16[256,2048]{1,0:T(8,128)(2,1)}, bf16[256,2048]{1,0:T(8,128)(2,1)S(1)}, u32[]{:S(2)}, u32[]{:S(2)}) %collective-permute-start.4) | collective-permute-done | bytes 1048608 | tf_op jit(solution)/shard_map/ppermute | solution.py:228
  107.4 13.7 %shard_map.136 = (bf16[1024,512]{1,0:T(8,128)(2,1)}, f32[4,1024]{1,0:T(4,128)}) custom-call(s32[2]{0:T(128)} %pad_add_fusion.place_ref, s32[1,1024]{1,0:T(1,128)} %bitcast.428, bf16[3,256,512]{2,1,0:T(8,128)(2,1)} %copy-done.55, bf16[3,256,512]{2,1,0:T(8,128)(2,1)} %copy-done.54, bf16[3,256,512]{2,1,0:T(8,128)(2,1)} %copy-done.56, ...), custom_call_target="tpu_custom_call" | custom-call | flops 1048576 | bytes 65536 | tf_op jit(solution)/shard_map/pallas_call | solution.py:166
  135.2 16.4 %collective-permute-done.10 = bf16[256,2048]{1,0:T(8,128)(2,1)S(1)} collective-permute-done((bf16[256,2048]{1,0:T(8,128)(2,1)S(1)}, bf16[256,2048]{1,0:T(8,128)(2,1)S(1)}, u32[]{:S(2)}, u32[]{:S(2)}) %collective-permute-start.10) | collective-permute-done | bytes 1048608 | tf_op jit(solution)/shard_map/ppermute | solution.py:228
  159.7 19.6 %collective-permute-done.13 = bf16[256,2048]{1,0:T(8,128)(2,1)S(1)} collective-permute-done((bf16[256,2048]{1,0:T(8,128)(2,1)S(1)}, bf16[256,2048]{1,0:T(8,128)(2,1)S(1)}, u32[]{:S(2)}, u32[]{:S(2)}) %collective-permute-start.13) | collective-permute-done | bytes 1048608 | tf_op jit(solution)/shard_map/ppermute | solution.py:228
  186.7 22.4 %collective-permute-done.15.refs_2_ = bf16[256,2048]{1,0:T(8,128)(2,1)S(1)} collective-permute-done((bf16[256,2048]{1,0:T(8,128)(2,1)S(1)}, bf16[256,2048]{1,0:T(8,128)(2,1)S(1)}, u32[]{:S(2)}, u32[]{:S(2)}) %collective-permute-start.15) | collective-permute-done | bytes 1048608 | tf_op jit(solution)/shard_map/ppermute | solution.py:228
  218.7 9.5 %convolution_bitcast_fusion.3 = f32[2,256,1376]{2,1,0:T(8,128)} fusion(bf16[2,2048,1376]{1,2,0:T(8,128)(2,1)} %all-gather.11.cloned.1.call-done, bf16[256,2048]{1,0:T(8,128)(2,1)} %get-tuple-element.229.refs_0_), kind=kOutput, calls=%fused_computation.4 | convolution fusion | flops 2885681152 | bytes 15138816 | tf_op jit(solution)/shard_map/td,sdf->stf/dot_general | solution.py:581
  228.3 14.1 %collective-permute-done.18 = bf16[256,2048]{1,0:T(8,128)(2,1)} collective-permute-done((bf16[256,2048]{1,0:T(8,128)(2,1)}, bf16[256,2048]{1,0:T(8,128)(2,1)}, u32[]{:S(2)}, u32[]{:S(2)}) %collective-permute-start.18) | collective-permute-done | bytes 1048608 | tf_op jit(solution)/shard_map/ppermute | solution.py:228
  255.3 7.0 %fusion.69 = (bf16[1,256,1376]{2,1,0:T(8,128)(2,1)S(1)}, bf16[1,256,1376]{2,1,0:T(8,128)(2,1)S(1)}, bf16[256,1376]{1,0:T(8,128)(2,1)}) fusion(f32[2,256,1376]{2,1,0:T(8,128)} %convolution_bitcast_fusion.3, bf16[1376,2048]{1,0:T(8,128)(2,1)} %all-gather.9.cloned.1.call-done.refs_4_, bf16[256,2048]{1,0:T(8,128)(2,1)} %refs_5_.1), kind=kOutput, calls=%fused_computation.172 | convolution fusion | flops 1448476672 | bytes 11616256 | tf_op jit(solution)/shard_map/dot_general | solution.py:27
  317.8 20.4 %shard_map.138 = (bf16[4,2,1376,256]{3,2,1,0:T(8,128)(2,1)}, bf16[4,2,1376,256]{3,2,1,0:T(8,128)(2,1)}) custom-call(s32[1]{0:T(128)} %bitcast.40.which_ref, bf16[256,2048]{1,0:T(8,128)(2,1)} %get-tuple-element.229.refs_0_, bf16[256,2048]{1,0:T(8,128)(2,1)} %collective-permute-done.17.refs_1_, bf16[256,2048]{1,0:T(8,128)(2,1)} %copy-done.74, ...), custom_call_target="tpu_custom_call" | custom-call | flops 1048576 | bytes 65536 | tf_op jit(solution)/shard_map/pallas_call | solution.py:373
  349.1 10.4 %shard_map.139 = (bf16[4,1,1376,256]{3,2,1,0:T(8,128)(2,1)}, bf16[4,1,1376,256]{3,2,1,0:T(8,128)(2,1)S(1)}) custom-call(s32[1]{0:T(128)} %bitcast.41.which_ref, bf16[256,2048]{1,0:T(8,128)(2,1)S(1)} %copy-done.17, bf16[256,2048]{1,0:T(8,128)(2,1)S(1)} %copy-done.42, bf16[256,2048]{1,0:T(8,128)(2,1)S(1)} %copy-done.28, bf16[256,2048]{1,0:T(8,128)(2,1)S(1)} %copy-done.26, ...), custom_call_target="tpu_custom_call" | custom-call | flops 1048576 | bytes 65536 | tf_op jit(solution)/shard_map/pallas_call | solution.py:373
  359.4 10.5 %collective-permute-done.24 = bf16[256,2048]{1,0:T(8,128)(2,1)S(1)} collective-permute-done((bf16[256,2048]{1,0:T(8,128)(2,1)S(1)}, bf16[256,2048]{1,0:T(8,128)(2,1)S(1)}, u32[]{:S(2)}, u32[]{:S(2)}) %collective-permute-start.24) | collective-permute-done | bytes 1048608 | tf_op jit(solution)/shard_map/ppermute | solution.py:228
  387.5 7.9 %shard_map.140 = bf16[1024,2048]{1,0:T(8,128)(2,1)S(1)} custom-call(bf16[256,1376]{1,0:T(8,128)(2,1)S(1)} %copy-done.30, bf16[256,1376]{1,0:T(8,128)(2,1)S(1)} %copy-done.32, bf16[256,1376]{1,0:T(8,128)(2,1)S(1)} %copy-done.34, bf16[256,1376]{1,0:T(8,128)(2,1)S(1)} %copy-done.48, bf16[1376,2048]{1,0:T(8,128)(2,1)S(1)} %copy-done.15), custom_call_target="tpu_custom_call" | custom-call | flops 1048576 | bytes 65536 | tf_op jit(solution)/shard_map/pallas_call | solution.py:431
  418.6 17.2 %collective-permute-done.30 = bf16[256,2048]{1,0:T(8,128)(2,1)S(1)} collective-permute-done((bf16[256,2048]{1,0:T(8,128)(2,1)S(1)}, bf16[256,2048]{1,0:T(8,128)(2,1)S(1)}, u32[]{:S(2)}, u32[]{:S(2)}) %collective-permute-start.30) | collective-permute-done | bytes 1048608 | tf_op jit(solution)/shard_map/ppermute | solution.py:228
  444.6 15.9 %collective-permute-done.31 = bf16[256,2048]{1,0:T(8,128)(2,1)S(1)} collective-permute-done((bf16[256,2048]{1,0:T(8,128)(2,1)S(1)}, bf16[256,2048]{1,0:T(8,128)(2,1)S(1)}, u32[]{:S(2)}, u32[]{:S(2)}) %collective-permute-start.31) | collective-permute-done | bytes 1048608 | tf_op jit(solution)/shard_map/ppermute | solution.py:228
  499.5 6.0 shard_map.143
  506.6 13.0 %shard_map.142 = (bf16[1024,512]{1,0:T(8,128)(2,1)}, f32[1024,512]{1,0:T(8,128)}, f32[1024,512]{1,0:T(8,128)}, bf16[2,1024,256]{2,1,0:T(8,128)(2,1)}) custom-call(s32[2]{0:T(128)} %pad_add_fusion.place_ref, s32[1,1024]{1,0:T(1,128)} %bitcast.429, f32[4,1024]{1,0:T(4,128)} %get-tuple-element.291.lse_ref, bf16[3,256,512]{2,1,0:T(8,128)(2,1)} %copy-done.55, ...), custom_call_target="tpu_custom_call" | custom-call | flops 1048576 | bytes 65536 | tf_op jit(solution)/shard_map/pallas_call | solution.py:192
  522.6 13.0 %shard_map.144 = (bf16[1024,512]{1,0:T(8,128)(2,1)}, f32[1024,512]{1,0:T(8,128)}, f32[1024,512]{1,0:T(8,128)}, bf16[2,1024,256]{2,1,0:T(8,128)(2,1)}) custom-call(s32[2]{0:T(128)} %pad_add_fusion.place_ref, s32[1,1024]{1,0:T(1,128)} %bitcast.430, ...), custom_call_target="tpu_custom_call", output_to_operand_aliasing={{0}: (15, {}), {1}: (16, {}), {2}: (17, {})} | custom-call | flops 1048576 | bytes 65536 | tf_op jit(solution)/shard_map/pallas_call | solution.py:192
  553.9 6.5 collective-permute-start.47
  570.2 6.5 bitcast_convert_fusion
  578.0 11.4 %shard_map.145 = (bf16[4,3,512,256]{3,2,1,0:T(8,128)(2,1)}, bf16[4,3,512,256]{3,2,1,0:T(8,128)(2,1)S(1)}) custom-call(s32[1]{0:T(128)} %bitcast.86.which_ref, bf16[256,2048]{1,0:T(8,128)(2,1)S(1)} %copy-done.20, bf16[256,2048]{1,0:T(8,128)(2,1)S(1)} %copy-done.23, bf16[256,2048]{1,0:T(8,128)(2,1)S(1)} %copy-done.4, bf16[256,2048]{1,0:T(8,128)(2,1)S(1)} %copy-done.7, ...), custom_call_target="tpu_custom_call" | custom-call | flops 1048576 | bytes 65536 | tf_op jit(solution)/shard_map/pallas_call | solution.py:373
  610.1 10.4 %collective-permute-done.53 = bf16[256,2048]{1,0:T(8,128)(2,1)S(1)} collective-permute-done((bf16[256,2048]{1,0:T(8,128)(2,1)S(1)}, bf16[256,2048]{1,0:T(8,128)(2,1)S(1)}, u32[]{:S(2)}, u32[]{:S(2)}) %collective-permute-start.53) | collective-permute-done | bytes 1048608 | tf_op jit(solution)/shard_map/ppermute | solution.py:228
  641.0 15.1 %collective-permute-done.63.refs_2_ = bf16[256,2048]{1,0:T(8,128)(2,1)S(1)} collective-permute-done((bf16[256,2048]{1,0:T(8,128)(2,1)S(1)}, bf16[256,2048]{1,0:T(8,128)(2,1)S(1)}, u32[]{:S(2)}, u32[]{:S(2)}) %collective-permute-start.63) | collective-permute-done | bytes 1048608 | tf_op jit(solution)/shard_map/ppermute | solution.py:228
  (468 shorter events, 342.1 us)
Async XLA Ops:
  7.2 49.5 %all-gather.5.cloned.1.call-start = ((), (), s32[]{:S(2)}) async-start(), calls=%async_computation | async-start | bytes 7077888 | tf_op jit(solution)/shard_map/all_gather | solution.py:531
  7.9 113.1 %all-gather.7.cloned.1.call-start = ((), (), s32[]{:S(2)}) async-start(), calls=%async_computation.1 | async-start | bytes 2359296 | tf_op jit(solution)/shard_map/all_gather | solution.py:532
  10.7 26.9 %collective-permute-start.1 = (bf16[256,2048]{1,0:T(8,128)(2,1)S(1)}, bf16[256,2048]{1,0:T(8,128)(2,1)}, u32[]{:S(2)}, u32[]{:S(2)}) collective-permute-start(bf16[256,2048]{1,0:T(8,128)(2,1)S(1)} %get-tuple-element.204.refs_0_), channel_id=1, source_target_pairs={{1,2},{2,1},{5,6},{6,5},{9,10},{10,9},{13,14},{14,13},{17,18},{18,... | collective-permute-start | bytes 3145736 | tf_op jit(solution)/shard_map/ppermute | solution.py:228
  14.3 204.4 %all-gather.11.cloned.1.call-start = ((), (), s32[]{:S(2)}) async-start(), calls=%async_computation.3 | async-start | bytes 12681216 | tf_op jit(solution)/shard_map/all_gather | solution.py:555
  37.6 27.9 %collective-permute-start.3 = (bf16[256,2048]{1,0:T(8,128)(2,1)}, bf16[256,2048]{1,0:T(8,128)(2,1)}, u32[]{:S(2)}, u32[]{:S(2)}) collective-permute-start(bf16[256,2048]{1,0:T(8,128)(2,1)} %collective-permute-done.1), channel_id=1, source_target_pairs={{1,0},{2,3},{5,4},{6,7},{9,8},{10,11},{13,12},{14,15},{17,16},{18,... | collective-permute-start | bytes 3145736 | tf_op jit(solution)/shard_map/ppermute | solution.py:228
  100.6 154.7 %all-gather.9.cloned.1.call-start = ((), (), s32[]{:S(2)}) async-start(), calls=%async_computation.2 | async-start | bytes 6340608 | tf_op jit(solution)/shard_map/all_gather | solution.py:556
  181.9 27.2 %collective-permute-start.15 = (bf16[256,2048]{1,0:T(8,128)(2,1)S(1)}, bf16[256,2048]{1,0:T(8,128)(2,1)S(1)}, u32[]{:S(2)}, u32[]{:S(2)}) collective-permute-start(bf16[256,2048]{1,0:T(8,128)(2,1)S(1)} %add_convert_fusion.13), channel_id=1, source_target_pairs={{1,2},{2,1},{5,6},{6,5},{9,10},{10,9},{13,14},{14,13},{17,18},{18,... | collective-permute-start | bytes 3145736 | tf_op jit(solution)/shard_map/ppermute | solution.py:228
  214.4 27.9 %collective-permute-start.18 = (bf16[256,2048]{1,0:T(8,128)(2,1)}, bf16[256,2048]{1,0:T(8,128)(2,1)}, u32[]{:S(2)}, u32[]{:S(2)}) collective-permute-start(bf16[256,2048]{1,0:T(8,128)(2,1)} %get-tuple-element.229.refs_0_), channel_id=1, source_target_pairs={{1,2},{2,1},{5,6},{6,5},{9,10},{10,9},{13,14},{14,13},{17,18},{18,... | collective-permute-start | bytes 3145736 | tf_op jit(solution)/shard_map/ppermute | solution.py:228
  245.7 27.1 %collective-permute-start.19 = (bf16[256,2048]{1,0:T(8,128)(2,1)}, bf16[256,2048]{1,0:T(8,128)(2,1)}, u32[]{:S(2)}, u32[]{:S(2)}) collective-permute-start(bf16[256,2048]{1,0:T(8,128)(2,1)} %collective-permute-done.17.refs_1_), channel_id=1, source_target_pairs={{1,2},{2,1},{5,6},{6,5},{9,10},{10,9},{13,14},{14,13},{17,18},{18,... | collective-permute-start | bytes 3145736 | tf_op jit(solution)/shard_map/ppermute | solution.py:228
  272.8 27.8 %collective-permute-start.21 = (bf16[256,2048]{1,0:T(8,128)(2,1)}, bf16[256,2048]{1,0:T(8,128)(2,1)S(1)}, u32[]{:S(2)}, u32[]{:S(2)}) collective-permute-start(bf16[256,2048]{1,0:T(8,128)(2,1)} %collective-permute-done.19), channel_id=1, source_target_pairs={{1,0},{2,3},{5,4},{6,7},{9,8},{10,11},{13,12},{14,15},{17,16},{18,... | collective-permute-start | bytes 3145736 | tf_op jit(solution)/shard_map/ppermute | solution.py:228
  340.0 32.9 %collective-permute-start.25 = (bf16[4,2,1376,256]{3,2,1,0:T(8,128)(2,1)}, bf16[4,2,1376,256]{3,2,1,0:T(8,128)(2,1)S(1)}, u32[]{:S(2)}, u32[]{:S(2)}) collective-permute-start(bf16[4,2,1376,256]{3,2,1,0:T(8,128)(2,1)} %get-tuple-element.247), channel_id=1, source_target_pairs={{0,4},{4,0},{8,12},{12,8},{16,20},{20,16},{24,28},{28,24},{1,5},{5... | collective-permute-start | bytes 16908296 | tf_op jit(solution)/shard_map/ppermute | solution.py:228
  342.2 27.7 %collective-permute-start.24 = (bf16[256,2048]{1,0:T(8,128)(2,1)S(1)}, bf16[256,2048]{1,0:T(8,128)(2,1)S(1)}, u32[]{:S(2)}, u32[]{:S(2)}) collective-permute-start(bf16[256,2048]{1,0:T(8,128)(2,1)S(1)} %add_convert_fusion.11), channel_id=1, source_target_pairs={{1,2},{2,1},{5,6},{6,5},{9,10},{10,9},{13,14},{14,13},{17,18},{18,... | collective-permute-start | bytes 3145736 | tf_op jit(solution)/shard_map/ppermute | solution.py:228
  345.5 27.4 %collective-permute-start.23 = (bf16[256,2048]{1,0:T(8,128)(2,1)}, bf16[256,2048]{1,0:T(8,128)(2,1)S(1)}, u32[]{:S(2)}, u32[]{:S(2)}) collective-permute-start(bf16[256,2048]{1,0:T(8,128)(2,1)} %fusion.4), channel_id=1, source_target_pairs={{0,1},{3,2},{4,5},{7,6},{8,9},{11,10},{12,13},{15,14},{16,17},{19,... | collective-permute-start | bytes 3145736 | tf_op jit(solution)/shard_map/ppermute | solution.py:228
  372.9 32.5 %collective-permute-start.28 = (bf16[4,1,1376,256]{3,2,1,0:T(8,128)(2,1)}, bf16[4,1,1376,256]{3,2,1,0:T(8,128)(2,1)}, u32[]{:S(2)}, u32[]{:S(2)}) collective-permute-start(bf16[4,1,1376,256]{3,2,1,0:T(8,128)(2,1)} %get-tuple-element.261), channel_id=1, source_target_pairs={{0,4},{4,0},{8,12},{12,8},{16,20},{20,16},{24,28},{28,24},{1,5},{5... | collective-permute-start | bytes 8454152 | tf_op jit(solution)/shard_map/ppermute | solution.py:228
  377.6 27.8 %collective-permute-start.26 = (bf16[256,2048]{1,0:T(8,128)(2,1)}, bf16[256,2048]{1,0:T(8,128)(2,1)}, u32[]{:S(2)}, u32[]{:S(2)}) collective-permute-start(bf16[256,2048]{1,0:T(8,128)(2,1)} %add_convert_fusion.10), channel_id=1, source_target_pairs={{1,2},{2,1},{5,6},{6,5},{9,10},{10,9},{13,14},{14,13},{17,18},{18,... | collective-permute-start | bytes 3145736 | tf_op jit(solution)/shard_map/ppermute | solution.py:228
  412.2 32.3 %collective-permute-start.33 = (bf16[2,2,688,256]{3,2,1,0:T(8,128)(2,1)S(1)}, bf16[2,2,688,256]{3,2,1,0:T(8,128)(2,1)S(1)}, u32[]{:S(2)}, u32[]{:S(2)}) collective-permute-start(bf16[2,2,688,256]{3,2,1,0:T(8,128)(2,1)S(1)} %fusion.40), channel_id=1, source_target_pairs={{0,8},{4,12},{8,0},{12,4},{16,24},{20,28},{24,16},{28,20},{1,9},{5... | collective-permute-start | bytes 4227080 | tf_op jit(solution)/shard_map/ppermute | solution.py:228
  412.3 32.3 %collective-permute-start.34 = (bf16[2,2,688,256]{3,2,1,0:T(8,128)(2,1)S(1)}, bf16[2,2,688,256]{3,2,1,0:T(8,128)(2,1)S(1)}, u32[]{:S(2)}, u32[]{:S(2)}) collective-permute-start(bf16[2,2,688,256]{3,2,1,0:T(8,128)(2,1)S(1)} %fusion.41), channel_id=1, source_target_pairs={{0,16},{4,20},{8,24},{12,28},{16,0},{20,4},{24,8},{28,12},{1,17},{... | collective-permute-start | bytes 4227080 | tf_op jit(solution)/shard_map/ppermute | solution.py:228
  552.4 37.0 %collective-permute-start.46 = (bf16[256,2048]{1,0:T(8,128)(2,1)S(1)}, bf16[256,2048]{1,0:T(8,128)(2,1)S(1)}, u32[]{:S(2)}, u32[]{:S(2)}) collective-permute-start(bf16[256,2048]{1,0:T(8,128)(2,1)S(1)} %fusion.6), channel_id=1, source_target_pairs={{0,1},{3,2},{4,5},{7,6},{8,9},{11,10},{12,13},{15,14},{16,17},{19,... | collective-permute-start | bytes 3145736 | tf_op jit(solution)/shard_map/ppermute | solution.py:228
  561.3 28.0 %collective-permute-start.48 = (bf16[1,512,256]{2,1,0:T(8,128)(2,1)S(1)}, bf16[1,512,256]{2,1,0:T(8,128)(2,1)S(1)}, u32[]{:S(2)}, u32[]{:S(2)}) collective-permute-start(bf16[1,512,256]{2,1,0:T(8,128)(2,1)S(1)} %get-tuple-element.343), channel_id=1, source_target_pairs={{0,16},{4,20},{8,24},{12,28},{16,0},{20,4},{24,8},{28,12},{1,17},{... | collective-permute-start | bytes 786440 | tf_op jit(solution)/shard_map/ppermute | solution.py:228
  592.9 27.6 %collective-permute-start.53 = (bf16[256,2048]{1,0:T(8,128)(2,1)S(1)}, bf16[256,2048]{1,0:T(8,128)(2,1)S(1)}, u32[]{:S(2)}, u32[]{:S(2)}) collective-permute-start(bf16[256,2048]{1,0:T(8,128)(2,1)S(1)} %add_convert_fusion.5), channel_id=1, source_target_pairs={{1,2},{2,1},{5,6},{6,5},{9,10},{10,9},{13,14},{14,13},{17,18},{18,... | collective-permute-start | bytes 3145736 | tf_op jit(solution)/shard_map/ppermute | solution.py:228
  595.9 27.2 %collective-permute-start.52 = (bf16[256,2048]{1,0:T(8,128)(2,1)S(1)}, bf16[256,2048]{1,0:T(8,128)(2,1)S(1)}, u32[]{:S(2)}, u32[]{:S(2)}) collective-permute-start(bf16[256,2048]{1,0:T(8,128)(2,1)S(1)} %get-tuple-element.364), channel_id=1, source_target_pairs={{0,1},{3,2},{4,5},{7,6},{8,9},{11,10},{12,13},{15,14},{16,17},{19,... | collective-permute-start | bytes 3145736 | tf_op jit(solution)/shard_map/ppermute | solution.py:228
  627.2 32.4 %collective-permute-start.69 = (bf16[3,512,256]{2,1,0:T(8,128)(2,1)S(1)}, bf16[3,512,256]{2,1,0:T(8,128)(2,1)S(1)}, u32[]{:S(2)}, u32[]{:S(2)}) collective-permute-start(bf16[3,512,256]{2,1,0:T(8,128)(2,1)S(1)} %get-tuple-element.403), channel_id=1, source_target_pairs={{0,24},{4,28},{8,16},{12,20},{16,8},{20,12},{24,0},{28,4},{1,25},{... | collective-permute-start | bytes 2359304 | tf_op jit(solution)/shard_map/ppermute | solution.py:228
  629.0 35.5 %collective-permute-start.68 = (bf16[3,512,256]{2,1,0:T(8,128)(2,1)S(1)}, bf16[3,512,256]{2,1,0:T(8,128)(2,1)S(1)}, u32[]{:S(2)}, u32[]{:S(2)}) collective-permute-start(bf16[3,512,256]{2,1,0:T(8,128)(2,1)S(1)} %get-tuple-element.404), channel_id=1, source_target_pairs={{0,16},{4,20},{8,24},{12,28},{16,0},{20,4},{24,8},{28,12},{1,17},{... | collective-permute-start | bytes 2359304 | tf_op jit(solution)/shard_map/ppermute | solution.py:228
  629.3 35.6 %collective-permute-start.67 = (bf16[3,512,256]{2,1,0:T(8,128)(2,1)S(1)}, bf16[3,512,256]{2,1,0:T(8,128)(2,1)S(1)}, u32[]{:S(2)}, u32[]{:S(2)}) collective-permute-start(bf16[3,512,256]{2,1,0:T(8,128)(2,1)S(1)} %get-tuple-element.405), channel_id=1, source_target_pairs={{0,8},{4,12},{8,0},{12,4},{16,24},{20,28},{24,16},{28,20},{1,9},{5... | collective-permute-start | bytes 2359304 | tf_op jit(solution)/shard_map/ppermute | solution.py:228
  (164 other events, 2267.6 us)
Sparse Core Ops, SparseCore 0:
  9.9 46.6 all-gather.4
  58.5 29.4 all-gather.6
  100.7 74.8 all-gather.10
  177.3 43.7 all-gather.8
